TPU v7x, 32 devices: a whole 2x2x4 slice. The times are simulated.
32 devices in a mesh: groups: 2 (over x), row: 16 (over z, y, core).
Axes of the slice: x: 2, y: 2, z: 4, core: 2. Of those that a mesh axis runs over, the one named last changes fastest.
Arguments:
- features: bfloat16 [32768, 256], P(('groups', 'row')), parts along dimension 0, may hold values from -6 to 6
- weight: bfloat16 [256, 256], replicated, may hold values from -0.375 to 0.375
- root_weight: bfloat16 [256, 256], replicated, may hold values from -0.375 to 0.375
- block_tiles: bfloat16 [6144, 128, 128], P(('groups', 'row')), parts along dimension 0, may hold values from -0.109375 to 0.109375
- tile_rows: int32 [6144], P(('groups', 'row')), parts along dimension 0, may hold values from 0 to 7, as said below
- tile_cols: int32 [6144], P(('groups', 'row')), parts along dimension 0, may hold values from 0 to 127, as said below
- tile_count: int32 [32], P(('groups', 'row')), parts along dimension 0, may hold values from 48 to 192, as said below
- cotangent: bfloat16 [32768, 256], P(('groups', 'row')), parts along dimension 0, may hold values from -6 to 6
Outputs:
- layer_out: bfloat16 [32768, 256], P(('groups', 'row')), parts along dimension 0
- grad_features: bfloat16 [32768, 256], P(('groups', 'row')), parts along dimension 0
- grad_weight: float32 [512, 256], P('groups'), parts along dimension 0
- grad_root: float32 [512, 256], P('groups'), parts along dimension 0
There are 2 independent parts, one for each index of `groups`. A program takes and returns all parts, laid end to end along the dimension named above; an argument that names none is the same for every part. Nothing has to cross between parts.
Inputs may be any that keep to these rules, and one draw needn't show every extreme that they name: `tile_rows`: the row block of a slot within its stripe of 8 blocks; stripe s owns slots s * 192 to (s + 1) * 192 - 1. `tile_cols`: a slot of stripe s names a column block from (s - 2) * 8 to (s + 3) * 8 - 1 that lies in the graph; within a stripe no pair of row block and column block appears twice, live or not. The live slots of each stripe are its first tile_count slots; some stripe has all 192 live.
All inputs are finite; a program needn't handle non-finite values.
Results may differ from a plain program's by a relative error of at most 0.0055.
Values may be sent and summed in bfloat16 or wider, within the bound.
No kernel may reach another device: no remote copies, remote signals or barrier semaphores. Data moves between devices by JAX's collectives and lax.ppermute only.
A program may use at most 128 MiB of HBM per device.

v0:
```python
import math

import jax
import jax.numpy as jnp
from jax import lax
from jax.sharding import PartitionSpec as P

REACH = 2


def from_behind(block, axis, distance):
    devices = range(lax.axis_size(axis))
    route = [(i - distance, i) for i in devices if i - distance in devices]
    return lax.ppermute(block, axis, route)


def tile_products(block_tiles, sources, take_index, put_index, slot_live, out_blocks, transposed):
    formula = "tji,tjf->tif" if transposed else "tij,tjf->tif"
    zeroed = jnp.zeros((out_blocks, sources.shape[1], sources.shape[2]), jnp.float32)
    picked = jnp.take(sources, take_index, axis=0)
    products = jnp.einsum(formula, block_tiles, picked, preferred_element_type=jnp.float32)
    return zeroed.at[put_index].add(products * slot_live[:, None, None])


def body(features, weight, root_weight, block_tiles, tile_rows, tile_cols, tile_count, cotangent):
    row_count, feature_width = features.shape
    block_size = block_tiles.shape[1]
    blocks_here = row_count // block_size
    slot_total = block_tiles.shape[0]
    window = 2 * REACH + 1
    stripe_index = lax.axis_index("row")
    local_cols = tile_cols - (stripe_index - REACH) * blocks_here
    slot_live = (jnp.arange(slot_total, dtype=jnp.int32) < tile_count[0]).astype(jnp.float32)
    projected = jnp.dot(features, weight, preferred_element_type=jnp.float32).astype(jnp.bfloat16)
    root_term = jnp.dot(features, root_weight, preferred_element_type=jnp.float32)
    from_below = []
    from_above = []
    lower_copy = projected
    upper_copy = projected
    for offset in range(1, REACH + 1):
        lower_copy = from_behind(lower_copy, "row", 1)
        upper_copy = from_behind(upper_copy, "row", -1)
        from_below.append(lower_copy)
        from_above.append(upper_copy)
    stacked = jnp.concatenate(from_below[::-1] + [projected] + from_above, axis=0)
    stacked = stacked.reshape(window * blocks_here, block_size, feature_width)
    aggregated = tile_products(
        block_tiles, stacked, local_cols, tile_rows, slot_live, blocks_here, False
    )
    pre_act = aggregated.reshape(row_count, feature_width) + root_term
    layer_out = jax.nn.silu(pre_act).astype(jnp.bfloat16)
    sigmoid_pre = jax.nn.sigmoid(pre_act)
    grad_pre = (
        cotangent.astype(jnp.float32) * (sigmoid_pre * (1.0 + pre_act * (1.0 - sigmoid_pre)))
    ).astype(jnp.bfloat16)
    grad_blocks = grad_pre.reshape(blocks_here, block_size, feature_width)
    spread = tile_products(
        block_tiles, grad_blocks, tile_rows, local_cols, slot_live, window * blocks_here, True
    )
    spread = spread.reshape(window, row_count, feature_width)
    lower_carry = spread[0]
    for offset in range(1, REACH + 1):
        lower_carry = from_behind(lower_carry, "row", -1) + spread[offset]
    upper_carry = spread[2 * REACH]
    for offset in range(1, REACH + 1):
        arrived = from_behind(upper_carry, "row", 1)
        upper_carry = arrived + spread[2 * REACH - offset] if offset < REACH else arrived
    summed = lower_carry + upper_carry
    grad_proj = summed.astype(jnp.bfloat16)
    local_weight = jnp.einsum("nf,ng->fg", features, grad_proj, preferred_element_type=jnp.float32)
    local_root = jnp.einsum("nf,ng->fg", features, grad_pre, preferred_element_type=jnp.float32)
    total_weight, total_root = lax.psum((local_weight, local_root), "row")
    grad_scale = 1.0 / math.sqrt(lax.axis_size("row") * row_count)
    grad_features = jnp.einsum("ng,fg->nf", grad_proj, weight, preferred_element_type=jnp.float32)
    grad_features = grad_features + jnp.einsum(
        "ng,fg->nf", grad_pre, root_weight, preferred_element_type=jnp.float32
    )
    return (
        layer_out,
        grad_features.astype(jnp.bfloat16),
        total_weight * grad_scale,
        total_root * grad_scale,
    )


def solution(mesh):
    placed = (
        P(("groups", "row"), None),
        P(),
        P(),
        P(("groups", "row"), None, None),
        P(("groups", "row")),
        P(("groups", "row")),
        P(("groups", "row")),
        P(("groups", "row"), None),
    )
    return jax.shard_map(
        body,
        mesh=mesh,
        in_specs=placed,
        out_specs=(
            P(("groups", "row"), None),
            P(("groups", "row"), None),
            P("groups", None),
            P("groups", None),
        ),
        check_vma=False,
    )
```

profile of v0, /device:TPU:0, one launch (start us, length us, event | category | flops | bytes accessed | tf_op | source)
XLA Modules:
  0.0 403.7 jit_solution(11712243752922342059)
XLA Ops:
  7.2 0.0 copy-start
  7.2 0.0 all-reduce.3.cloned.1.call-start
  7.2 1.0 copy-done
  8.2 1.2 convolution_convert_fusion
  9.4 0.0 copy-start.1
  9.4 2.4 collective-permute-start
  11.8 1.3 collective-permute-start.2
  13.8 0.7 compare_and_fusion.1
  14.5 0.0 collective-permute-done
  14.5 0.0 copy-start.3
  14.5 13.6 %collective-permute-start.1 = (bf16[1024,256]{1,0:T(8,128)(2,1)S(1)}, bf16[1024,256]{1,0:T(8,128)(2,1)S(1)}, u32[]{:S(2)}, u32[]{:S(2)}) collective-permute-start(bf16[1024,256]{1,0:T(8,128)(2,1)S(1)} %collective-permute-done), channel_id=1, source_target_pairs={{0,1},{1,2},{2,3},{3,4},{4,5},{5,6},{6,7},{7,8},{8,9},{9,10},{10,1... | collective-permute-start | bytes 1572872 | tf_op jit(solution)/shard_map/ppermute | solution.py:14
  28.1 0.7 compare_select_fusion.1
  28.8 0.7 compare_and_fusion
  29.5 0.0 collective-permute-done.2
  29.5 1.3 collective-permute-start.3
  30.8 0.0 copy-done.1
  30.8 0.0 copy-done.3
  30.8 0.0 collective-permute-done.1
  30.8 1.1 constant_dynamic-update-slice_fusion.3
  31.9 1.1 constant_dynamic-update-slice_fusion.2
  33.0 1.1 constant_dynamic-update-slice_fusion.1
  34.1 1.3 collective-permute-done.3
  35.5 8.3 %gather_fusion = bf16[192,128,256]{2,1,0:T(8,128)(2,1)} fusion(bf16[40,128,256]{2,1,0:T(8,128)(2,1)S(1)} %bitcast.41, s32[1024]{0:T(1024)S(1)} %pad_clamp_fusion.1), kind=kCustom, calls=%fused_computation | custom fusion | bytes 25166592 | tf_op jit(solution)/shard_map/jit(_take)/gather | solution.py:20
  43.7 17.6 %multiply_bitcast_fusion.1 = f32[192,128,256]{1,2,0:T(8,128)} fusion(f32[192]{0:T(256)S(1)} %get-tuple-element.24, bf16[192,128,128]{2,1,0:T(8,128)(2,1)} %param.11, bf16[192,128,256]{2,1,0:T(8,128)(2,1)} %gather_fusion, pred[192]{0:T(512)(128)(4,1)S(1)} %get-tuple-element.14), kind=kOutput, calls=%fused_computation.5 | convolution fusion | flops 1623195648 | bytes 44041152 | tf_op jit(solution)/shard_map/tij,tjf->tif/dot_general | solution.py:21
  61.4 24.6 %copy.17 = f32[192,128,256]{2,1,0:T(8,128)} copy(f32[192,128,256]{1,2,0:T(8,128)} %multiply_bitcast_fusion.1) | data formatting | bytes 50331648 | tf_op jit(solution)/shard_map/mul | solution.py:22
  86.0 0.1 broadcast_in_dim.32
  86.1 0.0 copy-start.4
  86.1 0.0 copy-start.5
  86.1 36.0 %scatter_fusion = f32[8,128,256]{2,1,0:T(8,128)S(1)} fusion(f32[8,128,256]{2,1,0:T(8,128)S(1)} %broadcast_in_dim.32, s32[192]{0:T(256)S(1)} %compare_select_fusion.1, f32[192,128,256]{2,1,0:T(8,128)} %copy.17), kind=kCustom, calls=%fused_computation.2 | custom fusion | flops 6291456 | bytes 75498240 | tf_op jit(solution)/shard_map/scatter-add | solution.py:22
  122.1 0.0 copy-done.4
  122.2 0.0 copy-done.5
  122.2 1.4 multiply_convert_fusion
  123.6 8.1 %gather_fusion.1 = bf16[192,128,256]{2,1,0:T(8,128)(2,1)} fusion(bf16[8,128,256]{2,1,0:T(8,128)(2,1)S(1)} %bitcast.40, s32[1024]{0:T(1024)S(1)} %pad_clamp_fusion), kind=kCustom, calls=%fused_computation.1 | custom fusion | bytes 25166592 | tf_op jit(solution)/shard_map/jit(_take)/gather | solution.py:20
  131.7 14.9 %multiply_bitcast_fusion = f32[192,128,256]{1,2,0:T(8,128)} fusion(f32[192]{0:T(256)S(1)} %get-tuple-element.24, bf16[192,128,128]{2,1,0:T(8,128)(2,1)} %param.11, bf16[192,128,256]{2,1,0:T(8,128)(2,1)} %gather_fusion.1, pred[192]{0:T(512)(128)(4,1)S(1)} %get-tuple-element.23), kind=kOutput, calls=%fused_computation.4 | convolution fusion | flops 1623195648 | bytes 44041152 | tf_op jit(solution)/shard_map/tji,tjf->tif/dot_general | solution.py:21
  146.7 24.7 %copy.19 = f32[192,128,256]{2,1,0:T(8,128)} copy(f32[192,128,256]{1,2,0:T(8,128)} %multiply_bitcast_fusion) | data formatting | bytes 50331648 | tf_op jit(solution)/shard_map/mul | solution.py:22
  171.3 3.0 broadcast_in_dim.37
  174.4 57.2 %scatter_fusion.1 = f32[40,128,256]{2,1,0:T(8,128)} fusion(f32[40,128,256]{2,1,0:T(8,128)} %broadcast_in_dim.37, s32[192]{0:T(256)S(1)} %get-tuple-element.15, f32[192,128,256]{2,1,0:T(8,128)} %copy.19), kind=kCustom, calls=%fused_computation.3 | custom fusion | flops 6291456 | bytes 75498240 | tf_op jit(solution)/shard_map/scatter-add | solution.py:22
  231.6 0.0 copy-start.2
  231.6 2.9 fusion.17
  234.4 1.3 collective-permute-start.4
  235.7 12.9 %collective-permute-start.6 = (f32[1024,256]{1,0:T(8,128)S(1)}, f32[1024,256]{1,0:T(8,128)S(1)}, u32[]{:S(2)}, u32[]{:S(2)}) collective-permute-start(f32[1024,256]{1,0:T(8,128)S(1)} %bitcast.42), channel_id=1, source_target_pairs={{0,1},{1,2},{2,3},{3,4},{4,5},{5,6},{6,7},{7,8},{8,9},{9,10},{10,1... | collective-permute-start | bytes 3145736 | tf_op jit(solution)/shard_map/ppermute | solution.py:14
  248.7 0.1 collective-permute-done.4
  248.8 0.1 bitcast_add_fusion.2
  249.0 1.3 collective-permute-start.5
  250.3 0.6 collective-permute-done.6
  250.9 0.1 bitcast_add_fusion
  251.0 29.5 %collective-permute-start.7 = (f32[1024,256]{1,0:T(8,128)S(1)}, f32[1024,256]{1,0:T(8,128)S(1)}, u32[]{:S(2)}, u32[]{:S(2)}) collective-permute-start(f32[1024,256]{1,0:T(8,128)S(1)} %bitcast_add_fusion), channel_id=1, source_target_pairs={{0,1},{1,2},{2,3},{3,4},{4,5},{5,6},{6,7},{7,8},{8,9},{9,10},{10,1... | collective-permute-start | bytes 3145736 | tf_op jit(solution)/shard_map/ppermute | solution.py:14
  280.5 1.0 convolution_bitcast_fusion
  281.6 0.3 fusion.18
  281.9 0.0 collective-permute-done.5
  281.9 0.8 collective-permute-done.7
  282.7 0.2 fusion.14
  283.0 1.0 convolution_bitcast_fusion.1
  284.0 0.0 all-reduce.3.cloned.1.call-update
  284.0 0.0 copy-done.2
  284.0 1.1 fusion.12
  285.2 108.1 %all-reduce.3.cloned.1.call-done = (f32[256,256]{0,1:T(8,128)}, f32[256,256]{0,1:T(8,128)}) async-done(((f32[256,256]{0,1:T(8,128)}, f32[256,256]{0,1:T(8,128)}), (f32[256,256]{0,1:T(8,128)}, f32[256,256]{0,1:T(8,128)})) %all-reduce.3.cloned.1.call-update) | async-done | bytes 524304 | tf_op jit(solution)/shard_map/psum | solution.py:72
  393.3 1.0 broadcast_multiply_fusion.1
  394.2 0.8 copy.20
  395.1 1.0 broadcast_multiply_fusion
  396.0 0.8 copy.21
  (4 shorter events, 0.1 us)
Async XLA Ops:
  7.2 1.0 copy-start
  7.2 386.1 %all-reduce.3.cloned.1.call-start = ((), (), s32[]{:S(2)}) async-start(), calls=%async_computation | async-start | bytes 1048576 | tf_op jit(solution)/shard_map/psum | solution.py:72
  9.4 21.4 %copy-start.1 = (bf16[1024,256]{1,0:T(8,128)(2,1)}, bf16[1024,256]{1,0:T(8,128)(2,1)S(1)}, u32[]{:S(2)}) copy-start(bf16[1024,256]{1,0:T(8,128)(2,1)S(1)} %convolution_convert_fusion) | copy-start | bytes 1572868
  9.4 5.0 %collective-permute-start = (bf16[1024,256]{1,0:T(8,128)(2,1)S(1)}, bf16[1024,256]{1,0:T(8,128)(2,1)S(1)}, u32[]{:S(2)}, u32[]{:S(2)}) collective-permute-start(bf16[1024,256]{1,0:T(8,128)(2,1)S(1)} %convolution_convert_fusion), channel_id=1, source_target_pairs={{0,1},{1,2},{2,3},{3,4},{4,5},{5,6},{6,7},{7,8},{8,9},{9,10},{10,1... | collective-permute-start | bytes 1572872 | tf_op jit(solution)/shard_map/ppermute | solution.py:14
  11.8 17.6 %collective-permute-start.2 = (bf16[1024,256]{1,0:T(8,128)(2,1)S(1)}, bf16[1024,256]{1,0:T(8,128)(2,1)}, u32[]{:S(2)}, u32[]{:S(2)}) collective-permute-start(bf16[1024,256]{1,0:T(8,128)(2,1)S(1)} %convolution_convert_fusion), channel_id=1, source_target_pairs={{1,0},{2,1},{3,2},{4,3},{5,4},{6,5},{7,6},{8,7},{9,8},{10,9},{11,1... | collective-permute-start | bytes 1572872 | tf_op jit(solution)/shard_map/ppermute | solution.py:14
  14.5 16.3 %copy-start.3 = (bf16[1024,256]{1,0:T(8,128)(2,1)}, bf16[1024,256]{1,0:T(8,128)(2,1)S(1)}, u32[]{:S(2)}) copy-start(bf16[1024,256]{1,0:T(8,128)(2,1)S(1)} %collective-permute-done) | copy-start | bytes 1572868
  14.5 16.3 %collective-permute-start.1 = (bf16[1024,256]{1,0:T(8,128)(2,1)S(1)}, bf16[1024,256]{1,0:T(8,128)(2,1)S(1)}, u32[]{:S(2)}, u32[]{:S(2)}) collective-permute-start(bf16[1024,256]{1,0:T(8,128)(2,1)S(1)} %collective-permute-done), channel_id=1, source_target_pairs={{0,1},{1,2},{2,3},{3,4},{4,5},{5,6},{6,7},{7,8},{8,9},{9,10},{10,1... | collective-permute-start | bytes 1572872 | tf_op jit(solution)/shard_map/ppermute | solution.py:14
  29.5 6.0 %collective-permute-start.3 = (bf16[1024,256]{1,0:T(8,128)(2,1)}, bf16[1024,256]{1,0:T(8,128)(2,1)S(1)}, u32[]{:S(2)}, u32[]{:S(2)}) collective-permute-start(bf16[1024,256]{1,0:T(8,128)(2,1)} %collective-permute-done.2), channel_id=1, source_target_pairs={{1,0},{2,1},{3,2},{4,3},{5,4},{6,5},{7,6},{8,7},{9,8},{10,9},{11,1... | collective-permute-start | bytes 1572872 | tf_op jit(solution)/shard_map/ppermute | solution.py:14
  86.1 36.1 %copy-start.4 = (bf16[256,256]{1,0:T(8,128)(2,1)S(1)}, bf16[256,256]{1,0:T(8,128)(2,1)}, u32[]{:S(2)}) copy-start(bf16[256,256]{1,0:T(8,128)(2,1)} %param.10) | copy-start | bytes 393220
  86.1 36.1 %copy-start.5 = (bf16[1024,256]{1,0:T(8,128)(2,1)S(1)}, bf16[1024,256]{1,0:T(8,128)(2,1)}, u32[]{:S(2)}) copy-start(bf16[1024,256]{1,0:T(8,128)(2,1)} %param.15) | copy-start | bytes 1572868
  231.6 52.4 %copy-start.2 = (bf16[256,256]{1,0:T(8,128)(2,1)S(1)}, bf16[256,256]{1,0:T(8,128)(2,1)}, u32[]{:S(2)}) copy-start(bf16[256,256]{1,0:T(8,128)(2,1)} %param.9) | copy-start | bytes 393220
  234.4 14.4 %collective-permute-start.4 = (f32[1024,256]{1,0:T(8,128)S(1)}, f32[1024,256]{1,0:T(8,128)S(1)}, u32[]{:S(2)}, u32[]{:S(2)}) collective-permute-start(f32[1024,256]{1,0:T(8,128)S(1)} %bitcast.43), channel_id=1, source_target_pairs={{1,0},{2,1},{3,2},{4,3},{5,4},{6,5},{7,6},{8,7},{9,8},{10,9},{11,1... | collective-permute-start | bytes 3145736 | tf_op jit(solution)/shard_map/ppermute | solution.py:14
  235.7 15.1 %collective-permute-start.6 = (f32[1024,256]{1,0:T(8,128)S(1)}, f32[1024,256]{1,0:T(8,128)S(1)}, u32[]{:S(2)}, u32[]{:S(2)}) collective-permute-start(f32[1024,256]{1,0:T(8,128)S(1)} %bitcast.42), channel_id=1, source_target_pairs={{0,1},{1,2},{2,3},{3,4},{4,5},{5,6},{6,7},{7,8},{8,9},{9,10},{10,1... | collective-permute-start | bytes 3145736 | tf_op jit(solution)/shard_map/ppermute | solution.py:14
  249.0 32.9 %collective-permute-start.5 = (f32[1024,256]{1,0:T(8,128)S(1)}, f32[1024,256]{1,0:T(8,128)S(1)}, u32[]{:S(2)}, u32[]{:S(2)}) collective-permute-start(f32[1024,256]{1,0:T(8,128)S(1)} %bitcast_add_fusion.2), channel_id=1, source_target_pairs={{1,0},{2,1},{3,2},{4,3},{5,4},{6,5},{7,6},{8,7},{9,8},{10,9},{11,1... | collective-permute-start | bytes 3145736 | tf_op jit(solution)/shard_map/ppermute | solution.py:14
  251.0 31.7 %collective-permute-start.7 = (f32[1024,256]{1,0:T(8,128)S(1)}, f32[1024,256]{1,0:T(8,128)S(1)}, u32[]{:S(2)}, u32[]{:S(2)}) collective-permute-start(f32[1024,256]{1,0:T(8,128)S(1)} %bitcast_add_fusion), channel_id=1, source_target_pairs={{0,1},{1,2},{2,3},{3,4},{4,5},{5,6},{6,7},{7,8},{8,9},{9,10},{10,1... | collective-permute-start | bytes 3145736 | tf_op jit(solution)/shard_map/ppermute | solution.py:14
Sparse Core Ops, SparseCore 0:
  284.1 109.0 all-reduce.2
where the time goes:
time: 406 us; the launch traced here: 404 us
  waiting for transfers between devices  111 us (27%)
  other arithmetic  97.7 us (24%)
  local copies, waits for them, and re-layouts  77.7 us (19%)
  starting transfers between devices  63.6 us (16%)
  matrix products  38.7 us (10%)
  between operations  14.9 us (4%)
    psum x1, waiting for transfers between devices, body(): total_weight, total_root = lax.psum((local_weight, local_root), 'row')  108 us
    scatter-add x2, other arithmetic, tile_products(): return zeroed.at[put_index].add(products * slot_live[:, None, None])  93.2 us
    ppermute x8, starting transfers between devices, from_behind(): return lax.ppermute(block, axis, route)  63.5 us
    mul x2, local copies, waits for them, and re-layouts, tile_products(): return zeroed.at[put_index].add(products * slot_live[:, None, None])  49.3 us
    dot_general x2, matrix products, tile_products(): jnp.einsum(formula, block_tiles, picked, preferred_element_type=jnp.float32)  32.5 us
    gather x2, local copies, waits for them, and re-layouts, tile_products(): picked = jnp.take(sources, take_index, axis=0)  16.4 us
  transfers between devices with their start and end apart: 9, of which 5 were waited for; matrix products, arithmetic and copies ran while one was open for 2% of the time, Pallas kernels for 0%

commit v1 on v0

v1 whole, which is shorter than its diff:
```python
import functools
import math

import jax
import jax.numpy as jnp
from jax import lax
from jax.experimental import pallas as pl
from jax.experimental.pallas import tpu as pltpu
from jax.sharding import PartitionSpec as P

REACH = 2
F32, BF16 = jnp.float32, jnp.bfloat16

OWN, OWN_X, SIDE, SIDE_X, PLANE, PLANE_X = range(6)
PARTS = 6


def vmem_spec():
    return pl.BlockSpec(memory_space=pltpu.VMEM)


def smem_spec():
    return pl.BlockSpec(memory_space=pltpu.SMEM)


def in_vmem(array):
    return pltpu.with_memory_space_constraint(array, pltpu.VMEM)


def kernel_call(kernel, name, outs, args, flops, bytes_accessed=1 << 20):
    return pl.pallas_call(
        kernel,
        out_shape=[pltpu.VMEM(shape, dtype) for shape, dtype in outs],
        in_specs=[vmem_spec()] * len(args),
        out_specs=[vmem_spec()] * len(outs),
        compiler_params=pltpu.CompilerParams(vmem_limit_bytes=12 << 20),
        cost_estimate=pl.CostEstimate(flops=flops, bytes_accessed=bytes_accessed, transcendentals=0),
        name=name,
    )(*[in_vmem(a) for a in args])


def flip_core(array, count):
    return lax.ppermute(array, "row", [(i, i ^ 1) for i in range(count)])


def flip_side(array, count):
    return lax.ppermute(array, "row", [(i, i ^ 2) for i in range(count)])


def over_planes(array, count, back):
    step = [(i, i + 4) for i in range(count) if i % 4 < 2 and i + 4 < count]
    step += [(i, i - 4) for i in range(count) if i % 4 >= 2 and i >= 4]
    return lax.ppermute(array, "row", [(b, a) for a, b in step] if back else step)


def dense_kernel(stripe_ref, rows_ref, cols_ref, count_ref, tiles_ref, a_ref, sem):
    block = tiles_ref.shape[1]
    width = a_ref.shape[1]
    blocks = width // block
    stripe = stripe_ref[0]
    core, side = stripe & 1, (stripe >> 1) & 1
    first = (stripe >> 1) * (2 * blocks)
    live = count_ref[0]

    def clear(i, carry):
        for part in range(PARTS):
            a_ref[part, pl.ds(pl.multiple_of(i * 64, 64), 64), :] = jnp.zeros((64, width), BF16)
        return carry

    def placed(slot):
        away = cols_ref[slot] - first + 2 * blocks
        chip = away // (2 * blocks)
        within = away - chip * (2 * blocks)
        other = within // blocks
        column = within - other * blocks
        near = jnp.where(side == 0, 2, 0)
        part = jnp.where(chip == 1, OWN, jnp.where(chip == near, SIDE, PLANE)) + (other ^ core)
        target = a_ref.at[
            part,
            pl.ds(pl.multiple_of(rows_ref[slot] * block, block), block),
            pl.ds(pl.multiple_of(column * block, block), block),
        ]
        return pltpu.make_async_copy(tiles_ref.at[slot], target, sem)

    def start(slot, carry):
        placed(slot).start()
        return carry

    def finish(slot, carry):
        placed(slot).wait()
        return carry

    lax.fori_loop(0, width // 64, clear, 0)
    lax.fori_loop(0, live, start, 0)
    lax.fori_loop(0, live, finish, 0)


def dense_adjacency(stripe, tile_rows, tile_cols, tile_count, block_tiles, width):
    return pl.pallas_call(
        dense_kernel,
        out_shape=pltpu.VMEM((PARTS, width, width), BF16),
        in_specs=[smem_spec()] * 4 + [pl.BlockSpec(memory_space=pl.ANY)],
        out_specs=vmem_spec(),
        scratch_shapes=[pltpu.SemaphoreType.DMA],
        compiler_params=pltpu.CompilerParams(vmem_limit_bytes=12 << 20),
        cost_estimate=pl.CostEstimate(flops=0, bytes_accessed=20 << 20, transcendentals=0),
        name="dense_adjacency",
    )(stripe, tile_rows, tile_cols, tile_count, block_tiles)


def dot(a, b):
    return jnp.dot(a, b, preferred_element_type=F32)


def dot_nt(a, b):
    return lax.dot_general(a, b, (((1,), (1,)), ((), ())), preferred_element_type=F32)


def gather_kernel(terms, started, *refs):
    a_ref, out_ref = refs[0], refs[-1]
    sources = refs[1:-1]
    total = sources[-1][...] if started else None
    for (part, low), source in zip(terms, sources):
        product = dot(a_ref[part, :, low : low + source.shape[0]], source[...])
        total = product if total is None else total + product
    out_ref[...] = total


def gathered(dense, terms, sources, total, name):
    rows, width = dense.shape[1], sources[0].shape[1]
    args = [dense, *sources] + ([] if total is None else [total])
    flops = sum(2 * rows * s.shape[0] * width for s in sources)
    return kernel_call(
        functools.partial(gather_kernel, terms, total is not None), name, [((rows, width), F32)], args, flops
    )[0]


def middle_kernel(
    half, a_ref, last_ref, total_ref, x_ref, w_ref, r_ref, cot_ref,
    out_ref, grad_ref, ax_ref, ht_ref, low_ref, high_ref,
):
    rows = x_ref.shape[0]
    step = 256
    for at in range(0, rows, step):
        here = slice(at, at + step)
        ax = total_ref[here, :] + dot(a_ref[PLANE_X, here, half:], last_ref[...])
        ax = ax.astype(BF16)
        ax_ref[here, :] = ax
        pre = dot(ax, w_ref[...]) + dot(x_ref[here, :], r_ref[...])
        gate = jax.nn.sigmoid(pre)
        out_ref[here, :] = (pre * gate).astype(BF16)
        grad = (cot_ref[here, :].astype(F32) * (gate * (1.0 + pre * (1.0 - gate)))).astype(BF16)
        grad_ref[here, :] = grad
        ht_ref[:, here] = dot_nt(w_ref[...], grad).astype(BF16)
    low_ref[...] = dot(ht_ref[...], a_ref[PLANE_X, :, :half]).T.astype(BF16)
    high_ref[...] = dot(ht_ref[...], a_ref[PLANE_X, :, half:]).T.astype(BF16)


def spread_kernel(part, half, a_ref, ht_ref, low_ref, high_ref):
    low_ref[...] = dot(ht_ref[...], a_ref[part, :, :half]).T.astype(low_ref.dtype)
    high_ref[...] = dot(ht_ref[...], a_ref[part, :, half:]).T.astype(high_ref.dtype)


def spread(dense, ht, part, half, dtype, name):
    rows, width = dense.shape[1], ht.shape[0]
    return kernel_call(
        functools.partial(spread_kernel, part, half),
        name,
        [((half, width), dtype), ((rows - half, width), dtype)],
        [dense, ht],
        2 * rows * rows * width,
    )


def own_kernel(half, a_ref, ht_ref, grad_ref, r_ref, low_ref, high_ref):
    for out, here in ((low_ref, slice(0, half)), (high_ref, slice(half, None))):
        out[...] = dot(ht_ref[...], a_ref[OWN, :, here]).T + dot_nt(grad_ref[here, :], r_ref[...])


def final_kernel(half, own0_ref, own1_ref, x0_ref, x1_ref, in0_ref, in1_ref, out_ref):
    out_ref[:half, :] = (own0_ref[...] + x0_ref[...].astype(F32) + in0_ref[...].astype(F32)).astype(BF16)
    out_ref[half:, :] = (own1_ref[...] + x1_ref[...].astype(F32) + in1_ref[...].astype(F32)).astype(BF16)


def added(a, b, name):
    return (a.astype(F32) + b.astype(F32)).astype(BF16)


def weight_sums(local_weight, local_root, core, side, count):
    kept = jnp.where(core == 0, local_weight, local_root)
    kept = kept + flip_core(jnp.where(core == 0, local_root, local_weight), count)
    half = kept.shape[0] // 2
    top, bottom = kept[:half], kept[half:]
    part = jnp.where(side == 0, top, bottom) + flip_side(jnp.where(side == 0, bottom, top), count)
    hop = 4
    while hop < count:
        part = part + lax.ppermute(part, "row", [(i, i ^ hop) for i in range(count)])
        hop *= 2
    other = flip_side(part, count)
    kept = jnp.concatenate([jnp.where(side == 0, part, other), jnp.where(side == 0, other, part)], axis=0)
    other = flip_core(kept, count)
    return jnp.where(core == 0, kept, other), jnp.where(core == 0, other, kept)


def body(features, weight, root_weight, block_tiles, tile_rows, tile_cols, tile_count, cotangent):
    count = lax.axis_size("row")
    rows, width = features.shape
    half = rows // 2
    index = lax.axis_index("row").astype(jnp.int32)
    core, side = index & 1, (index >> 1) & 1

    low, high = features[:half], features[half:]
    side_low = flip_side(low, count)
    side_high = flip_side(high, count)
    own_x = flip_core(features, count)
    plane_low = over_planes(side_low, count, False)
    plane_high = over_planes(side_high, count, False)
    side_x_low = flip_core(side_low, count)
    side_x_high = flip_core(side_high, count)
    plane_x_low = flip_core(plane_low, count)
    plane_x_high = flip_core(plane_high, count)

    dense = dense_adjacency(index.reshape(1), tile_rows, tile_cols, tile_count, block_tiles, rows)
    total = gathered(dense, [(OWN, 0), (OWN_X, 0)], [features, own_x], None, "gather_own")
    total = gathered(
        dense,
        [(SIDE, 0), (SIDE, half), (SIDE_X, 0), (SIDE_X, half)],
        [side_low, side_high, side_x_low, side_x_high],
        total,
        "gather_side",
    )
    total = gathered(
        dense,
        [(PLANE, 0), (PLANE_X, 0), (PLANE, half)],
        [plane_low, plane_x_low, plane_high],
        total,
        "gather_plane",
    )
    layer_out, grad_pre, gathered_x, ht, px_low, px_high = kernel_call(
        functools.partial(middle_kernel, half),
        "middle",
        [
            ((rows, width), BF16),
            ((rows, width), BF16),
            ((rows, width), BF16),
            ((width, rows), BF16),
            ((half, width), BF16),
            ((rows - half, width), BF16),
        ],
        [dense, plane_x_high, total, features, weight, root_weight, cotangent],
        3 * 2 * rows * rows * width,
    )

    px_low, px_high = flip_core(px_low, count), flip_core(px_high, count)
    p_low, p_high = spread(dense, ht, PLANE, half, BF16, "spread_plane")
    far_low = over_planes(added(p_low, px_low, "low"), count, True)
    far_high = over_planes(added(p_high, px_high, "high"), count, True)
    sx_low, sx_high = spread(dense, ht, SIDE_X, half, BF16, "spread_side_x")
    sx_low, sx_high = flip_core(sx_low, count), flip_core(sx_high, count)
    s_low, s_high = spread(dense, ht, SIDE, half, F32, "spread_side")
    s_low, s_high = s_low + sx_low.astype(F32), s_high + sx_high.astype(F32)
    ox_low, ox_high = spread(dense, ht, OWN_X, half, BF16, "spread_own_x")
    ox_low, ox_high = flip_core(ox_low, count), flip_core(ox_high, count)
    own_low, own_high = kernel_call(
        functools.partial(own_kernel, half),
        "spread_own",
        [((half, width), F32), ((rows - half, width), F32)],
        [dense, ht, grad_pre, root_weight],
        3 * rows * rows * width,
    )
    in_low = flip_side(added(s_low, far_low, "low"), count)
    in_high = flip_side(added(s_high, far_high, "high"), count)

    grad_scale = 1.0 / math.sqrt(count * rows)
    local_weight = jnp.einsum("nf,ng->fg", gathered_x, grad_pre, preferred_element_type=F32)
    local_root = jnp.einsum("nf,ng->fg", features, grad_pre, preferred_element_type=F32)
    total_weight, total_root = weight_sums(local_weight, local_root, core, side, count)

    grad_features = kernel_call(
        functools.partial(final_kernel, half),
        "final",
        [((rows, width), BF16)],
        [own_low, own_high, ox_low, ox_high, in_low, in_high],
        rows * width * 4,
    )[0]
    return layer_out, grad_features, total_weight * grad_scale, total_root * grad_scale


def solution(mesh):
    placed = (
        P(("groups", "row"), None),
        P(),
        P(),
        P(("groups", "row"), None, None),
        P(("groups", "row")),
        P(("groups", "row")),
        P(("groups", "row")),
        P(("groups", "row"), None),
    )
    return jax.shard_map(
        body,
        mesh=mesh,
        in_specs=placed,
        out_specs=(
            P(("groups", "row"), None),
            P(("groups", "row"), None),
            P("groups", None),
            P("groups", None),
        ),
        check_vma=False,
    )
```

time: 406 us -> 93.3 us (0.23)
  other arithmetic: 97.7 us -> 1.3 us
  waiting for transfers between devices: 111 us -> 34.7 us
  local copies, waits for them, and re-layouts: 77.7 us -> 11.5 us
  matrix products: 38.7 us -> 1.4 us
  starting transfers between devices: 63.6 us -> 29.8 us
  Pallas kernels: 0 us -> 13.6 us
  between operations: 14.9 us -> 1.7 us
    psum x1 -> x0, waiting for transfers between devices: 108 us -> none  [body(): total_weight, total_root = lax.psum((local_weight, local_root), 'row')]
    scatter-add x2 -> x0, other arithmetic: 93.2 us -> none  [tile_products(): return zeroed.at[put_index].add(products * slot_live[:, None, None])]
    mul x2 -> x0, local copies, waits for them, and re-layouts: 49.3 us -> none  [tile_products(): return zeroed.at[put_index].add(products * slot_live[:, None, None])]
    dot_general x8 -> x2, matrix products: 38.7 us -> 1.4 us  [the longest x1 1.06 us: body(): jnp.einsum('nf,ng->fg', features, grad_pre, preferred_element_type=F32)]
    ppermute x8 -> x25, starting transfers between devices: 63.5 us -> 29.8 us  [the longest x4 10.3 us: over_planes(): lax.ppermute(array, 'row', [(b, a) for a, b in step] if back else step)]
    ppermute x8 -> x25, waiting for transfers between devices: 2.93 us -> 34.7 us  [the longest x6 21.5 us: flip_side(): return lax.ppermute(array, 'row', [(i, i ^ 2) for i in range(count)])]
    gather x2 -> x0, local copies, waits for them, and re-layouts: 16.4 us -> none  [tile_products(): picked = jnp.take(sources, take_index, axis=0)]
    pallas_call x0 -> x11, Pallas kernels: none -> 13.6 us  [the longest x10 10.1 us: kernel_call(): pl.pallas_call(kernel, out_shape=[pltpu.VMEM(shape, dtype) for shape, dty...]
  transfers between devices with their start and end apart: 9 -> 25, of which waited for: 5 -> 7; matrix products, arithmetic and copies ran while one was open for 2% -> 2% of each run, Pallas kernels for 0% -> 12%
where the time goes in v1:
time: 93.3 us; the launch traced here: 93.9 us
  waiting for transfers between devices  34.7 us (37%)
  starting transfers between devices  29.8 us (32%)
  Pallas kernels  13.6 us (15%)
  local copies, waits for them, and re-layouts  11.5 us (12%)
  between operations  1.7 us (2%)
  matrix products  1.4 us (2%)
  other arithmetic  1.3 us (1%)
    ppermute x6, waiting for transfers between devices, flip_side(): return lax.ppermute(array, 'row', [(i, i ^ 2) for i in range(count)])  21.5 us
    ppermute x2, waiting for transfers between devices, weight_sums(): lax.ppermute(part, 'row', [(i, i ^ hop) for i in range(count)])  13.1 us
    unnamed x26, local copies, waits for them, and re-layouts  10.3 us
    ppermute x4, starting transfers between devices, over_planes(): lax.ppermute(array, 'row', [(b, a) for a, b in step] if back else step)  10.3 us
    pallas_call x10, Pallas kernels, kernel_call(): pl.pallas_call(kernel, out_shape=[pltpu.VMEM(shape, dtype) for shape, dty...  10.1 us
    ppermute x6, starting transfers between devices, flip_side(): return lax.ppermute(array, 'row', [(i, i ^ 2) for i in range(count)])  9.21 us
    ppermute x2, starting transfers between devices, weight_sums(): lax.ppermute(part, 'row', [(i, i ^ hop) for i in range(count)])  5.81 us
    ppermute x13, starting transfers between devices, flip_core(): return lax.ppermute(array, 'row', [(i, i ^ 1) for i in range(count)])  4.48 us
  transfers between devices with their start and end apart: 25, of which 7 were waited for; matrix products, arithmetic and copies ran while one was open for 2% of the time, Pallas kernels for 12%

profile of v1, /device:TPU:0, one launch (start us, length us, event | category | flops | bytes accessed | tf_op | source)
XLA Modules:
  0.0 93.9 jit_solution(15276220254521810534)
XLA Ops:
  0.6 0.0 copy-start.2
  0.6 1.1 %fusion = (bf16[512,256]{1,0:T(8,128)(2,1)S(1)}, bf16[512,256]{1,0:T(8,128)(2,1)S(1)}) fusion(bf16[1024,256]{1,0:T(8,128)(2,1)} %x_ref.1), kind=kLoop, calls=%fused_computation.14 | loop fusion | bytes 1048576 | tf_op jit(solution)/shard_map/slice | solution.py:212
  1.8 3.0 %collective-permute-start.3 = (bf16[512,256]{1,0:T(8,128)(2,1)S(1)}, bf16[512,256]{1,0:T(8,128)(2,1)S(1)}, u32[]{:S(2)}, u32[]{:S(2)}) collective-permute-start(bf16[512,256]{1,0:T(8,128)(2,1)S(1)} %get-tuple-element.38), channel_id=1, source_target_pairs={{0,2},{1,3},{2,0},{3,1},{4,6},{5,7},{6,4},{7,5},{8,10},{9,11},{10,... | collective-permute-start | bytes 786440 | tf_op jit(solution)/shard_map/ppermute | solution.py:47
  4.8 0.1 collective-permute-start
  4.9 7.1 %collective-permute-done.3.refs_1_ = bf16[512,256]{1,0:T(8,128)(2,1)S(1)} collective-permute-done((bf16[512,256]{1,0:T(8,128)(2,1)S(1)}, bf16[512,256]{1,0:T(8,128)(2,1)S(1)}, u32[]{:S(2)}, u32[]{:S(2)}) %collective-permute-start.3) | collective-permute-done | bytes 262176 | tf_op jit(solution)/shard_map/ppermute | solution.py:47
  11.9 4.0 %collective-permute-start.4 = (bf16[512,256]{1,0:T(8,128)(2,1)S(1)}, bf16[512,256]{1,0:T(8,128)(2,1)S(1)}, u32[]{:S(2)}, u32[]{:S(2)}) collective-permute-start(bf16[512,256]{1,0:T(8,128)(2,1)S(1)} %collective-permute-done.3.refs_1_), channel_id=1, source_target_pairs={{0,4},{1,5},{4,8},{5,9},{8,12},{9,13},{6,2},{7,3},{10,6},{11,7},{1... | collective-permute-start | bytes 786440 | tf_op jit(solution)/shard_map/ppermute | solution.py:53
  16.0 0.8 collective-permute-done.refs_2_
  16.7 3.7 %collective-permute-start.1 = (bf16[512,256]{1,0:T(8,128)(2,1)S(1)}, bf16[512,256]{1,0:T(8,128)(2,1)S(1)}, u32[]{:S(2)}, u32[]{:S(2)}) collective-permute-start(bf16[512,256]{1,0:T(8,128)(2,1)S(1)} %collective-permute-done.refs_2_), channel_id=1, source_target_pairs={{0,4},{1,5},{4,8},{5,9},{8,12},{9,13},{6,2},{7,3},{10,6},{11,7},{1... | collective-permute-start | bytes 786440 | tf_op jit(solution)/shard_map/ppermute | solution.py:53
  20.4 0.1 collective-permute-start.6
  20.5 0.5 collective-permute-start.7
  21.0 0.0 collective-permute-done.4.refs_1_
  21.0 0.1 collective-permute-start.5
  21.7 0.0 copy-start.3
  21.8 2.8 %copy-done.3 = bf16[192,128,128]{2,1,0:T(8,128)(2,1)S(1)} copy-done((bf16[192,128,128]{2,1,0:T(8,128)(2,1)S(1)}, bf16[192,128,128]{2,1,0:T(8,128)(2,1)}, u32[]{:S(2)}) %copy-start.3) | copy-done | bytes 6291480
  24.5 0.7 copy-done.7
  25.2 0.7 copy-done.8
  25.9 3.5 %dense_adjacency.1.refs_0_.a_ref = bf16[6,1024,1024]{2,1,0:T(8,128)(2,1)S(1)} custom-call(s32[1]{0:T(128)} %bitcast.stripe_ref, s32[192]{0:T(256)S(1)} %copy-done.7, s32[192]{0:T(256)S(1)} %copy-done.8, s32[1]{0:T(128)S(6)} %copy.14.count_ref, bf16[192,128,128]{2,1,0:T(8,128)(2,1)S(1)} %copy-done.3), custom_call_target="tpu_custom_call" | custom-call | bytes 20971520 | tf_op jit(solution)/shard_map/dense_adjacency/pallas_call | solution.py:99
  29.4 1.2 %collective-permute-start.2 = (bf16[512,256]{1,0:T(8,128)(2,1)S(1)}, bf16[512,256]{1,0:T(8,128)(2,1)S(1)}, u32[]{:S(2)}, u32[]{:S(2)}) collective-permute-start(bf16[512,256]{1,0:T(8,128)(2,1)S(1)} %collective-permute-done.1.refs_3_), channel_id=1, source_target_pairs={{0,1},{1,0},{2,3},{3,2},{4,5},{5,4},{6,7},{7,6},{8,9},{9,8},{10,11... | collective-permute-start | bytes 786440 | tf_op jit(solution)/shard_map/ppermute | solution.py:43
  30.7 1.2 %gather_own.1.refs_5_ = f32[1024,256]{1,0:T(8,128)S(1)} custom-call(bf16[6,1024,1024]{2,1,0:T(8,128)(2,1)S(1)} %dense_adjacency.1.refs_0_.a_ref, bf16[1024,256]{1,0:T(8,128)(2,1)S(1)} %copy-done.2, bf16[1024,256]{1,0:T(8,128)(2,1)S(1)} %collective-permute-done.8.refs_2_), custom_call_target="tpu_custom_call" | custom-call | flops 1073741824 | bytes 1048576 | tf_op jit(solution)/shard_map/gather_own/pallas_call | solution.py:31
  31.9 0.0 copy-start.4
  31.9 0.0 copy-start.5
  32.0 0.0 copy-start.6
  32.0 0.0 collective-permute-done.6.refs_3_
  32.0 1.3 %gather_side.1.refs_4_ = f32[1024,256]{1,0:T(8,128)S(1)} custom-call(bf16[6,1024,1024]{2,1,0:T(8,128)(2,1)S(1)} %dense_adjacency.1.refs_0_.a_ref, bf16[512,256]{1,0:T(8,128)(2,1)S(1)} %collective-permute-done.3.refs_1_, bf16[512,256]{1,0:T(8,128)(2,1)S(1)} %collective-permute-done.refs_2_, bf16[512,256]{1,0:T(8,128)(2,1)S(1)} %collective-permute-done.6.refs_3_, ...), custom_call_target="tpu_custom_call" | custom-call | flops 1073741824 | bytes 1048576 | tf_op jit(solution)/shard_map/gather_side/pallas_call | solution.py:31
  33.3 0.0 collective-permute-done.5.refs_2_
  33.3 1.0 %gather_plane.1.total_ref = f32[1024,256]{1,0:T(8,128)S(1)} custom-call(bf16[6,1024,1024]{2,1,0:T(8,128)(2,1)S(1)} %dense_adjacency.1.refs_0_.a_ref, bf16[512,256]{1,0:T(8,128)(2,1)S(1)} %collective-permute-done.4.refs_1_, bf16[512,256]{1,0:T(8,128)(2,1)S(1)} %collective-permute-done.5.refs_2_, bf16[512,256]{1,0:T(8,128)(2,1)S(1)} %collective-permute-done.1.refs_3_, ...), custom_call_target="tpu_custom_call" | custom-call | flops 805306368 | bytes 1048576 | tf_op jit(solution)/shard_map/gather_plane/pallas_call | solution.py:31
  34.2 0.0 collective-permute-done.2.last_ref
  34.3 2.4 %middle.1 = (bf16[1024,256]{1,0:T(8,128)(2,1)S(1)}, bf16[1024,256]{1,0:T(8,128)(2,1)S(1)}, bf16[1024,256]{1,0:T(8,128)(2,1)S(1)}, bf16[256,1024]{1,0:T(8,128)(2,...) custom-call(bf16[6,1024,1024]{2,1,0:T(8,128)(2,1)S(1)} %dense_adjacency.1.refs_0_.a_ref, ...), custom_call_target="tpu_custom_call" | custom-call | flops 1610612736 | bytes 1048576 | tf_op jit(solution)/shard_map/middle/pallas_call | solution.py:31
  36.7 0.3 fusion.1
  37.0 1.1 %broadcast_select_fusion = (f32[256,256]{1,0:T(8,128)}, f32[256,256]{1,0:T(8,128)S(1)}) fusion(f32[256,256]{1,0:T(8,128)S(1)} %fusion.1, pred[]{:T(512)S(6)} %eq.4, bf16[1024,256]{1,0:T(8,128)(2,1)S(1)} %get-tuple-element.22.grad_ref, bf16[1024,256]{1,0:T(8,128)(2,1)S(1)} %copy-done.2), kind=kOutput, calls=%fused_computation.10 | convolution fusion | flops 134283264 | bytes 1835009 | tf_op jit(solution)/shard_map/nf,ng->fg/dot_general | solution.py:276
  38.1 0.9 collective-permute-start.19
  38.9 4.6 %copy-done.1 = bf16[6,1024,1024]{2,1,0:T(8,128)(2,1)S(1)} copy-done((bf16[6,1024,1024]{2,1,0:T(8,128)(2,1)S(1)}, bf16[6,1024,1024]{2,1,0:T(8,128)(2,1)}, u32[]{:S(2)}) %copy-start.1) | copy-done | bytes 12582936
  43.5 0.8 spread_side_x.1
  44.3 0.6 collective-permute-start.15
  44.9 0.1 collective-permute-start.12
  44.9 0.4 collective-permute-start.11
  45.4 0.8 spread_plane.1
  46.2 0.8 spread_side.1
  47.0 0.1 select_add_fusion
  47.1 3.1 %collective-permute-start.20 = (f32[128,256]{1,0:T(8,128)S(1)}, f32[128,256]{1,0:T(8,128)S(1)}, u32[]{:S(2)}, u32[]{:S(2)}) collective-permute-start(f32[128,256]{1,0:T(8,128)S(1)} %slice_select_fusion), channel_id=1, source_target_pairs={{0,2},{1,3},{2,0},{3,1},{4,6},{5,7},{6,4},{7,5},{8,10},{9,11},{10,... | collective-permute-start | bytes 393224 | tf_op jit(solution)/shard_map/ppermute | solution.py:47
  50.2 0.1 add_convert_fusion.1
  50.3 1.3 %collective-permute-start.17 = (bf16[512,256]{1,0:T(8,128)(2,1)S(1)}, bf16[512,256]{1,0:T(8,128)(2,1)S(1)}, u32[]{:S(2)}, u32[]{:S(2)}) collective-permute-start(bf16[512,256]{1,0:T(8,128)(2,1)S(1)} %add_convert_fusion.1), channel_id=1, source_target_pairs={{4,0},{5,1},{8,4},{9,5},{12,8},{13,9},{2,6},{3,7},{6,10},{7,11},{1... | collective-permute-start | bytes 786440 | tf_op jit(solution)/shard_map/ppermute | solution.py:53
  51.6 2.4 %collective-permute-done.20 = f32[128,256]{1,0:T(8,128)S(1)} collective-permute-done((f32[128,256]{1,0:T(8,128)S(1)}, f32[128,256]{1,0:T(8,128)S(1)}, u32[]{:S(2)}, u32[]{:S(2)}) %collective-permute-start.20) | collective-permute-done | bytes 131104 | tf_op jit(solution)/shard_map/ppermute | solution.py:47
  54.0 4.6 %collective-permute-start.21 = (f32[128,256]{1,0:T(8,128)S(1)}, f32[128,256]{1,0:T(8,128)S(1)}, u32[]{:S(2)}, u32[]{:S(2)}) collective-permute-start(f32[128,256]{1,0:T(8,128)S(1)} %select_add_fusion.1), channel_id=1, source_target_pairs={{0,4},{1,5},{2,6},{3,7},{4,0},{5,1},{6,2},{7,3},{8,12},{9,13},{10,... | collective-permute-start | bytes 393224 | tf_op jit(solution)/shard_map/ppermute | solution.py:197
  58.6 0.1 add_convert_fusion.3
  58.7 1.3 %collective-permute-start.13 = (bf16[512,256]{1,0:T(8,128)(2,1)S(1)}, bf16[512,256]{1,0:T(8,128)(2,1)S(1)}, u32[]{:S(2)}, u32[]{:S(2)}) collective-permute-start(bf16[512,256]{1,0:T(8,128)(2,1)S(1)} %add_convert_fusion.3), channel_id=1, source_target_pairs={{4,0},{5,1},{8,4},{9,5},{12,8},{13,9},{2,6},{3,7},{6,10},{7,11},{1... | collective-permute-start | bytes 786440 | tf_op jit(solution)/shard_map/ppermute | solution.py:53
  60.0 0.8 spread_own_x.1
  60.8 5.4 %collective-permute-done.21 = f32[128,256]{1,0:T(8,128)S(1)} collective-permute-done((f32[128,256]{1,0:T(8,128)S(1)}, f32[128,256]{1,0:T(8,128)S(1)}, u32[]{:S(2)}, u32[]{:S(2)}) %collective-permute-start.21) | collective-permute-done | bytes 131104 | tf_op jit(solution)/shard_map/ppermute | solution.py:197
  66.2 0.6 collective-permute-start.9
  66.8 1.2 %collective-permute-start.22 = (f32[128,256]{1,0:T(8,128)S(1)}, f32[128,256]{1,0:T(8,128)S(1)}, u32[]{:S(2)}, u32[]{:S(2)}) collective-permute-start(f32[128,256]{1,0:T(8,128)S(1)} %add.38), channel_id=1, source_target_pairs={{0,8},{1,9},{2,10},{3,11},{4,12},{5,13},{6,14},{7,15},{8,0},{9,1},... | collective-permute-start | bytes 393224 | tf_op jit(solution)/shard_map/ppermute | solution.py:197
  68.0 0.1 add_convert_fusion
  68.1 7.7 %collective-permute-done.22 = f32[128,256]{1,0:T(8,128)S(1)} collective-permute-done((f32[128,256]{1,0:T(8,128)S(1)}, f32[128,256]{1,0:T(8,128)S(1)}, u32[]{:S(2)}, u32[]{:S(2)}) %collective-permute-start.22) | collective-permute-done | bytes 131104 | tf_op jit(solution)/shard_map/ppermute | solution.py:197
  75.8 0.8 collective-permute-start.18
  76.6 1.3 %collective-permute-start.23 = (f32[128,256]{1,0:T(8,128)S(1)}, f32[128,256]{1,0:T(8,128)S(1)}, u32[]{:S(2)}, u32[]{:S(2)}) collective-permute-start(f32[128,256]{1,0:T(8,128)S(1)} %add.39), channel_id=1, source_target_pairs={{0,2},{1,3},{2,0},{3,1},{4,6},{5,7},{6,4},{7,5},{8,10},{9,11},{10,... | collective-permute-start | bytes 393224 | tf_op jit(solution)/shard_map/ppermute | solution.py:47
  77.9 0.1 add_convert_fusion.2
  78.0 0.9 collective-permute-start.14
  78.9 8.9 %collective-permute-done.23 = f32[128,256]{1,0:T(8,128)S(1)} collective-permute-done((f32[128,256]{1,0:T(8,128)S(1)}, f32[128,256]{1,0:T(8,128)S(1)}, u32[]{:S(2)}, u32[]{:S(2)}) %collective-permute-start.23) | collective-permute-done | bytes 131104 | tf_op jit(solution)/shard_map/ppermute | solution.py:47
  87.9 0.1 collective-permute-start.24
  88.0 0.8 copy.12
  88.8 0.9 spread_own.1
  89.7 2.4 %collective-permute-done.14.in0_ref = bf16[512,256]{1,0:T(8,128)(2,1)S(1)} collective-permute-done((bf16[512,256]{1,0:T(8,128)(2,1)S(1)}, bf16[512,256]{1,0:T(8,128)(2,1)S(1)}, u32[]{:S(2)}, u32[]{:S(2)}) %collective-permute-start.14) | collective-permute-done | bytes 262176 | tf_op jit(solution)/shard_map/ppermute | solution.py:47
  92.1 0.2 final.1
  92.3 0.8 copy.13
  93.1 0.8 select_multiply_fusion
  (39 shorter events, 0.2 us)
Async XLA Ops:
  0.6 30.1 %copy-start.2 = (bf16[1024,256]{1,0:T(8,128)(2,1)S(1)}, bf16[1024,256]{1,0:T(8,128)(2,1)}, u32[]{:S(2)}) copy-start(bf16[1024,256]{1,0:T(8,128)(2,1)} %x_ref.1) | copy-start | bytes 1572868
  1.8 10.2 %collective-permute-start.3 = (bf16[512,256]{1,0:T(8,128)(2,1)S(1)}, bf16[512,256]{1,0:T(8,128)(2,1)S(1)}, u32[]{:S(2)}, u32[]{:S(2)}) collective-permute-start(bf16[512,256]{1,0:T(8,128)(2,1)S(1)} %get-tuple-element.38), channel_id=1, source_target_pairs={{0,2},{1,3},{2,0},{3,1},{4,6},{5,7},{6,4},{7,5},{8,10},{9,11},{10,... | collective-permute-start | bytes 786440 | tf_op jit(solution)/shard_map/ppermute | solution.py:47
  4.8 11.9 %collective-permute-start = (bf16[512,256]{1,0:T(8,128)(2,1)S(1)}, bf16[512,256]{1,0:T(8,128)(2,1)S(1)}, u32[]{:S(2)}, u32[]{:S(2)}) collective-permute-start(bf16[512,256]{1,0:T(8,128)(2,1)S(1)} %get-tuple-element.39), channel_id=1, source_target_pairs={{0,2},{1,3},{2,0},{3,1},{4,6},{5,7},{6,4},{7,5},{8,10},{9,11},{10,... | collective-permute-start | bytes 786440 | tf_op jit(solution)/shard_map/ppermute | solution.py:47
  4.9 25.8 %collective-permute-start.8 = (bf16[1024,256]{1,0:T(8,128)(2,1)}, bf16[1024,256]{1,0:T(8,128)(2,1)S(1)}, u32[]{:S(2)}, u32[]{:S(2)}) collective-permute-start(bf16[1024,256]{1,0:T(8,128)(2,1)} %x_ref.1), channel_id=1, source_target_pairs={{0,1},{1,0},{2,3},{3,2},{4,5},{5,4},{6,7},{7,6},{8,9},{9,8},{10,11... | collective-permute-start | bytes 1572872 | tf_op jit(solution)/shard_map/ppermute | solution.py:43
  11.9 9.1 %collective-permute-start.4 = (bf16[512,256]{1,0:T(8,128)(2,1)S(1)}, bf16[512,256]{1,0:T(8,128)(2,1)S(1)}, u32[]{:S(2)}, u32[]{:S(2)}) collective-permute-start(bf16[512,256]{1,0:T(8,128)(2,1)S(1)} %collective-permute-done.3.refs_1_), channel_id=1, source_target_pairs={{0,4},{1,5},{4,8},{5,9},{8,12},{9,13},{6,2},{7,3},{10,6},{11,7},{1... | collective-permute-start | bytes 786440 | tf_op jit(solution)/shard_map/ppermute | solution.py:53
  16.7 12.7 %collective-permute-start.1 = (bf16[512,256]{1,0:T(8,128)(2,1)S(1)}, bf16[512,256]{1,0:T(8,128)(2,1)S(1)}, u32[]{:S(2)}, u32[]{:S(2)}) collective-permute-start(bf16[512,256]{1,0:T(8,128)(2,1)S(1)} %collective-permute-done.refs_2_), channel_id=1, source_target_pairs={{0,4},{1,5},{4,8},{5,9},{8,12},{9,13},{6,2},{7,3},{10,6},{11,7},{1... | collective-permute-start | bytes 786440 | tf_op jit(solution)/shard_map/ppermute | solution.py:53
  20.4 11.5 %collective-permute-start.6 = (bf16[512,256]{1,0:T(8,128)(2,1)S(1)}, bf16[512,256]{1,0:T(8,128)(2,1)S(1)}, u32[]{:S(2)}, u32[]{:S(2)}) collective-permute-start(bf16[512,256]{1,0:T(8,128)(2,1)S(1)} %collective-permute-done.3.refs_1_), channel_id=1, source_target_pairs={{0,1},{1,0},{2,3},{3,2},{4,5},{5,4},{6,7},{7,6},{8,9},{9,8},{10,11... | collective-permute-start | bytes 786440 | tf_op jit(solution)/shard_map/ppermute | solution.py:43
  20.5 11.5 %collective-permute-start.7 = (bf16[512,256]{1,0:T(8,128)(2,1)S(1)}, bf16[512,256]{1,0:T(8,128)(2,1)S(1)}, u32[]{:S(2)}, u32[]{:S(2)}) collective-permute-start(bf16[512,256]{1,0:T(8,128)(2,1)S(1)} %collective-permute-done.refs_2_), channel_id=1, source_target_pairs={{0,1},{1,0},{2,3},{3,2},{4,5},{5,4},{6,7},{7,6},{8,9},{9,8},{10,11... | collective-permute-start | bytes 786440 | tf_op jit(solution)/shard_map/ppermute | solution.py:43
  21.0 12.2 %collective-permute-start.5 = (bf16[512,256]{1,0:T(8,128)(2,1)S(1)}, bf16[512,256]{1,0:T(8,128)(2,1)S(1)}, u32[]{:S(2)}, u32[]{:S(2)}) collective-permute-start(bf16[512,256]{1,0:T(8,128)(2,1)S(1)} %collective-permute-done.4.refs_1_), channel_id=1, source_target_pairs={{0,1},{1,0},{2,3},{3,2},{4,5},{5,4},{6,7},{7,6},{8,9},{9,8},{10,11... | collective-permute-start | bytes 786440 | tf_op jit(solution)/shard_map/ppermute | solution.py:43
  21.7 2.8 %copy-start.3 = (bf16[192,128,128]{2,1,0:T(8,128)(2,1)S(1)}, bf16[192,128,128]{2,1,0:T(8,128)(2,1)}, u32[]{:S(2)}) copy-start(bf16[192,128,128]{2,1,0:T(8,128)(2,1)} %tiles_ref.1) | copy-start | bytes 18874372
  24.5 0.7 copy-start.7
  25.2 0.7 copy-start.8
  29.4 4.8 %copy-start = (bf16[6,1024,1024]{2,1,0:T(8,128)(2,1)}, bf16[6,1024,1024]{2,1,0:T(8,128)(2,1)S(1)}, u32[]{:S(2)}) copy-start(bf16[6,1024,1024]{2,1,0:T(8,128)(2,1)S(1)} %dense_adjacency.1.refs_0_.a_ref) | copy-start | bytes 37748740
  29.4 4.8 %collective-permute-start.2 = (bf16[512,256]{1,0:T(8,128)(2,1)S(1)}, bf16[512,256]{1,0:T(8,128)(2,1)S(1)}, u32[]{:S(2)}, u32[]{:S(2)}) collective-permute-start(bf16[512,256]{1,0:T(8,128)(2,1)S(1)} %collective-permute-done.1.refs_3_), channel_id=1, source_target_pairs={{0,1},{1,0},{2,3},{3,2},{4,5},{5,4},{6,7},{7,6},{8,9},{9,8},{10,11... | collective-permute-start | bytes 786440 | tf_op jit(solution)/shard_map/ppermute | solution.py:43
  31.9 2.3 %copy-start.4 = (bf16[1024,256]{1,0:T(8,128)(2,1)S(1)}, bf16[1024,256]{1,0:T(8,128)(2,1)}, u32[]{:S(2)}) copy-start(bf16[1024,256]{1,0:T(8,128)(2,1)} %cot_ref.1) | copy-start | bytes 1572868
  31.9 2.3 %copy-start.5 = (bf16[256,256]{1,0:T(8,128)(2,1)S(1)}, bf16[256,256]{1,0:T(8,128)(2,1)}, u32[]{:S(2)}) copy-start(bf16[256,256]{1,0:T(8,128)(2,1)} %r_ref.3) | copy-start | bytes 393220
  32.0 2.3 %copy-start.6 = (bf16[256,256]{1,0:T(8,128)(2,1)S(1)}, bf16[256,256]{1,0:T(8,128)(2,1)}, u32[]{:S(2)}) copy-start(bf16[256,256]{1,0:T(8,128)(2,1)} %w_ref.1) | copy-start | bytes 393220
  38.1 9.0 %collective-permute-start.19 = (f32[256,256]{1,0:T(8,128)}, f32[256,256]{1,0:T(8,128)S(1)}, u32[]{:S(2)}, u32[]{:S(2)}) collective-permute-start(f32[256,256]{1,0:T(8,128)} %get-tuple-element.42), channel_id=1, source_target_pairs={{0,1},{1,0},{2,3},{3,2},{4,5},{5,4},{6,7},{7,6},{8,9},{9,8},{10,11... | collective-permute-start | bytes 786440 | tf_op jit(solution)/shard_map/ppermute | solution.py:43
  38.9 11.3 %collective-permute-start.16 = (bf16[512,256]{1,0:T(8,128)(2,1)S(1)}, bf16[512,256]{1,0:T(8,128)(2,1)S(1)}, u32[]{:S(2)}, u32[]{:S(2)}) collective-permute-start(bf16[512,256]{1,0:T(8,128)(2,1)S(1)} %get-tuple-element.34), channel_id=1, source_target_pairs={{0,1},{1,0},{2,3},{3,2},{4,5},{5,4},{6,7},{7,6},{8,9},{9,8},{10,11... | collective-permute-start | bytes 786440 | tf_op jit(solution)/shard_map/ppermute | solution.py:43
  38.9 4.6 %copy-start.1 = (bf16[6,1024,1024]{2,1,0:T(8,128)(2,1)S(1)}, bf16[6,1024,1024]{2,1,0:T(8,128)(2,1)}, u32[]{:S(2)}) copy-start(bf16[6,1024,1024]{2,1,0:T(8,128)(2,1)} %copy-done) | copy-start | bytes 37748740
  44.3 21.9 %collective-permute-start.15 = (bf16[512,256]{1,0:T(8,128)(2,1)S(1)}, bf16[512,256]{1,0:T(8,128)(2,1)S(1)}, u32[]{:S(2)}, u32[]{:S(2)}) collective-permute-start(bf16[512,256]{1,0:T(8,128)(2,1)S(1)} %get-tuple-element.32), channel_id=1, source_target_pairs={{0,1},{1,0},{2,3},{3,2},{4,5},{5,4},{6,7},{7,6},{8,9},{9,8},{10,11... | collective-permute-start | bytes 786440 | tf_op jit(solution)/shard_map/ppermute | solution.py:43
  44.9 13.8 %collective-permute-start.12 = (bf16[512,256]{1,0:T(8,128)(2,1)S(1)}, bf16[512,256]{1,0:T(8,128)(2,1)S(1)}, u32[]{:S(2)}, u32[]{:S(2)}) collective-permute-start(bf16[512,256]{1,0:T(8,128)(2,1)S(1)} %get-tuple-element.30), channel_id=1, source_target_pairs={{0,1},{1,0},{2,3},{3,2},{4,5},{5,4},{6,7},{7,6},{8,9},{9,8},{10,11... | collective-permute-start | bytes 786440 | tf_op jit(solution)/shard_map/ppermute | solution.py:43
  44.9 15.0 %slice-start = ((s8[12582912]{0:T(1024)(128)(4,1)}), s8[4194304]{0:T(1024)(128)(4,1)S(1)}, s32[]{:S(2)}) async-start(s8[12582912]{0:T(1024)(128)(4,1)} %bitcast.7), calls=%async_computation | async-start | bytes 8388608
  44.9 15.1 %slice-start.1 = ((s8[12582912]{0:T(1024)(128)(4,1)}), s8[4194304]{0:T(1024)(128)(4,1)S(1)}, s32[]{:S(2)}) async-start(s8[12582912]{0:T(1024)(128)(4,1)} %bitcast.7), calls=%async_computation.1 | async-start | bytes 8388608
  44.9 31.7 %collective-permute-start.11 = (bf16[512,256]{1,0:T(8,128)(2,1)S(1)}, bf16[512,256]{1,0:T(8,128)(2,1)S(1)}, u32[]{:S(2)}, u32[]{:S(2)}) collective-permute-start(bf16[512,256]{1,0:T(8,128)(2,1)S(1)} %get-tuple-element.28), channel_id=1, source_target_pairs={{0,1},{1,0},{2,3},{3,2},{4,5},{5,4},{6,7},{7,6},{8,9},{9,8},{10,11... | collective-permute-start | bytes 786440 | tf_op jit(solution)/shard_map/ppermute | solution.py:43
  46.2 13.8 %slice-start.2 = ((s8[12582912]{0:T(1024)(128)(4,1)}), s8[4194304]{0:T(1024)(128)(4,1)S(1)}, s32[]{:S(2)}) async-start(s8[12582912]{0:T(1024)(128)(4,1)} %bitcast.7), calls=%async_computation.2 | async-start | bytes 8388608
  47.1 6.9 %collective-permute-start.20 = (f32[128,256]{1,0:T(8,128)S(1)}, f32[128,256]{1,0:T(8,128)S(1)}, u32[]{:S(2)}, u32[]{:S(2)}) collective-permute-start(f32[128,256]{1,0:T(8,128)S(1)} %slice_select_fusion), channel_id=1, source_target_pairs={{0,2},{1,3},{2,0},{3,1},{4,6},{5,7},{6,4},{7,5},{8,10},{9,11},{10,... | collective-permute-start | bytes 393224 | tf_op jit(solution)/shard_map/ppermute | solution.py:47
  50.3 16.5 %collective-permute-start.17 = (bf16[512,256]{1,0:T(8,128)(2,1)S(1)}, bf16[512,256]{1,0:T(8,128)(2,1)S(1)}, u32[]{:S(2)}, u32[]{:S(2)}) collective-permute-start(bf16[512,256]{1,0:T(8,128)(2,1)S(1)} %add_convert_fusion.1), channel_id=1, source_target_pairs={{4,0},{5,1},{8,4},{9,5},{12,8},{13,9},{2,6},{3,7},{6,10},{7,11},{1... | collective-permute-start | bytes 786440 | tf_op jit(solution)/shard_map/ppermute | solution.py:53
  54.0 12.1 %collective-permute-start.21 = (f32[128,256]{1,0:T(8,128)S(1)}, f32[128,256]{1,0:T(8,128)S(1)}, u32[]{:S(2)}, u32[]{:S(2)}) collective-permute-start(f32[128,256]{1,0:T(8,128)S(1)} %select_add_fusion.1), channel_id=1, source_target_pairs={{0,4},{1,5},{2,6},{3,7},{4,0},{5,1},{6,2},{7,3},{8,12},{9,13},{10,... | collective-permute-start | bytes 393224 | tf_op jit(solution)/shard_map/ppermute | solution.py:197
  58.7 19.3 %collective-permute-start.13 = (bf16[512,256]{1,0:T(8,128)(2,1)S(1)}, bf16[512,256]{1,0:T(8,128)(2,1)S(1)}, u32[]{:S(2)}, u32[]{:S(2)}) collective-permute-start(bf16[512,256]{1,0:T(8,128)(2,1)S(1)} %add_convert_fusion.3), channel_id=1, source_target_pairs={{4,0},{5,1},{8,4},{9,5},{12,8},{13,9},{2,6},{3,7},{6,10},{7,11},{1... | collective-permute-start | bytes 786440 | tf_op jit(solution)/shard_map/ppermute | solution.py:53
  66.2 23.5 %collective-permute-start.10 = (bf16[512,256]{1,0:T(8,128)(2,1)S(1)}, bf16[512,256]{1,0:T(8,128)(2,1)S(1)}, u32[]{:S(2)}, u32[]{:S(2)}) collective-permute-start(bf16[512,256]{1,0:T(8,128)(2,1)S(1)} %get-tuple-element.26), channel_id=1, source_target_pairs={{0,1},{1,0},{2,3},{3,2},{4,5},{5,4},{6,7},{7,6},{8,9},{9,8},{10,11... | collective-permute-start | bytes 786440 | tf_op jit(solution)/shard_map/ppermute | solution.py:43
  66.2 23.5 %collective-permute-start.9 = (bf16[512,256]{1,0:T(8,128)(2,1)S(1)}, bf16[512,256]{1,0:T(8,128)(2,1)S(1)}, u32[]{:S(2)}, u32[]{:S(2)}) collective-permute-start(bf16[512,256]{1,0:T(8,128)(2,1)S(1)} %get-tuple-element.25), channel_id=1, source_target_pairs={{0,1},{1,0},{2,3},{3,2},{4,5},{5,4},{6,7},{7,6},{8,9},{9,8},{10,11... | collective-permute-start | bytes 786440 | tf_op jit(solution)/shard_map/ppermute | solution.py:43
  66.8 9.0 %collective-permute-start.22 = (f32[128,256]{1,0:T(8,128)S(1)}, f32[128,256]{1,0:T(8,128)S(1)}, u32[]{:S(2)}, u32[]{:S(2)}) collective-permute-start(f32[128,256]{1,0:T(8,128)S(1)} %add.38), channel_id=1, source_target_pairs={{0,8},{1,9},{2,10},{3,11},{4,12},{5,13},{6,14},{7,15},{8,0},{9,1},... | collective-permute-start | bytes 393224 | tf_op jit(solution)/shard_map/ppermute | solution.py:197
  75.8 13.9 %collective-permute-start.18 = (bf16[512,256]{1,0:T(8,128)(2,1)S(1)}, bf16[512,256]{1,0:T(8,128)(2,1)S(1)}, u32[]{:S(2)}, u32[]{:S(2)}) collective-permute-start(bf16[512,256]{1,0:T(8,128)(2,1)S(1)} %add_convert_fusion), channel_id=1, source_target_pairs={{0,2},{1,3},{2,0},{3,1},{4,6},{5,7},{6,4},{7,5},{8,10},{9,11},{10,... | collective-permute-start | bytes 786440 | tf_op jit(solution)/shard_map/ppermute | solution.py:47
  76.6 11.2 %collective-permute-start.23 = (f32[128,256]{1,0:T(8,128)S(1)}, f32[128,256]{1,0:T(8,128)S(1)}, u32[]{:S(2)}, u32[]{:S(2)}) collective-permute-start(f32[128,256]{1,0:T(8,128)S(1)} %add.39), channel_id=1, source_target_pairs={{0,2},{1,3},{2,0},{3,1},{4,6},{5,7},{6,4},{7,5},{8,10},{9,11},{10,... | collective-permute-start | bytes 393224 | tf_op jit(solution)/shard_map/ppermute | solution.py:47
  78.0 14.1 %collective-permute-start.14 = (bf16[512,256]{1,0:T(8,128)(2,1)S(1)}, bf16[512,256]{1,0:T(8,128)(2,1)S(1)}, u32[]{:S(2)}, u32[]{:S(2)}) collective-permute-start(bf16[512,256]{1,0:T(8,128)(2,1)S(1)} %add_convert_fusion.2), channel_id=1, source_target_pairs={{0,2},{1,3},{2,0},{3,1},{4,6},{5,7},{6,4},{7,5},{8,10},{9,11},{10,... | collective-permute-start | bytes 786440 | tf_op jit(solution)/shard_map/ppermute | solution.py:47
  87.9 5.2 %collective-permute-start.24 = (f32[256,256]{1,0:T(8,128)S(1)}, f32[256,256]{1,0:T(8,128)S(1)}, u32[]{:S(2)}, u32[]{:S(2)}) collective-permute-start(f32[256,256]{1,0:T(8,128)S(1)} %pad_maximum_fusion), channel_id=1, source_target_pairs={{0,1},{1,0},{2,3},{3,2},{4,5},{5,4},{6,7},{7,6},{8,9},{9,8},{10,11... | collective-permute-start | bytes 786440 | tf_op jit(solution)/shard_map/ppermute | solution.py:43

commit v2 on v1

v2 whole, which is shorter than its diff:
```python
import functools
import math

import jax
import jax.numpy as jnp
from jax import lax
from jax.experimental import pallas as pl
from jax.experimental.pallas import tpu as pltpu
from jax.sharding import PartitionSpec as P

REACH = 2
F32, BF16 = jnp.float32, jnp.bfloat16

OWN, OWN_X, SIDE, SIDE_X, PLANE, PLANE_X = range(6)
PARTS = 6
LIMIT = 4 << 20
CUT = 128
COST = pl.CostEstimate(flops=0, bytes_accessed=0, transcendentals=0)
FORWARD = 8
BACKWARD = 8


def vmem_spec():
    return pl.BlockSpec(memory_space=pltpu.VMEM)


def after(array, *others):
    return lax.optimization_barrier((array, *others))[0]


def smem_spec():
    return pl.BlockSpec(memory_space=pltpu.SMEM)


def hbm_spec():
    return pl.BlockSpec(memory_space=pltpu.HBM)


def in_vmem(array):
    return pltpu.with_memory_space_constraint(array, pltpu.VMEM)


def in_hbm(array):
    return pltpu.with_memory_space_constraint(array, pltpu.HBM)


def kernel_call(kernel, name, outs, args):
    return pl.pallas_call(
        kernel,
        out_shape=[pltpu.VMEM(shape, dtype) for shape, dtype in outs],
        in_specs=[vmem_spec()] * len(args),
        out_specs=[vmem_spec()] * len(outs),
        compiler_params=pltpu.CompilerParams(vmem_limit_bytes=LIMIT),
        cost_estimate=COST,
        name=name,
    )(*[in_vmem(a) for a in args])


def flip_core(array, count):
    return lax.ppermute(array, "row", [(i, i ^ 1) for i in range(count)])


def flip_side(array, count):
    return lax.ppermute(array, "row", [(i, i ^ 2) for i in range(count)])


def over_planes(array, count, back, ends):
    step = [(i, i + 4) for i in range(count) if i % 4 < 2 and i + 4 < count]
    step += [(i, i - 4) for i in range(count) if i % 4 >= 2 and i >= 4]
    if ends:
        step += [(count - 4, count - 2), (count - 3, count - 1), (2, 0), (3, 1)]
    return lax.ppermute(array, "row", [(b, a) for a, b in step] if back else step)


def past_side(array, count, back):
    step = [(i, (i ^ 2) + 4) for i in range(count) if i % 4 >= 2 and i + 4 < count]
    step += [(i, (i ^ 2) - 4) for i in range(count) if i % 4 < 2 and i >= 4]
    return lax.ppermute(array, "row", [(b, a) for a, b in step] if back else step)


def dense_kernel(count_ref, rows_hbm, cols_hbm, tiles_ref, a_ref, rows_ref, cols_ref, sem, index_sems):
    block = tiles_ref.shape[1]
    width = a_ref.shape[1]
    blocks = width // block
    fetches = [
        pltpu.make_async_copy(src, dst, index_sems.at[i])
        for i, (src, dst) in enumerate(((rows_hbm, rows_ref), (cols_hbm, cols_ref)))
    ]
    for fetch in fetches:
        fetch.start()
    stripe = lax.axis_index("row")
    core, side = stripe & 1, (stripe >> 1) & 1
    first = (stripe >> 1) * (2 * blocks)

    def clear(i, carry):
        for part in range(PARTS):
            a_ref[part, pl.ds(pl.multiple_of(i * 64, 64), 64), :] = jnp.zeros((64, width), BF16)
        return carry

    def placed(slot):
        away = cols_ref[slot] - first + 2 * blocks
        chip = away // (2 * blocks)
        within = away - chip * (2 * blocks)
        other = within // blocks
        column = within - other * blocks
        near = jnp.where(side == 0, 2, 0)
        part = jnp.where(chip == 1, OWN, jnp.where(chip == near, SIDE, PLANE)) + (other ^ core)
        target = a_ref.at[
            part,
            pl.ds(pl.multiple_of(rows_ref[slot] * block, block), block),
            pl.ds(pl.multiple_of(column * block, block), block),
        ]
        return pltpu.make_async_copy(tiles_ref.at[slot], target, sem)

    def start(slot, carry):
        placed(slot).start()
        return carry

    def finish(slot, carry):
        placed(slot).wait()
        return carry

    lax.fori_loop(0, width // 64, clear, 0)
    for fetch in fetches:
        fetch.wait()
    live = count_ref[0]
    lax.fori_loop(0, live, start, 0)
    lax.fori_loop(0, live, finish, 0)


def dense_adjacency(tile_rows, tile_cols, tile_count, block_tiles, width):
    slots = tile_rows.shape[0]
    return pl.pallas_call(
        dense_kernel,
        out_shape=pltpu.VMEM((PARTS, width, width), BF16),
        in_specs=[smem_spec()] + [hbm_spec()] * 3,
        out_specs=vmem_spec(),
        scratch_shapes=[
            pltpu.SMEM((slots,), jnp.int32),
            pltpu.SMEM((slots,), jnp.int32),
            pltpu.SemaphoreType.DMA,
            pltpu.SemaphoreType.DMA((2,)),
        ],
        compiler_params=pltpu.CompilerParams(vmem_limit_bytes=LIMIT),
        cost_estimate=COST,
        name="dense_adjacency",
    )(tile_count, *[in_hbm(a) for a in (tile_rows, tile_cols, block_tiles)])


def dot(a, b):
    return jnp.dot(a, b, preferred_element_type=F32)


def dot_nt(a, b):
    return lax.dot_general(a, b, (((1,), (1,)), ((), ())), preferred_element_type=F32)


def dot_tn(a, b):
    return lax.dot_general(a, b, (((0,), (0,)), ((), ())), preferred_element_type=F32)


def gather_kernel(terms, started, *refs):
    a_ref, out_ref = refs[0], refs[-1]
    sources = refs[1:-1]
    total = sources[-1][...] if started else None
    for (part, low), source in zip(terms, sources):
        product = dot(a_ref[part, :, low : low + source.shape[0]], source[...])
        total = product if total is None else total + product
    out_ref[...] = total


def gathered(dense, terms, sources, total, name):
    rows, width = dense.shape[1], sources[0].shape[1]
    args = [dense, *sources] + ([] if total is None else [total])
    return kernel_call(
        functools.partial(gather_kernel, terms, total is not None), name, [((rows, width), F32)], args
    )[0]


def cut_kernel(at, src_ref, out_ref, sems):
    copies = []
    rows = out_ref.shape[0]
    for i, low in enumerate(range(0, rows, CUT)):
        size = min(CUT, rows - low)
        copies.append(
            pltpu.make_async_copy(src_ref.at[pl.ds(at + low, size)], out_ref.at[pl.ds(low, size)], sems.at[i])
        )
    for copy in copies:
        copy.start()
    for copy in copies:
        copy.wait()


def cut(array, at, end):
    return pl.pallas_call(
        functools.partial(cut_kernel, at),
        out_shape=pltpu.VMEM((end - at, array.shape[1]), array.dtype),
        in_specs=[hbm_spec()],
        out_specs=vmem_spec(),
        scratch_shapes=[pltpu.SemaphoreType.DMA((pl.cdiv(end - at, CUT),))],
        compiler_params=pltpu.CompilerParams(vmem_limit_bytes=LIMIT),
        cost_estimate=COST,
        name="cut",
    )(in_hbm(array))


def middle_kernel(terms, end, a_ref, total_ref, x_ref, w_ref, r_ref, cot_ref, *refs):
    last_refs, refs = refs[: len(terms)], refs[len(terms) :]
    out_hbm, grad_ref, ax_ref, ht_ref, px_ref, out_ref, sems = refs
    rows = x_ref.shape[0]
    step = rows // sems.shape[0]
    copies = []
    for i in range(sems.shape[0]):
        here = slice(i * step, (i + 1) * step)
        ax = total_ref[here, :]
        for (part, low, high), last_ref in zip(terms, last_refs):
            ax = ax + dot(a_ref[part, here, low:high], last_ref[...])
        ax = ax.astype(BF16)
        ax_ref[here, :] = ax
        pre = dot(ax, w_ref[...]) + dot(x_ref[here, :], r_ref[...])
        gate = jax.nn.sigmoid(pre)
        out_ref[here, :] = (pre * gate).astype(BF16)
        copies.append(
            pltpu.make_async_copy(
                out_ref.at[pl.ds(i * step, step)], out_hbm.at[pl.ds(i * step, step)], sems.at[i]
            )
        )
        copies[-1].start()
        grad = (cot_ref[here, :].astype(F32) * (gate * (1.0 + pre * (1.0 - gate)))).astype(BF16)
        grad_ref[here, :] = grad
        ht_ref[:, here] = dot_nt(w_ref[...], grad).astype(BF16)
    px_ref[...] = dot(ht_ref[...], a_ref[PLANE_X, :, :end]).T.astype(BF16)
    for copy in copies:
        copy.wait()


def middle(terms, end, *args):
    rows, width = args[2].shape
    wide = pltpu.VMEM((rows, width), BF16)
    return pl.pallas_call(
        functools.partial(middle_kernel, terms, end),
        out_shape=[
            pltpu.HBM((rows, width), BF16), wide, wide, pltpu.VMEM((width, rows), BF16), pltpu.VMEM((end, width), BF16)
        ],
        in_specs=[vmem_spec()] * len(args),
        out_specs=[hbm_spec()] + [vmem_spec()] * 4,
        scratch_shapes=[wide, pltpu.SemaphoreType.DMA((4,))],
        compiler_params=pltpu.CompilerParams(vmem_limit_bytes=LIMIT),
        cost_estimate=COST,
        name="middle",
    )(*[in_vmem(a) for a in args])


def spread_kernel(part, cuts, a_ref, ht_ref, *out_refs):
    for (low, high), out_ref in zip(cuts, out_refs):
        out_ref[...] = dot(ht_ref[...], a_ref[part, :, low:high]).T.astype(out_ref.dtype)


def spread(dense, ht, part, cuts, dtype, name):
    rows, width = dense.shape[1], ht.shape[0]
    return kernel_call(
        functools.partial(spread_kernel, part, cuts),
        name,
        [((high - low, width), dtype) for low, high in cuts],
        [dense, ht],
    )


def spread_two_kernel(low, high, a_ref, ht_ref, px_ref, p_ref):
    for part, out_ref in ((PLANE_X, px_ref), (PLANE, p_ref)):
        out_ref[...] = dot(ht_ref[...], a_ref[part, :, low:high]).T.astype(BF16)


def spread_two(dense, ht, here, name):
    shape = (here[1] - here[0], ht.shape[0])
    return kernel_call(functools.partial(spread_two_kernel, *here), name, [(shape, BF16)] * 2, [dense, ht])


def own_kernel(cuts, a_ref, ht_ref, grad_ref, r_ref, *out_refs):
    for (low, high), out_ref in zip(cuts, out_refs):
        out_ref[...] = dot(ht_ref[...], a_ref[OWN, :, low:high]).T + dot_nt(grad_ref[low:high, :], r_ref[...])


def final_kernel(low, terms, *refs):
    out_ref, chunk_ref, sem = refs[-3:]
    total = refs[0][...]
    for ref in refs[1:terms]:
        total = total + ref[...].astype(F32)
    chunk_ref[...] = total.astype(BF16)
    copy = pltpu.make_async_copy(chunk_ref, out_ref.at[pl.ds(low, chunk_ref.shape[0])], sem)
    copy.start()
    copy.wait()


def final(low, args, rows, result):
    terms = len(args)
    chunk, width = args[0].shape
    return pl.pallas_call(
        functools.partial(final_kernel, low, terms),
        out_shape=pltpu.HBM((rows, width), BF16),
        in_specs=[vmem_spec()] * terms + ([] if result is None else [hbm_spec()]),
        out_specs=hbm_spec(),
        scratch_shapes=[pltpu.VMEM((chunk, width), BF16), pltpu.SemaphoreType.DMA],
        input_output_aliases={} if result is None else {terms: 0},
        compiler_params=pltpu.CompilerParams(vmem_limit_bytes=LIMIT),
        cost_estimate=COST,
        name="final",
    )(*[in_vmem(a) for a in args], *([] if result is None else [in_hbm(result)]))


def relay_kernel(own_ref, other_ref, arrived_ref, out_ref):
    out_ref[...] = (own_ref[...] + other_ref[...].astype(F32) + arrived_ref[...].astype(F32)).astype(BF16)


def relayed(own, other, arrived):
    return kernel_call(relay_kernel, "relay", [(own.shape, BF16)], [own, other, arrived])[0]


def weight_kernel(ax_ref, x_ref, grad_ref, kept_ref, sent_ref):
    core = lax.axis_index("row") & 1
    first = dot_tn(ax_ref[...], grad_ref[...])
    second = dot_tn(x_ref[...], grad_ref[...])
    kept_ref[...] = jnp.where(core == 0, first, second)
    sent_ref[...] = jnp.where(core == 0, second, first)


def scaled_kernel(scale, kept_ref, other_ref, weight_out, root_out, weight_ref, root_ref, sems):
    core = lax.axis_index("row") & 1
    kept, other = kept_ref[...] * scale, other_ref[...] * scale
    weight_ref[...] = jnp.where(core == 0, kept, other)
    root_ref[...] = jnp.where(core == 0, other, kept)
    copies = [
        pltpu.make_async_copy(weight_ref, weight_out, sems.at[0]),
        pltpu.make_async_copy(root_ref, root_out, sems.at[1]),
    ]
    for copy in copies:
        copy.start()
    for copy in copies:
        copy.wait()


def scaled(scale, kept, other):
    shape = kept.shape
    return pl.pallas_call(
        functools.partial(scaled_kernel, scale),
        out_shape=[pltpu.HBM(shape, F32)] * 2,
        in_specs=[vmem_spec()] * 2,
        out_specs=[hbm_spec()] * 2,
        scratch_shapes=[pltpu.VMEM(shape, F32)] * 2 + [pltpu.SemaphoreType.DMA((2,))],
        compiler_params=pltpu.CompilerParams(vmem_limit_bytes=LIMIT),
        cost_estimate=COST,
        name="scaled",
    )(in_vmem(kept), in_vmem(other))


def added(a, b, dtype=BF16):
    return (a.astype(F32) + b.astype(F32)).astype(dtype)


def body(features, weight, root_weight, block_tiles, tile_rows, tile_cols, tile_count, cotangent):
    count = lax.axis_size("row")
    rows, width = features.shape
    split = rows * FORWARD // 16

    side_low = flip_side(cut(features, 0, split), count)
    dense = dense_adjacency(tile_rows, tile_cols, tile_count, block_tiles, rows)
    high = cut(after(features, dense), split, rows)
    side_low, high = lax.optimization_barrier((side_low, high))
    side_high = flip_side(high, count)
    plane_high = past_side(high, count, False)
    plane_low = over_planes(side_low, count, False, True)
    side_x_low = flip_core(side_low, count)
    own_x = flip_core(after(features, side_low), count)
    total = gathered(dense, [(OWN, 0), (OWN_X, 0)], [features, own_x], None, "gather_own")
    total = gathered(dense, [(SIDE, 0), (SIDE_X, 0)], [side_low, side_x_low], total, "gather_side")
    plane_low = after(plane_low, total)
    plane_x_low = flip_core(plane_low, count)
    side_x_high = flip_core(side_high, count)
    plane_x_high = flip_core(plane_high, count)
    total = gathered(dense, [(SIDE, split), (PLANE, split)], [side_high, plane_high], total, "gather_high")
    total = gathered(dense, [(PLANE, 0), (PLANE_X, 0)], [plane_low, plane_x_low], total, "gather_plane")

    split_back = rows * BACKWARD // 16
    back = [(0, split_back), (split_back, rows)]
    layer_out, grad_pre, gathered_x, ht, px_low = middle(
        [(SIDE_X, split, rows), (PLANE_X, split, rows)], split_back,
        dense, total, features, weight, root_weight, cotangent, side_x_high, plane_x_high,
    )

    (p_low,) = spread(dense, ht, PLANE, back[:1], BF16, "spread_plane_low")
    far_low = over_planes(added(p_low, flip_core(px_low, count)), count, True, True)
    px_high, p_high = spread_two(dense, ht, back[1], "spread_plane_high")
    far_high = over_planes(added(p_high, flip_core(px_high, count)), count, True, False)

    square = ((width, width), F32)
    kept, sent = kernel_call(weight_kernel, "weight_products", [square, square], [gathered_x, features, grad_pre])
    kept = kept + flip_core(sent, count)
    mine = kept.astype(BF16)
    kept = added(mine, flip_side(mine, count), F32)

    ht = after(ht, mine)
    sx = [flip_core(share, count) for share in spread(dense, ht, SIDE_X, back, BF16, "spread_side_x")]
    s = spread(dense, ht, SIDE, back, F32, "spread_side")
    ox = [flip_core(share, count) for share in spread(dense, ht, OWN_X, back, BF16, "spread_own_x")]
    own = kernel_call(
        functools.partial(own_kernel, back),
        "spread_own",
        [((high - low, width), F32) for low, high in back],
        [dense, ht, grad_pre, root_weight],
    )
    low = relayed(after(s[0], *own), sx[0], far_low)
    near_low = flip_side(low, count)
    high = relayed(after(s[1], near_low), sx[1], far_high)
    near_high = flip_side(high, count)
    hop, ties = 4, [low, high]
    while hop < count:
        mine = (after(kept, ties.pop(0)) if ties else kept).astype(BF16)
        kept = added(mine, lax.ppermute(mine, "row", [(i, i ^ hop) for i in range(count)]), F32)
        hop *= 2
    grad_features = final(back[0][0], [own[0], ox[0], near_low], rows, None)
    grad_features = final(back[1][0], [own[1], ox[1], near_high], rows, grad_features)
    other = flip_core(kept, count)
    total_weight, total_root = scaled(1.0 / math.sqrt(count * rows), kept, other)

    return layer_out, grad_features, total_weight, total_root


def solution(mesh):
    placed = (
        P(("groups", "row"), None),
        P(),
        P(),
        P(("groups", "row"), None, None),
        P(("groups", "row")),
        P(("groups", "row")),
        P(("groups", "row")),
        P(("groups", "row"), None),
    )
    return jax.shard_map(
        body,
        mesh=mesh,
        in_specs=placed,
        out_specs=(
            P(("groups", "row"), None),
            P(("groups", "row"), None),
            P("groups", None),
            P("groups", None),
        ),
        check_vma=False,
    )
```

time: 93.3 us -> 71.1 us (0.76); the launches traced: 93.9 us -> 70.4 us
  local copies, waits for them, and re-layouts: 11.5 us -> 0.03 us
  starting transfers between devices: 29.8 us -> 18.5 us
  Pallas kernels: 13.6 us -> 19.3 us
  waiting for transfers between devices: 34.7 us -> 30.7 us
  matrix products: 1.4 us -> 0 us
  other arithmetic: 1.3 us -> 0.27 us
    ppermute x4 -> x3, waiting for transfers between devices: 0.01 us -> 12.8 us  [over_planes(): lax.ppermute(array, 'row', [(b, a) for a, b in step] if back else step)]
    ppermute x6 -> x5, waiting for transfers between devices: 21.5 us -> 9.47 us  [flip_side(): return lax.ppermute(array, 'row', [(i, i ^ 2) for i in range(count)])]
    unnamed x26 -> x8, local copies, waits for them, and re-layouts: 10.3 us -> 0.03 us
    pallas_call x0 -> x6, Pallas kernels: none -> 7.58 us  [the longest x1 3.14 us: middle(): pl.pallas_call(functools.partial(middle_kernel, terms, end), out_shape=[p...]
    ppermute x4 -> x3, starting transfers between devices: 10.3 us -> 3.43 us  [over_planes(): lax.ppermute(array, 'row', [(b, a) for a, b in step] if back else step)]
    ppermute x2 -> x3, waiting for transfers between devices: 13.1 us -> 7.85 us  [the longest x2 7.85 us: body(): lax.ppermute(mine, 'row', [(i, i ^ hop) for i in range(count)])]
    ppermute x2 -> x3, starting transfers between devices: 5.81 us -> 1.82 us  [the longest x2 1.15 us: body(): lax.ppermute(mine, 'row', [(i, i ^ hop) for i in range(count)])]
    pallas_call x10 -> x13, Pallas kernels: 10.1 us -> 8.64 us  [kernel_call(): pl.pallas_call(kernel, out_shape=[pltpu.VMEM(shape, dtype) for shape, dty...]
  transfers between devices with their start and end apart: 25 -> 24, of which waited for: 7 -> 9; matrix products, arithmetic and copies ran while one was open for 2% -> 0% of each run, Pallas kernels for 12% -> 19%
where the time goes in v2:
time: 71.1 us; the launch traced here: 70.4 us
  waiting for transfers between devices  30.7 us (43%)
  Pallas kernels  19.3 us (27%)
  starting transfers between devices  18.5 us (26%)
  between operations  1.64 us (2%)
    ppermute x3, waiting for transfers between devices, over_planes(): lax.ppermute(array, 'row', [(b, a) for a, b in step] if back else step)  12.8 us
    ppermute x5, waiting for transfers between devices, flip_side(): return lax.ppermute(array, 'row', [(i, i ^ 2) for i in range(count)])  9.47 us
    ppermute x5, starting transfers between devices, flip_side(): return lax.ppermute(array, 'row', [(i, i ^ 2) for i in range(count)])  9.34 us
    pallas_call x13, Pallas kernels, kernel_call(): pl.pallas_call(kernel, out_shape=[pltpu.VMEM(shape, dtype) for shape, dty...  8.64 us
    ppermute x2, waiting for transfers between devices, body(): lax.ppermute(mine, 'row', [(i, i ^ hop) for i in range(count)])  7.85 us
    ppermute x13, starting transfers between devices, flip_core(): return lax.ppermute(array, 'row', [(i, i ^ 1) for i in range(count)])  3.9 us
    ppermute x3, starting transfers between devices, over_planes(): lax.ppermute(array, 'row', [(b, a) for a, b in step] if back else step)  3.43 us
    pallas_call x1, Pallas kernels, middle(): pl.pallas_call(functools.partial(middle_kernel, terms, end), out_shape=[p...  3.14 us
  transfers between devices with their start and end apart: 24, of which 9 were waited for; matrix products, arithmetic and copies ran while one was open for 0% of the time, Pallas kernels for 19%

profile of v2, /device:TPU:0, one launch (start us, length us, event | category | flops | bytes accessed | tf_op | source)
XLA Modules:
  0.0 70.4 jit_solution(18282967220280650216)
XLA Ops:
  0.6 0.0 copy-start
  0.6 1.0 %cut.2 = bf16[512,256]{1,0:T(8,128)(2,1)S(1)} custom-call(bf16[1024,256]{1,0:T(8,128)(2,1)} %x_ref.3), custom_call_target="tpu_custom_call" | custom-call | tf_op jit(solution)/shard_map/cut/pallas_call | solution.py:195
  1.7 3.0 %collective-permute-start = (bf16[512,256]{1,0:T(8,128)(2,1)S(1)}, bf16[512,256]{1,0:T(8,128)(2,1)S(1)}, u32[]{:S(2)}, u32[]{:S(2)}) collective-permute-start(bf16[512,256]{1,0:T(8,128)(2,1)S(1)} %cut.2), channel_id=1, source_target_pairs={{0,2},{1,3},{2,0},{3,1},{4,6},{5,7},{6,4},{7,5},{8,10},{9,11},{10,... | collective-permute-start | bytes 786440 | tf_op jit(solution)/shard_map/ppermute | solution.py:64
  5.4 3.1 %dense_adjacency.1.refs_0_.a_ref = bf16[6,1024,1024]{2,1,0:T(8,128)(2,1)S(1)} custom-call(s32[1]{0:T(128)S(6)} %copy.14.count_ref, s32[192]{0:T(256)} %rows_hbm.1, s32[192]{0:T(256)} %cols_hbm.1, bf16[192,128,128]{2,1,0:T(8,128)(2,1)} %tiles_ref.1), custom_call_target="tpu_custom_call" | custom-call | tf_op jit(solution)/shard_map/dense_adjacency/pallas_call | solution.py:133
  8.5 1.0 %cut.3 = bf16[512,256]{1,0:T(8,128)(2,1)S(1)} custom-call(bf16[1024,256]{1,0:T(8,128)(2,1)} %x_ref.3), custom_call_target="tpu_custom_call" | custom-call | tf_op jit(solution)/shard_map/cut/pallas_call | solution.py:195
  9.5 1.6 %collective-permute-done.refs_1_ = bf16[512,256]{1,0:T(8,128)(2,1)S(1)} collective-permute-done((bf16[512,256]{1,0:T(8,128)(2,1)S(1)}, bf16[512,256]{1,0:T(8,128)(2,1)S(1)}, u32[]{:S(2)}, u32[]{:S(2)}) %collective-permute-start) | collective-permute-done | bytes 262176 | tf_op jit(solution)/shard_map/ppermute | solution.py:64
  11.0 1.4 %collective-permute-start.3 = (bf16[1024,256]{1,0:T(8,128)(2,1)S(1)}, bf16[1024,256]{1,0:T(8,128)(2,1)S(1)}, u32[]{:S(2)}, u32[]{:S(2)}) collective-permute-start(bf16[1024,256]{1,0:T(8,128)(2,1)S(1)} %copy-done), channel_id=1, source_target_pairs={{0,1},{1,0},{2,3},{3,2},{4,5},{5,4},{6,7},{7,6},{8,9},{9,8},{10,11... | collective-permute-start | bytes 1572872 | tf_op jit(solution)/shard_map/ppermute | solution.py:60
  12.4 0.1 collective-permute-start.2
  12.5 1.8 %collective-permute-start.1 = (bf16[512,256]{1,0:T(8,128)(2,1)S(1)}, bf16[512,256]{1,0:T(8,128)(2,1)S(1)}, u32[]{:S(2)}, u32[]{:S(2)}) collective-permute-start(bf16[512,256]{1,0:T(8,128)(2,1)S(1)} %collective-permute-done.refs_1_), channel_id=1, source_target_pairs={{0,4},{1,5},{4,8},{5,9},{8,12},{9,13},{6,2},{7,3},{10,6},{11,7},{1... | collective-permute-start | bytes 786440 | tf_op jit(solution)/shard_map/ppermute | solution.py:72
  14.3 0.2 collective-permute-start.5
  14.5 0.7 collective-permute-start.6
  15.2 1.3 %gather_own.1.refs_3_ = f32[1024,256]{1,0:T(8,128)S(1)} custom-call(bf16[6,1024,1024]{2,1,0:T(8,128)(2,1)S(1)} %dense_adjacency.1.refs_0_.a_ref, bf16[1024,256]{1,0:T(8,128)(2,1)S(1)} %copy-done, bf16[1024,256]{1,0:T(8,128)(2,1)S(1)} %collective-permute-done.3.refs_2_), custom_call_target="tpu_custom_call" | custom-call | tf_op jit(solution)/shard_map/gather_own/pallas_call | solution.py:48
  16.5 0.0 collective-permute-done.2.refs_2_
  16.5 0.7 %gather_side.1.refs_3_ = f32[1024,256]{1,0:T(8,128)S(1)} custom-call(bf16[6,1024,1024]{2,1,0:T(8,128)(2,1)S(1)} %dense_adjacency.1.refs_0_.a_ref, bf16[512,256]{1,0:T(8,128)(2,1)S(1)} %collective-permute-done.refs_1_, bf16[512,256]{1,0:T(8,128)(2,1)S(1)} %collective-permute-done.2.refs_2_, f32[1024,256]{1,0:T(8,128)S(1)} %gather_own.1.refs_3_), custom_call_target="tpu_custom_call" | custom-call | tf_op jit(solution)/shard_map/gather_side/pallas_call | solution.py:48
  17.2 0.0 copy-start.1
  17.2 0.0 copy-start.2
  17.2 0.0 copy-start.3
  17.2 4.4 %collective-permute-done.1.refs_1_ = bf16[512,256]{1,0:T(8,128)(2,1)S(1)} collective-permute-done((bf16[512,256]{1,0:T(8,128)(2,1)S(1)}, bf16[512,256]{1,0:T(8,128)(2,1)S(1)}, u32[]{:S(2)}, u32[]{:S(2)}) %collective-permute-start.1) | collective-permute-done | bytes 262176 | tf_op jit(solution)/shard_map/ppermute | solution.py:72
  21.6 0.0 collective-permute-start.4
  21.6 5.2 %collective-permute-done.5.refs_1_ = bf16[512,256]{1,0:T(8,128)(2,1)S(1)} collective-permute-done((bf16[512,256]{1,0:T(8,128)(2,1)S(1)}, bf16[512,256]{1,0:T(8,128)(2,1)S(1)}, u32[]{:S(2)}, u32[]{:S(2)}) %collective-permute-start.5) | collective-permute-done | bytes 262176 | tf_op jit(solution)/shard_map/ppermute | solution.py:64
  26.8 0.5 collective-permute-start.8
  27.3 0.7 %gather_high.1.refs_3_ = f32[1024,256]{1,0:T(8,128)S(1)} custom-call(bf16[6,1024,1024]{2,1,0:T(8,128)(2,1)S(1)} %dense_adjacency.1.refs_0_.a_ref, bf16[512,256]{1,0:T(8,128)(2,1)S(1)} %collective-permute-done.5.refs_1_, bf16[512,256]{1,0:T(8,128)(2,1)S(1)} %collective-permute-done.6.refs_2_, f32[1024,256]{1,0:T(8,128)S(1)} %gather_side.1.refs_3_), custom_call_target="tpu_custom_call" | custom-call | tf_op jit(solution)/shard_map/gather_high/pallas_call | solution.py:48
  28.0 0.0 collective-permute-done.4.refs_2_
  28.0 0.7 %gather_plane.1.total_ref = f32[1024,256]{1,0:T(8,128)S(1)} custom-call(bf16[6,1024,1024]{2,1,0:T(8,128)(2,1)S(1)} %dense_adjacency.1.refs_0_.a_ref, bf16[512,256]{1,0:T(8,128)(2,1)S(1)} %collective-permute-done.1.refs_1_, bf16[512,256]{1,0:T(8,128)(2,1)S(1)} %collective-permute-done.4.refs_2_, f32[1024,256]{1,0:T(8,128)S(1)} %gather_high.1.refs_3_), custom_call_target="tpu_custom_call" | custom-call | tf_op jit(solution)/shard_map/gather_plane/pallas_call | solution.py:48
  28.7 0.0 collective-permute-done.8.refs_1_
  28.8 3.1 %middle.1 = (bf16[1024,256]{1,0:T(8,128)(2,1)}, bf16[1024,256]{1,0:T(8,128)(2,1)S(1)}, bf16[1024,256]{1,0:T(8,128)(2,1)S(1)}, bf16[256,1024]{1,0:T(8,128)(2,1)S(1)}, bf16[512,256]{1,0:T(8,128)(2,1)S(1)}) custom-call(bf16[6,1024,1024]{2,1,0:T(8,128)(2,1)S(1)} %dense_adjacency.1.refs_0_.a_ref, f32[1024,256]{1,0:T(8,128)S(1)} %gather_plane.1.total_ref, ...), custom_call_target="tpu_custom_call" | custom-call | tf_op jit(solution)/shard_map/middle/pallas_call | solution.py:240
  31.9 0.5 weight_products.1
  32.4 0.1 collective-permute-start.9
  32.5 0.5 collective-permute-start.12
  33.0 0.5 spread_plane_low.1
  33.5 0.5 collective-permute-done.9
  34.1 1.9 %collective-permute-start.20 = (bf16[256,256]{1,0:T(8,128)(2,1)S(1)}, bf16[256,256]{1,0:T(8,128)(2,1)S(1)}, u32[]{:S(2)}, u32[]{:S(2)}) collective-permute-start(bf16[256,256]{1,0:T(8,128)(2,1)S(1)} %add_convert_fusion.2), channel_id=1, source_target_pairs={{0,2},{1,3},{2,0},{3,1},{4,6},{5,7},{6,4},{7,5},{8,10},{9,11},{10,... | collective-permute-start | bytes 393224 | tf_op jit(solution)/shard_map/ppermute | solution.py:64
  36.0 0.0 collective-permute-done.12
  36.0 0.1 add_convert_fusion.1
  36.0 0.3 collective-permute-start.13
  36.4 0.8 %spread_side_x.1 = (bf16[512,256]{1,0:T(8,128)(2,1)S(1)}, bf16[512,256]{1,0:T(8,128)(2,1)S(1)}) custom-call(bf16[6,1024,1024]{2,1,0:T(8,128)(2,1)S(1)} %dense_adjacency.1.refs_0_.a_ref, bf16[256,1024]{1,0:T(8,128)(2,1)S(1)} %get-tuple-element.44.ht_ref), custom_call_target="tpu_custom_call" | custom-call | tf_op jit(solution)/shard_map/spread_side_x/pallas_call | solution.py:48
  37.1 0.1 collective-permute-start.11
  37.2 0.8 %spread_plane_high.1 = (bf16[512,256]{1,0:T(8,128)(2,1)S(1)}, bf16[512,256]{1,0:T(8,128)(2,1)S(1)}) custom-call(bf16[6,1024,1024]{2,1,0:T(8,128)(2,1)S(1)} %dense_adjacency.1.refs_0_.a_ref, bf16[256,1024]{1,0:T(8,128)(2,1)S(1)} %get-tuple-element.44.ht_ref), custom_call_target="tpu_custom_call" | custom-call | tf_op jit(solution)/shard_map/spread_plane_high/pallas_call | solution.py:48
  38.0 0.6 collective-permute-start.16
  38.6 0.8 %spread_side.1 = (f32[512,256]{1,0:T(8,128)S(1)}, f32[512,256]{1,0:T(8,128)S(1)}) custom-call(bf16[6,1024,1024]{2,1,0:T(8,128)(2,1)S(1)} %dense_adjacency.1.refs_0_.a_ref, bf16[256,1024]{1,0:T(8,128)(2,1)S(1)} %get-tuple-element.44.ht_ref), custom_call_target="tpu_custom_call" | custom-call | tf_op jit(solution)/shard_map/spread_side/pallas_call | solution.py:48
  39.4 0.9 %spread_own.1 = (f32[512,256]{1,0:T(8,128)S(1)}, f32[512,256]{1,0:T(8,128)S(1)}) custom-call(bf16[6,1024,1024]{2,1,0:T(8,128)(2,1)S(1)} %dense_adjacency.1.refs_0_.a_ref, bf16[256,1024]{1,0:T(8,128)(2,1)S(1)} %get-tuple-element.44.ht_ref, bf16[1024,256]{1,0:T(8,128)(2,1)S(1)} %get-tuple-element.41.grad_ref, bf16[256,256]{1,0:T(8,128)(2,1)S(1)} %copy-done.1), custom_call_target="tpu_custom_call" | custom-call | tf_op jit(solution)/shard_map/spread_own/pallas_call | solution.py:48
  40.3 0.0 collective-permute-done.20
  40.4 4.2 %collective-permute-done.13.arrived_ref = bf16[512,256]{1,0:T(8,128)(2,1)S(1)} collective-permute-done((bf16[512,256]{1,0:T(8,128)(2,1)S(1)}, bf16[512,256]{1,0:T(8,128)(2,1)S(1)}, u32[]{:S(2)}, u32[]{:S(2)}) %collective-permute-start.13) | collective-permute-done | bytes 262176 | tf_op jit(solution)/shard_map/ppermute | solution.py:72
  44.6 0.0 collective-permute-done.11.other_ref
  44.6 0.1 relay.2
  44.7 2.5 %collective-permute-start.14 = (bf16[512,256]{1,0:T(8,128)(2,1)S(1)}, bf16[512,256]{1,0:T(8,128)(2,1)S(1)}, u32[]{:S(2)}, u32[]{:S(2)}) collective-permute-start(bf16[512,256]{1,0:T(8,128)(2,1)S(1)} %relay.2), channel_id=1, source_target_pairs={{0,2},{1,3},{2,0},{3,1},{4,6},{5,7},{6,4},{7,5},{8,10},{9,11},{10,... | collective-permute-start | bytes 786440 | tf_op jit(solution)/shard_map/ppermute | solution.py:64
  47.3 0.0 collective-permute-start.21
  47.3 0.1 add_convert_fusion
  47.4 1.3 %collective-permute-start.17 = (bf16[512,256]{1,0:T(8,128)(2,1)S(1)}, bf16[512,256]{1,0:T(8,128)(2,1)S(1)}, u32[]{:S(2)}, u32[]{:S(2)}) collective-permute-start(bf16[512,256]{1,0:T(8,128)(2,1)S(1)} %add_convert_fusion), channel_id=1, source_target_pairs={{4,0},{5,1},{8,4},{9,5},{12,8},{13,9},{2,6},{3,7},{6,10},{7,11},{1... | collective-permute-start | bytes 786440 | tf_op jit(solution)/shard_map/ppermute | solution.py:72
  48.7 0.1 collective-permute-start.15
  48.7 4.9 %collective-permute-done.21 = bf16[256,256]{1,0:T(8,128)(2,1)S(1)} collective-permute-done((bf16[256,256]{1,0:T(8,128)(2,1)S(1)}, bf16[256,256]{1,0:T(8,128)(2,1)S(1)}, u32[]{:S(2)}, u32[]{:S(2)}) %collective-permute-start.21) | collective-permute-done | bytes 131104 | tf_op jit(solution)/shard_map/ppermute | solution.py:418
  53.7 4.2 %collective-permute-done.17.arrived_ref = bf16[512,256]{1,0:T(8,128)(2,1)S(1)} collective-permute-done((bf16[512,256]{1,0:T(8,128)(2,1)S(1)}, bf16[512,256]{1,0:T(8,128)(2,1)S(1)}, u32[]{:S(2)}, u32[]{:S(2)}) %collective-permute-start.17) | collective-permute-done | bytes 262176 | tf_op jit(solution)/shard_map/ppermute | solution.py:72
  57.9 0.1 relay.3
  58.0 1.1 %collective-permute-start.22 = (bf16[256,256]{1,0:T(8,128)(2,1)S(1)}, bf16[256,256]{1,0:T(8,128)(2,1)S(1)}, u32[]{:S(2)}, u32[]{:S(2)}) collective-permute-start(bf16[256,256]{1,0:T(8,128)(2,1)S(1)} %convert_add_fusion.1), channel_id=1, source_target_pairs={{0,8},{1,9},{2,10},{3,11},{4,12},{5,13},{6,14},{7,15},{8,0},{9,1},... | collective-permute-start | bytes 393224 | tf_op jit(solution)/shard_map/ppermute | solution.py:418
  59.1 0.8 %spread_own_x.1 = (bf16[512,256]{1,0:T(8,128)(2,1)S(1)}, bf16[512,256]{1,0:T(8,128)(2,1)S(1)}) custom-call(bf16[6,1024,1024]{2,1,0:T(8,128)(2,1)S(1)} %dense_adjacency.1.refs_0_.a_ref, bf16[256,1024]{1,0:T(8,128)(2,1)S(1)} %get-tuple-element.44.ht_ref), custom_call_target="tpu_custom_call" | custom-call | tf_op jit(solution)/shard_map/spread_own_x/pallas_call | solution.py:48
  59.9 0.1 collective-permute-start.19
  60.0 0.5 collective-permute-start.10
  60.5 1.7 %collective-permute-start.18 = (bf16[512,256]{1,0:T(8,128)(2,1)S(1)}, bf16[512,256]{1,0:T(8,128)(2,1)S(1)}, u32[]{:S(2)}, u32[]{:S(2)}) collective-permute-start(bf16[512,256]{1,0:T(8,128)(2,1)S(1)} %relay.3), channel_id=1, source_target_pairs={{0,2},{1,3},{2,0},{3,1},{4,6},{5,7},{6,4},{7,5},{8,10},{9,11},{10,... | collective-permute-start | bytes 786440 | tf_op jit(solution)/shard_map/ppermute | solution.py:64
  62.1 2.9 %collective-permute-done.22 = bf16[256,256]{1,0:T(8,128)(2,1)S(1)} collective-permute-done((bf16[256,256]{1,0:T(8,128)(2,1)S(1)}, bf16[256,256]{1,0:T(8,128)(2,1)S(1)}, u32[]{:S(2)}, u32[]{:S(2)}) %collective-permute-start.22) | collective-permute-done | bytes 131104 | tf_op jit(solution)/shard_map/ppermute | solution.py:418
  65.1 0.1 collective-permute-start.23
  65.2 0.8 %final.2.refs_3_ = bf16[1024,256]{1,0:T(8,128)(2,1)} custom-call(f32[512,256]{1,0:T(8,128)S(1)} %get-tuple-element.49.refs_0_, bf16[512,256]{1,0:T(8,128)(2,1)S(1)} %collective-permute-done.19.refs_1_, bf16[512,256]{1,0:T(8,128)(2,1)S(1)} %collective-permute-done.14.refs_2_), custom_call_target="tpu_custom_call" | custom-call | tf_op jit(solution)/shard_map/final/pallas_call | solution.py:298
  66.0 2.7 %collective-permute-done.18.refs_2_ = bf16[512,256]{1,0:T(8,128)(2,1)S(1)} collective-permute-done((bf16[512,256]{1,0:T(8,128)(2,1)S(1)}, bf16[512,256]{1,0:T(8,128)(2,1)S(1)}, u32[]{:S(2)}, u32[]{:S(2)}) %collective-permute-start.18) | collective-permute-done | bytes 262176 | tf_op jit(solution)/shard_map/ppermute | solution.py:64
  68.8 0.8 %final.3 = bf16[1024,256]{1,0:T(8,128)(2,1)} custom-call(f32[512,256]{1,0:T(8,128)S(1)} %get-tuple-element.45.refs_0_, bf16[512,256]{1,0:T(8,128)(2,1)S(1)} %collective-permute-done.10.refs_1_, bf16[512,256]{1,0:T(8,128)(2,1)S(1)} %collective-permute-done.18.refs_2_, bf16[1024,256]{1,0:T(8,128)(2,1)} %final.2.refs_3_), custom_call_target="tpu_custom_call", output_to_operand_aliasing={{}: (3, {})} | custom-call | tf_op jit(solution)/shard_map/final/pallas_call | solution.py:298
  69.6 0.9 %scaled.1 = (f32[256,256]{1,0:T(8,128)}, f32[256,256]{1,0:T(8,128)}) custom-call(f32[256,256]{1,0:T(8,128)S(1)} %convert_add_fusion.kept_ref, f32[256,256]{1,0:T(8,128)S(1)} %collective-permute-done.23.other_ref), custom_call_target="tpu_custom_call" | custom-call | tf_op jit(solution)/shard_map/scaled/pallas_call | solution.py:344
  (18 shorter events, 0.2 us)
Async XLA Ops:
  0.6 10.4 %copy-start = (bf16[1024,256]{1,0:T(8,128)(2,1)S(1)}, bf16[1024,256]{1,0:T(8,128)(2,1)}, u32[]{:S(2)}) copy-start(bf16[1024,256]{1,0:T(8,128)(2,1)} %x_ref.3) | copy-start | bytes 1572868
  1.7 9.3 %collective-permute-start = (bf16[512,256]{1,0:T(8,128)(2,1)S(1)}, bf16[512,256]{1,0:T(8,128)(2,1)S(1)}, u32[]{:S(2)}, u32[]{:S(2)}) collective-permute-start(bf16[512,256]{1,0:T(8,128)(2,1)S(1)} %cut.2), channel_id=1, source_target_pairs={{0,2},{1,3},{2,0},{3,1},{4,6},{5,7},{6,4},{7,5},{8,10},{9,11},{10,... | collective-permute-start | bytes 786440 | tf_op jit(solution)/shard_map/ppermute | solution.py:64
  11.0 4.2 %collective-permute-start.3 = (bf16[1024,256]{1,0:T(8,128)(2,1)S(1)}, bf16[1024,256]{1,0:T(8,128)(2,1)S(1)}, u32[]{:S(2)}, u32[]{:S(2)}) collective-permute-start(bf16[1024,256]{1,0:T(8,128)(2,1)S(1)} %copy-done), channel_id=1, source_target_pairs={{0,1},{1,0},{2,3},{3,2},{4,5},{5,4},{6,7},{7,6},{8,9},{9,8},{10,11... | collective-permute-start | bytes 1572872 | tf_op jit(solution)/shard_map/ppermute | solution.py:60
  12.4 4.1 %collective-permute-start.2 = (bf16[512,256]{1,0:T(8,128)(2,1)S(1)}, bf16[512,256]{1,0:T(8,128)(2,1)S(1)}, u32[]{:S(2)}, u32[]{:S(2)}) collective-permute-start(bf16[512,256]{1,0:T(8,128)(2,1)S(1)} %collective-permute-done.refs_1_), channel_id=1, source_target_pairs={{0,1},{1,0},{2,3},{3,2},{4,5},{5,4},{6,7},{7,6},{8,9},{9,8},{10,11... | collective-permute-start | bytes 786440 | tf_op jit(solution)/shard_map/ppermute | solution.py:60
  12.5 9.1 %collective-permute-start.1 = (bf16[512,256]{1,0:T(8,128)(2,1)S(1)}, bf16[512,256]{1,0:T(8,128)(2,1)S(1)}, u32[]{:S(2)}, u32[]{:S(2)}) collective-permute-start(bf16[512,256]{1,0:T(8,128)(2,1)S(1)} %collective-permute-done.refs_1_), channel_id=1, source_target_pairs={{0,4},{1,5},{4,8},{5,9},{8,12},{9,13},{6,2},{7,3},{10,6},{11,7},{1... | collective-permute-start | bytes 786440 | tf_op jit(solution)/shard_map/ppermute | solution.py:72
  14.3 12.5 %collective-permute-start.5 = (bf16[512,256]{1,0:T(8,128)(2,1)S(1)}, bf16[512,256]{1,0:T(8,128)(2,1)S(1)}, u32[]{:S(2)}, u32[]{:S(2)}) collective-permute-start(bf16[512,256]{1,0:T(8,128)(2,1)S(1)} %cut.3), channel_id=1, source_target_pairs={{0,2},{1,3},{2,0},{3,1},{4,6},{5,7},{6,4},{7,5},{8,10},{9,11},{10,... | collective-permute-start | bytes 786440 | tf_op jit(solution)/shard_map/ppermute | solution.py:64
  14.5 12.3 %collective-permute-start.6 = (bf16[512,256]{1,0:T(8,128)(2,1)S(1)}, bf16[512,256]{1,0:T(8,128)(2,1)S(1)}, u32[]{:S(2)}, u32[]{:S(2)}) collective-permute-start(bf16[512,256]{1,0:T(8,128)(2,1)S(1)} %cut.3), channel_id=1, source_target_pairs={{2,4},{3,5},{6,8},{7,9},{10,12},{11,13},{4,2},{5,3},{8,6},{9,7},{1... | collective-permute-start | bytes 786440 | tf_op jit(solution)/shard_map/ppermute | solution.py:78
  17.2 11.6 %copy-start.1 = (bf16[256,256]{1,0:T(8,128)(2,1)S(1)}, bf16[256,256]{1,0:T(8,128)(2,1)}, u32[]{:S(2)}) copy-start(bf16[256,256]{1,0:T(8,128)(2,1)} %r_ref.3) | copy-start | bytes 393220
  17.2 11.6 %copy-start.2 = (bf16[1024,256]{1,0:T(8,128)(2,1)S(1)}, bf16[1024,256]{1,0:T(8,128)(2,1)}, u32[]{:S(2)}) copy-start(bf16[1024,256]{1,0:T(8,128)(2,1)} %cot_ref.1) | copy-start | bytes 1572868
  17.2 11.6 %copy-start.3 = (bf16[256,256]{1,0:T(8,128)(2,1)S(1)}, bf16[256,256]{1,0:T(8,128)(2,1)}, u32[]{:S(2)}) copy-start(bf16[256,256]{1,0:T(8,128)(2,1)} %w_ref.1) | copy-start | bytes 393220
  21.6 6.4 %collective-permute-start.4 = (bf16[512,256]{1,0:T(8,128)(2,1)S(1)}, bf16[512,256]{1,0:T(8,128)(2,1)S(1)}, u32[]{:S(2)}, u32[]{:S(2)}) collective-permute-start(bf16[512,256]{1,0:T(8,128)(2,1)S(1)} %collective-permute-done.1.refs_1_), channel_id=1, source_target_pairs={{0,1},{1,0},{2,3},{3,2},{4,5},{5,4},{6,7},{7,6},{8,9},{9,8},{10,11... | collective-permute-start | bytes 786440 | tf_op jit(solution)/shard_map/ppermute | solution.py:60
  26.8 2.0 %collective-permute-start.7 = (bf16[512,256]{1,0:T(8,128)(2,1)S(1)}, bf16[512,256]{1,0:T(8,128)(2,1)S(1)}, u32[]{:S(2)}, u32[]{:S(2)}) collective-permute-start(bf16[512,256]{1,0:T(8,128)(2,1)S(1)} %collective-permute-done.5.refs_1_), channel_id=1, source_target_pairs={{0,1},{1,0},{2,3},{3,2},{4,5},{5,4},{6,7},{7,6},{8,9},{9,8},{10,11... | collective-permute-start | bytes 786440 | tf_op jit(solution)/shard_map/ppermute | solution.py:60
  26.8 2.0 %collective-permute-start.8 = (bf16[512,256]{1,0:T(8,128)(2,1)S(1)}, bf16[512,256]{1,0:T(8,128)(2,1)S(1)}, u32[]{:S(2)}, u32[]{:S(2)}) collective-permute-start(bf16[512,256]{1,0:T(8,128)(2,1)S(1)} %collective-permute-done.6.refs_2_), channel_id=1, source_target_pairs={{0,1},{1,0},{2,3},{3,2},{4,5},{5,4},{6,7},{7,6},{8,9},{9,8},{10,11... | collective-permute-start | bytes 786440 | tf_op jit(solution)/shard_map/ppermute | solution.py:60
  32.4 1.6 %collective-permute-start.9 = (f32[256,256]{1,0:T(8,128)S(1)}, f32[256,256]{1,0:T(8,128)S(1)}, u32[]{:S(2)}, u32[]{:S(2)}) collective-permute-start(f32[256,256]{1,0:T(8,128)S(1)} %get-tuple-element.43), channel_id=1, source_target_pairs={{0,1},{1,0},{2,3},{3,2},{4,5},{5,4},{6,7},{7,6},{8,9},{9,8},{10,11... | collective-permute-start | bytes 786440 | tf_op jit(solution)/shard_map/ppermute | solution.py:60
  32.5 3.4 %collective-permute-start.12 = (bf16[512,256]{1,0:T(8,128)(2,1)S(1)}, bf16[512,256]{1,0:T(8,128)(2,1)S(1)}, u32[]{:S(2)}, u32[]{:S(2)}) collective-permute-start(bf16[512,256]{1,0:T(8,128)(2,1)S(1)} %get-tuple-element.52), channel_id=1, source_target_pairs={{0,1},{1,0},{2,3},{3,2},{4,5},{5,4},{6,7},{7,6},{8,9},{9,8},{10,11... | collective-permute-start | bytes 786440 | tf_op jit(solution)/shard_map/ppermute | solution.py:60
  34.1 6.3 %collective-permute-start.20 = (bf16[256,256]{1,0:T(8,128)(2,1)S(1)}, bf16[256,256]{1,0:T(8,128)(2,1)S(1)}, u32[]{:S(2)}, u32[]{:S(2)}) collective-permute-start(bf16[256,256]{1,0:T(8,128)(2,1)S(1)} %add_convert_fusion.2), channel_id=1, source_target_pairs={{0,2},{1,3},{2,0},{3,1},{4,6},{5,7},{6,4},{7,5},{8,10},{9,11},{10,... | collective-permute-start | bytes 393224 | tf_op jit(solution)/shard_map/ppermute | solution.py:64
  36.0 8.6 %collective-permute-start.13 = (bf16[512,256]{1,0:T(8,128)(2,1)S(1)}, bf16[512,256]{1,0:T(8,128)(2,1)S(1)}, u32[]{:S(2)}, u32[]{:S(2)}) collective-permute-start(bf16[512,256]{1,0:T(8,128)(2,1)S(1)} %add_convert_fusion.1), channel_id=1, source_target_pairs={{4,0},{5,1},{8,4},{9,5},{12,8},{13,9},{2,6},{3,7},{6,10},{7,11},{1... | collective-permute-start | bytes 786440 | tf_op jit(solution)/shard_map/ppermute | solution.py:72
  37.1 7.5 %collective-permute-start.11 = (bf16[512,256]{1,0:T(8,128)(2,1)S(1)}, bf16[512,256]{1,0:T(8,128)(2,1)S(1)}, u32[]{:S(2)}, u32[]{:S(2)}) collective-permute-start(bf16[512,256]{1,0:T(8,128)(2,1)S(1)} %get-tuple-element.51), channel_id=1, source_target_pairs={{0,1},{1,0},{2,3},{3,2},{4,5},{5,4},{6,7},{7,6},{8,9},{9,8},{10,11... | collective-permute-start | bytes 786440 | tf_op jit(solution)/shard_map/ppermute | solution.py:60
  38.0 9.3 %collective-permute-start.16 = (bf16[512,256]{1,0:T(8,128)(2,1)S(1)}, bf16[512,256]{1,0:T(8,128)(2,1)S(1)}, u32[]{:S(2)}, u32[]{:S(2)}) collective-permute-start(bf16[512,256]{1,0:T(8,128)(2,1)S(1)} %get-tuple-element.56), channel_id=1, source_target_pairs={{0,1},{1,0},{2,3},{3,2},{4,5},{5,4},{6,7},{7,6},{8,9},{9,8},{10,11... | collective-permute-start | bytes 786440 | tf_op jit(solution)/shard_map/ppermute | solution.py:60
  44.7 9.0 %collective-permute-start.14 = (bf16[512,256]{1,0:T(8,128)(2,1)S(1)}, bf16[512,256]{1,0:T(8,128)(2,1)S(1)}, u32[]{:S(2)}, u32[]{:S(2)}) collective-permute-start(bf16[512,256]{1,0:T(8,128)(2,1)S(1)} %relay.2), channel_id=1, source_target_pairs={{0,2},{1,3},{2,0},{3,1},{4,6},{5,7},{6,4},{7,5},{8,10},{9,11},{10,... | collective-permute-start | bytes 786440 | tf_op jit(solution)/shard_map/ppermute | solution.py:64
  47.3 6.4 %collective-permute-start.21 = (bf16[256,256]{1,0:T(8,128)(2,1)S(1)}, bf16[256,256]{1,0:T(8,128)(2,1)S(1)}, u32[]{:S(2)}, u32[]{:S(2)}) collective-permute-start(bf16[256,256]{1,0:T(8,128)(2,1)S(1)} %convert_add_fusion.2), channel_id=1, source_target_pairs={{0,4},{1,5},{2,6},{3,7},{4,0},{5,1},{6,2},{7,3},{8,12},{9,13},{10,... | collective-permute-start | bytes 393224 | tf_op jit(solution)/shard_map/ppermute | solution.py:418
  47.4 10.5 %collective-permute-start.17 = (bf16[512,256]{1,0:T(8,128)(2,1)S(1)}, bf16[512,256]{1,0:T(8,128)(2,1)S(1)}, u32[]{:S(2)}, u32[]{:S(2)}) collective-permute-start(bf16[512,256]{1,0:T(8,128)(2,1)S(1)} %add_convert_fusion), channel_id=1, source_target_pairs={{4,0},{5,1},{8,4},{9,5},{12,8},{13,9},{2,6},{3,7},{6,10},{7,11},{1... | collective-permute-start | bytes 786440 | tf_op jit(solution)/shard_map/ppermute | solution.py:72
  48.7 9.2 %collective-permute-start.15 = (bf16[512,256]{1,0:T(8,128)(2,1)S(1)}, bf16[512,256]{1,0:T(8,128)(2,1)S(1)}, u32[]{:S(2)}, u32[]{:S(2)}) collective-permute-start(bf16[512,256]{1,0:T(8,128)(2,1)S(1)} %get-tuple-element.54), channel_id=1, source_target_pairs={{0,1},{1,0},{2,3},{3,2},{4,5},{5,4},{6,7},{7,6},{8,9},{9,8},{10,11... | collective-permute-start | bytes 786440 | tf_op jit(solution)/shard_map/ppermute | solution.py:60
  58.0 7.1 %collective-permute-start.22 = (bf16[256,256]{1,0:T(8,128)(2,1)S(1)}, bf16[256,256]{1,0:T(8,128)(2,1)S(1)}, u32[]{:S(2)}, u32[]{:S(2)}) collective-permute-start(bf16[256,256]{1,0:T(8,128)(2,1)S(1)} %convert_add_fusion.1), channel_id=1, source_target_pairs={{0,8},{1,9},{2,10},{3,11},{4,12},{5,13},{6,14},{7,15},{8,0},{9,1},... | collective-permute-start | bytes 393224 | tf_op jit(solution)/shard_map/ppermute | solution.py:418
  59.9 5.3 %collective-permute-start.19 = (bf16[512,256]{1,0:T(8,128)(2,1)S(1)}, bf16[512,256]{1,0:T(8,128)(2,1)S(1)}, u32[]{:S(2)}, u32[]{:S(2)}) collective-permute-start(bf16[512,256]{1,0:T(8,128)(2,1)S(1)} %get-tuple-element.57), channel_id=1, source_target_pairs={{0,1},{1,0},{2,3},{3,2},{4,5},{5,4},{6,7},{7,6},{8,9},{9,8},{10,11... | collective-permute-start | bytes 786440 | tf_op jit(solution)/shard_map/ppermute | solution.py:60
  60.0 6.0 %collective-permute-start.10 = (bf16[512,256]{1,0:T(8,128)(2,1)S(1)}, bf16[512,256]{1,0:T(8,128)(2,1)S(1)}, u32[]{:S(2)}, u32[]{:S(2)}) collective-permute-start(bf16[512,256]{1,0:T(8,128)(2,1)S(1)} %get-tuple-element.46), channel_id=1, source_target_pairs={{0,1},{1,0},{2,3},{3,2},{4,5},{5,4},{6,7},{7,6},{8,9},{9,8},{10,11... | collective-permute-start | bytes 786440 | tf_op jit(solution)/shard_map/ppermute | solution.py:60
  60.5 8.3 %collective-permute-start.18 = (bf16[512,256]{1,0:T(8,128)(2,1)S(1)}, bf16[512,256]{1,0:T(8,128)(2,1)S(1)}, u32[]{:S(2)}, u32[]{:S(2)}) collective-permute-start(bf16[512,256]{1,0:T(8,128)(2,1)S(1)} %relay.3), channel_id=1, source_target_pairs={{0,2},{1,3},{2,0},{3,1},{4,6},{5,7},{6,4},{7,5},{8,10},{9,11},{10,... | collective-permute-start | bytes 786440 | tf_op jit(solution)/shard_map/ppermute | solution.py:64
  65.1 4.4 %collective-permute-start.23 = (f32[256,256]{1,0:T(8,128)S(1)}, f32[256,256]{1,0:T(8,128)S(1)}, u32[]{:S(2)}, u32[]{:S(2)}) collective-permute-start(f32[256,256]{1,0:T(8,128)S(1)} %convert_add_fusion.kept_ref), channel_id=1, source_target_pairs={{0,1},{1,0},{2,3},{3,2},{4,5},{5,4},{6,7},{7,6},{8,9},{9,8},{10,11... | collective-permute-start | bytes 786440 | tf_op jit(solution)/shard_map/ppermute | solution.py:60

commit v3 on v2

v3 whole, which is shorter than its diff:
```python
import functools
import math

import jax
import jax.numpy as jnp
from jax import lax
from jax.experimental import pallas as pl
from jax.experimental.pallas import tpu as pltpu
from jax.sharding import PartitionSpec as P

REACH = 2
F32, BF16 = jnp.float32, jnp.bfloat16

OWN, OWN_X, SIDE, SIDE_X, PLANE, PLANE_X = range(6)
PARTS = 6
LIMIT = 4 << 20
CUT = 128
SHORT = pl.CostEstimate(flops=0, bytes_accessed=0, transcendentals=0)
LONG = pl.CostEstimate(flops=10**10, bytes_accessed=0, transcendentals=0)
FORWARD = 10


def vmem_spec():
    return pl.BlockSpec(memory_space=pltpu.VMEM)


def after(array, *others):
    return lax.optimization_barrier((array, *others))[0]


def smem_spec():
    return pl.BlockSpec(memory_space=pltpu.SMEM)


def hbm_spec():
    return pl.BlockSpec(memory_space=pltpu.HBM)


def in_vmem(array):
    return pltpu.with_memory_space_constraint(array, pltpu.VMEM)


def in_hbm(array):
    return pltpu.with_memory_space_constraint(array, pltpu.HBM)


def kernel_call(kernel, name, outs, args, cost=SHORT):
    return pl.pallas_call(
        kernel,
        out_shape=[pltpu.VMEM(shape, dtype) for shape, dtype in outs],
        in_specs=[vmem_spec()] * len(args),
        out_specs=[vmem_spec()] * len(outs),
        compiler_params=pltpu.CompilerParams(vmem_limit_bytes=LIMIT),
        cost_estimate=cost,
        name=name,
    )(*[in_vmem(a) for a in args])


def flip_core(array, count):
    return lax.ppermute(array, "row", [(i, i ^ 1) for i in range(count)])


def flip_side(array, count):
    return lax.ppermute(array, "row", [(i, i ^ 2) for i in range(count)])


def over_planes(array, count, back):
    step = [(i, i + 4) for i in range(count) if i % 4 < 2 and i + 4 < count]
    step += [(i, i - 4) for i in range(count) if i % 4 >= 2 and i >= 4]
    if back:
        step = [(b, a) for a, b in step]
        step += [(0, count - 4), (1, count - 3), (count - 2, 2), (count - 1, 3)]
    else:
        step += [(count - 4, count - 2), (count - 3, count - 1), (2, 0), (3, 1)]
    return lax.ppermute(array, "row", step)


def past_side(array, count, back):
    step = [(i, (i ^ 2) + 4) for i in range(count) if i % 4 >= 2 and i + 4 < count]
    step += [(i, (i ^ 2) - 4) for i in range(count) if i % 4 < 2 and i >= 4]
    return lax.ppermute(array, "row", [(b, a) for a, b in step] if back else step)


def dense_kernel(count_ref, rows_hbm, cols_hbm, tiles_ref, a_ref, rows_ref, cols_ref, sem, index_sems):
    block = tiles_ref.shape[1]
    width = a_ref.shape[1]
    blocks = width // block
    fetches = [
        pltpu.make_async_copy(src, dst, index_sems.at[i])
        for i, (src, dst) in enumerate(((rows_hbm, rows_ref), (cols_hbm, cols_ref)))
    ]
    for fetch in fetches:
        fetch.start()
    stripe = lax.axis_index("row")
    core, side = stripe & 1, (stripe >> 1) & 1
    first = (stripe >> 1) * (2 * blocks)

    def clear(i, carry):
        for part in range(PARTS):
            a_ref[part, pl.ds(pl.multiple_of(i * 64, 64), 64), :] = jnp.zeros((64, width), BF16)
        return carry

    def placed(slot):
        away = cols_ref[slot] - first + 2 * blocks
        chip = away // (2 * blocks)
        within = away - chip * (2 * blocks)
        other = within // blocks
        column = within - other * blocks
        near = jnp.where(side == 0, 2, 0)
        part = jnp.where(chip == 1, OWN, jnp.where(chip == near, SIDE, PLANE)) + (other ^ core)
        target = a_ref.at[
            part,
            pl.ds(pl.multiple_of(rows_ref[slot] * block, block), block),
            pl.ds(pl.multiple_of(column * block, block), block),
        ]
        return pltpu.make_async_copy(tiles_ref.at[slot], target, sem)

    def start(slot, carry):
        placed(slot).start()
        return carry

    def finish(slot, carry):
        placed(slot).wait()
        return carry

    lax.fori_loop(0, width // 64, clear, 0)
    for fetch in fetches:
        fetch.wait()
    live = count_ref[0]
    lax.fori_loop(0, live, start, 0)
    lax.fori_loop(0, live, finish, 0)


def dense_adjacency(tile_rows, tile_cols, tile_count, block_tiles, width):
    slots = tile_rows.shape[0]
    return pl.pallas_call(
        dense_kernel,
        out_shape=pltpu.VMEM((PARTS, width, width), BF16),
        in_specs=[smem_spec()] + [hbm_spec()] * 3,
        out_specs=vmem_spec(),
        scratch_shapes=[
            pltpu.SMEM((slots,), jnp.int32),
            pltpu.SMEM((slots,), jnp.int32),
            pltpu.SemaphoreType.DMA,
            pltpu.SemaphoreType.DMA((2,)),
        ],
        compiler_params=pltpu.CompilerParams(vmem_limit_bytes=LIMIT),
        cost_estimate=SHORT,
        name="dense_adjacency",
    )(tile_count, *[in_hbm(a) for a in (tile_rows, tile_cols, block_tiles)])


def dot(a, b):
    return jnp.dot(a, b, preferred_element_type=F32)


def dot_nt(a, b):
    return lax.dot_general(a, b, (((1,), (1,)), ((), ())), preferred_element_type=F32)


def dot_tn(a, b):
    return lax.dot_general(a, b, (((0,), (0,)), ((), ())), preferred_element_type=F32)


def gather_kernel(terms, started, *refs):
    a_ref, out_ref = refs[0], refs[-1]
    sources = refs[1:-1]
    total = sources[-1][...] if started else None
    for (part, low), source in zip(terms, sources):
        product = dot(a_ref[part, :, low : low + source.shape[0]], source[...])
        total = product if total is None else total + product
    out_ref[...] = total


def gathered(dense, terms, sources, total, name, cost=SHORT):
    rows, width = dense.shape[1], sources[0].shape[1]
    args = [dense, *sources] + ([] if total is None else [total])
    return kernel_call(
        functools.partial(gather_kernel, terms, total is not None), name, [((rows, width), F32)], args, cost
    )[0]


def cut_kernel(at, src_ref, out_ref, sems):
    copies = []
    rows = out_ref.shape[0]
    for i, low in enumerate(range(0, rows, CUT)):
        size = min(CUT, rows - low)
        copies.append(
            pltpu.make_async_copy(src_ref.at[pl.ds(at + low, size)], out_ref.at[pl.ds(low, size)], sems.at[i])
        )
    for copy in copies:
        copy.start()
    for copy in copies:
        copy.wait()


def cut(array, at, end):
    return pl.pallas_call(
        functools.partial(cut_kernel, at),
        out_shape=pltpu.VMEM((end - at, array.shape[1]), array.dtype),
        in_specs=[hbm_spec()],
        out_specs=vmem_spec(),
        scratch_shapes=[pltpu.SemaphoreType.DMA((pl.cdiv(end - at, CUT),))],
        compiler_params=pltpu.CompilerParams(vmem_limit_bytes=LIMIT),
        cost_estimate=SHORT,
        name="cut",
    )(in_hbm(array))


def middle_kernel(terms, a_ref, total_ref, x_ref, w_ref, r_ref, cot_ref, *refs):
    last_refs, refs = refs[: len(terms)], refs[len(terms) :]
    out_hbm, grad_ref, ax_ref, ht_ref, px_ref, out_ref, sems = refs
    rows = x_ref.shape[0]
    step = rows // sems.shape[0]
    copies = []
    for i in range(sems.shape[0]):
        here = slice(i * step, (i + 1) * step)
        ax = total_ref[here, :]
        for (part, low, high), last_ref in zip(terms, last_refs):
            ax = ax + dot(a_ref[part, here, low:high], last_ref[...])
        ax = ax.astype(BF16)
        ax_ref[here, :] = ax
        pre = dot(ax, w_ref[...]) + dot(x_ref[here, :], r_ref[...])
        gate = jax.nn.sigmoid(pre)
        out_ref[here, :] = (pre * gate).astype(BF16)
        copies.append(
            pltpu.make_async_copy(
                out_ref.at[pl.ds(i * step, step)], out_hbm.at[pl.ds(i * step, step)], sems.at[i]
            )
        )
        copies[-1].start()
        grad = (cot_ref[here, :].astype(F32) * (gate * (1.0 + pre * (1.0 - gate)))).astype(BF16)
        grad_ref[here, :] = grad
        ht_ref[:, here] = dot_nt(w_ref[...], grad).astype(BF16)
    px_ref[...] = dot(ht_ref[...], a_ref[PLANE_X, :, :]).T.astype(BF16)
    for copy in copies:
        copy.wait()


def middle(terms, *args):
    rows, width = args[2].shape
    wide = pltpu.VMEM((rows, width), BF16)
    return pl.pallas_call(
        functools.partial(middle_kernel, terms),
        out_shape=[
            pltpu.HBM((rows, width), BF16), wide, wide, pltpu.VMEM((width, rows), BF16), wide
        ],
        in_specs=[vmem_spec()] * len(args),
        out_specs=[hbm_spec()] + [vmem_spec()] * 4,
        scratch_shapes=[wide, pltpu.SemaphoreType.DMA((4,))],
        compiler_params=pltpu.CompilerParams(vmem_limit_bytes=LIMIT),
        cost_estimate=SHORT,
        name="middle",
    )(*[in_vmem(a) for a in args])


def spread_kernel(part, a_ref, ht_ref, out_ref):
    half = out_ref.shape[0] // 2
    for here in (slice(0, half), slice(half, None)):
        out_ref[here, :] = dot(ht_ref[...], a_ref[part, :, here]).T.astype(out_ref.dtype)


def spread(dense, ht, part, dtype, name):
    shape = (dense.shape[1], ht.shape[0])
    return kernel_call(functools.partial(spread_kernel, part), name, [(shape, dtype)], [dense, ht])[0]


def own_kernel(a_ref, ht_ref, grad_ref, r_ref, out_ref):
    half = out_ref.shape[0] // 2
    for here in (slice(0, half), slice(half, None)):
        out_ref[here, :] = dot(ht_ref[...], a_ref[OWN, :, here]).T + dot_nt(grad_ref[here, :], r_ref[...])


def final_kernel(own_ref, other_ref, arrived_ref, out_ref):
    out_ref[...] = (own_ref[...] + other_ref[...].astype(F32) + arrived_ref[...].astype(F32)).astype(BF16)


def scaled_kernel(
    scale, out_ref, kept_ref, other_ref, out_hbm, weight_hbm, root_hbm, weight_ref, root_ref, sems
):
    copies = [pltpu.make_async_copy(out_ref, out_hbm, sems.at[0])]
    copies[0].start()
    core = lax.axis_index("row") & 1
    kept, other = kept_ref[...] * scale, other_ref[...] * scale
    weight_ref[...] = jnp.where(core == 0, kept, other)
    root_ref[...] = jnp.where(core == 0, other, kept)
    copies.append(pltpu.make_async_copy(weight_ref, weight_hbm, sems.at[1]))
    copies.append(pltpu.make_async_copy(root_ref, root_hbm, sems.at[2]))
    for copy in copies[1:]:
        copy.start()
    for copy in copies:
        copy.wait()


def scaled(scale, result, kept, other):
    shape = kept.shape
    return pl.pallas_call(
        functools.partial(scaled_kernel, scale),
        out_shape=[pltpu.HBM(result.shape, BF16), pltpu.HBM(shape, F32), pltpu.HBM(shape, F32)],
        in_specs=[vmem_spec()] * 3,
        out_specs=[hbm_spec()] * 3,
        scratch_shapes=[pltpu.VMEM(shape, F32)] * 2 + [pltpu.SemaphoreType.DMA((3,))],
        compiler_params=pltpu.CompilerParams(vmem_limit_bytes=LIMIT),
        cost_estimate=SHORT,
        name="scaled",
    )(in_vmem(result), in_vmem(kept), in_vmem(other))


def relay_kernel(own_ref, arrived_ref, out_ref):
    out_ref[...] = own_ref[...] + arrived_ref[...].astype(F32)


def relayed(own, arrived):
    return kernel_call(relay_kernel, "relay", [(own.shape, F32)], [own, arrived], LONG)[0]


def weight_kernel(ax_ref, x_ref, grad_ref, kept_ref, sent_ref):
    core = lax.axis_index("row") & 1
    first = dot_tn(ax_ref[...], grad_ref[...])
    second = dot_tn(x_ref[...], grad_ref[...])
    kept_ref[...] = jnp.where(core == 0, first, second)
    sent_ref[...] = jnp.where(core == 0, second, first)


def exchanged(kept, hop, count):
    mine = kept.astype(BF16)
    return added(mine, lax.ppermute(mine, "row", [(i, i ^ hop) for i in range(count)]), F32)


def added(a, b, dtype=BF16):
    return (a.astype(F32) + b.astype(F32)).astype(dtype)


def body(features, weight, root_weight, block_tiles, tile_rows, tile_cols, tile_count, cotangent):
    count = lax.axis_size("row")
    rows, width = features.shape
    split = rows * FORWARD // 16

    side_low = flip_side(cut(features, 0, split), count)
    dense = dense_adjacency(tile_rows, tile_cols, tile_count, block_tiles, rows)
    high = cut(after(features, dense), split, rows)
    side_low, high = lax.optimization_barrier((side_low, high))
    side_high = flip_side(high, count)
    plane_high = past_side(high, count, False)
    plane_low = over_planes(side_low, count, False)
    side_x_low = flip_core(side_low, count)
    own_x = flip_core(after(features, side_low), count)
    total = gathered(dense, [(OWN, 0), (OWN_X, 0)], [features, own_x], None, "gather_own")
    total = gathered(dense, [(SIDE, 0), (SIDE_X, 0)], [side_low, side_x_low], total, "gather_side")
    plane_low = after(plane_low, total)
    plane_x_low = flip_core(plane_low, count)
    side_x_high = flip_core(side_high, count)
    plane_x_high = flip_core(plane_high, count)
    total = gathered(dense, [(SIDE, split), (PLANE, split)], [side_high, plane_high], total, "gather_high")
    total = gathered(dense, [(PLANE, 0), (PLANE_X, 0)], [plane_low, plane_x_low], total, "gather_plane")

    layer_out, grad_pre, gathered_x, ht, px = middle(
        [(SIDE_X, split, rows), (PLANE_X, split, rows)],
        dense, total, features, weight, root_weight, cotangent, side_x_high, plane_x_high,
    )

    share = added(spread(dense, ht, PLANE, BF16, "spread_plane"), flip_core(px, count))
    far = over_planes(share, count, True)

    square = ((width, width), F32)
    kept, sent = kernel_call(weight_kernel, "weight_products", [square, square], [gathered_x, features, grad_pre])
    kept = kept + flip_core(sent, count)
    kept = exchanged(kept, 2, count)

    ht = after(ht, share)
    sx = flip_core(spread(dense, ht, SIDE_X, BF16, "spread_side_x"), count)
    s = spread(dense, ht, SIDE, F32, "spread_side")
    ox = spread(dense, ht, OWN_X, BF16, "spread_own_x")
    own = kernel_call(own_kernel, "spread_own", [((rows, width), F32)], [dense, ht, grad_pre, root_weight])[0]
    through = added(relayed(after(s, own, ox), far), sx)
    near = flip_side(through, count)
    kept = after(kept, through)
    hop = 4
    while hop < count:
        kept = exchanged(kept, hop, count)
        hop *= 2
    result = kernel_call(final_kernel, "final", [((rows, width), BF16)], [own, flip_core(ox, count), near], LONG)[0]
    grad_features, total_weight, total_root = scaled(
        1.0 / math.sqrt(count * rows), result, kept, flip_core(kept, count)
    )
    return layer_out, grad_features, total_weight, total_root


def solution(mesh):
    placed = (
        P(("groups", "row"), None),
        P(),
        P(),
        P(("groups", "row"), None, None),
        P(("groups", "row")),
        P(("groups", "row")),
        P(("groups", "row")),
        P(("groups", "row"), None),
    )
    return jax.shard_map(
        body,
        mesh=mesh,
        in_specs=placed,
        out_specs=(
            P(("groups", "row"), None),
            P(("groups", "row"), None),
            P("groups", None),
            P("groups", None),
        ),
        check_vma=False,
    )
```

time: 71.1 us -> 67.7 us (0.952)
  waiting for transfers between devices: 30.7 us -> 23.6 us
  starting transfers between devices: 18.5 us -> 21.3 us
  Pallas kernels: 19.3 us -> 20.4 us
    ppermute x5, starting transfers between devices: 4.58 us -> 10.7 us  [the longest x2 6.14 us: over_planes(): return lax.ppermute(array, 'row', step)]
    ppermute x5 -> x3, waiting for transfers between devices: 9.47 us -> 5.4 us  [flip_side(): return lax.ppermute(array, 'row', [(i, i ^ 2) for i in range(count)])]
    ppermute x5, waiting for transfers between devices: 20.7 us -> 18 us  [the longest x3 13.8 us: exchanged(): lax.ppermute(mine, 'row', [(i, i ^ hop) for i in range(count)])]
    pallas_call x1, Pallas kernels: 3.11 us -> 5.34 us  [dense_adjacency(): pl.pallas_call(dense_kernel, out_shape=pltpu.VMEM((PARTS, width, width),...]
    ppermute x13 -> x10, starting transfers between devices: 3.9 us -> 1.82 us  [flip_core(): return lax.ppermute(array, 'row', [(i, i ^ 1) for i in range(count)])]
    pallas_call x3 -> x1, Pallas kernels: 4.72 us -> 3.29 us  [middle(): pl.pallas_call(functools.partial(middle_kernel, terms), out_shape=[pltpu....]
    ppermute x5 -> x3, starting transfers between devices: 9.34 us -> 8.15 us  [flip_side(): return lax.ppermute(array, 'row', [(i, i ^ 2) for i in range(count)])]
    pallas_call x13 -> x12, Pallas kernels: 8.64 us -> 8.72 us  [kernel_call(): pl.pallas_call(kernel, out_shape=[pltpu.VMEM(shape, dtype) for shape, dty...]
  transfers between devices with their start and end apart: 24 -> 19, of which waited for: 9 -> 9; matrix products, arithmetic and copies ran while one was open for 0% -> 0% of each run, Pallas kernels for 19% -> 22%
where the time goes in v3:
time: 67.7 us; the launch traced here: 67.2 us
  waiting for transfers between devices  23.6 us (35%)
  starting transfers between devices  21.3 us (31%)
  Pallas kernels  20.4 us (30%)
  between operations  1.58 us (2%)
    ppermute x3, waiting for transfers between devices, exchanged(): lax.ppermute(mine, 'row', [(i, i ^ hop) for i in range(count)])  13.8 us
    pallas_call x12, Pallas kernels, kernel_call(): pl.pallas_call(kernel, out_shape=[pltpu.VMEM(shape, dtype) for shape, dty...  8.72 us
    ppermute x3, starting transfers between devices, flip_side(): return lax.ppermute(array, 'row', [(i, i ^ 2) for i in range(count)])  8.15 us
    ppermute x2, starting transfers between devices, over_planes(): return lax.ppermute(array, 'row', step)  6.14 us
    ppermute x3, waiting for transfers between devices, flip_side(): return lax.ppermute(array, 'row', [(i, i ^ 2) for i in range(count)])  5.4 us
    pallas_call x1, Pallas kernels, dense_adjacency(): pl.pallas_call(dense_kernel, out_shape=pltpu.VMEM((PARTS, width, width),...  5.34 us
    ppermute x3, starting transfers between devices, exchanged(): lax.ppermute(mine, 'row', [(i, i ^ hop) for i in range(count)])  4.57 us
    ppermute x2, waiting for transfers between devices, over_planes(): return lax.ppermute(array, 'row', step)  4.15 us
  transfers between devices with their start and end apart: 19, of which 9 were waited for; matrix products, arithmetic and copies ran while one was open for 0% of the time, Pallas kernels for 22%

profile of v3, /device:TPU:0, one launch (start us, length us, event | category | flops | bytes accessed | tf_op | source)
XLA Modules:
  0.0 67.2 jit_solution(8848463964531610789)
XLA Ops:
  0.6 0.0 copy-start
  0.6 1.1 %cut.2 = bf16[640,256]{1,0:T(8,128)(2,1)S(1)} custom-call(bf16[1024,256]{1,0:T(8,128)(2,1)} %x_ref.3), custom_call_target="tpu_custom_call" | custom-call | tf_op jit(solution)/shard_map/cut/pallas_call | solution.py:198
  1.7 3.0 %collective-permute-start = (bf16[640,256]{1,0:T(8,128)(2,1)S(1)}, bf16[640,256]{1,0:T(8,128)(2,1)S(1)}, u32[]{:S(2)}, u32[]{:S(2)}) collective-permute-start(bf16[640,256]{1,0:T(8,128)(2,1)S(1)} %cut.2), channel_id=1, source_target_pairs={{0,2},{1,3},{2,0},{3,1},{4,6},{5,7},{6,4},{7,5},{8,10},{9,11},{10,... | collective-permute-start | bytes 983048 | tf_op jit(solution)/shard_map/ppermute | solution.py:64
  5.4 5.3 %dense_adjacency.1.refs_0_.a_ref = bf16[6,1024,1024]{2,1,0:T(8,128)(2,1)S(1)} custom-call(s32[1]{0:T(128)S(6)} %copy.12.count_ref, s32[192]{0:T(256)} %rows_hbm.1, s32[192]{0:T(256)} %cols_hbm.1, bf16[192,128,128]{2,1,0:T(8,128)(2,1)} %tiles_ref.1), custom_call_target="tpu_custom_call" | custom-call | tf_op jit(solution)/shard_map/dense_adjacency/pallas_call | solution.py:136
  10.8 0.9 %cut.3 = bf16[384,256]{1,0:T(8,128)(2,1)S(1)} custom-call(bf16[1024,256]{1,0:T(8,128)(2,1)} %x_ref.3), custom_call_target="tpu_custom_call" | custom-call | tf_op jit(solution)/shard_map/cut/pallas_call | solution.py:198
  11.7 0.8 %collective-permute-done.refs_1_ = bf16[640,256]{1,0:T(8,128)(2,1)S(1)} collective-permute-done((bf16[640,256]{1,0:T(8,128)(2,1)S(1)}, bf16[640,256]{1,0:T(8,128)(2,1)S(1)}, u32[]{:S(2)}, u32[]{:S(2)}) %collective-permute-start) | collective-permute-done | bytes 327712 | tf_op jit(solution)/shard_map/ppermute | solution.py:64
  12.5 0.0 copy-done
  12.5 0.0 collective-permute-start.3
  12.5 0.5 collective-permute-start.2
  13.0 1.8 %collective-permute-start.1 = (bf16[640,256]{1,0:T(8,128)(2,1)S(1)}, bf16[640,256]{1,0:T(8,128)(2,1)S(1)}, u32[]{:S(2)}, u32[]{:S(2)}) collective-permute-start(bf16[640,256]{1,0:T(8,128)(2,1)S(1)} %collective-permute-done.refs_1_), channel_id=1, source_target_pairs={{0,4},{1,5},{4,8},{5,9},{8,12},{9,13},{6,2},{7,3},{10,6},{11,7},{1... | collective-permute-start | bytes 983048 | tf_op jit(solution)/shard_map/ppermute | solution.py:75
  14.8 0.7 collective-permute-start.6
  15.4 4.3 %collective-permute-start.5 = (bf16[384,256]{1,0:T(8,128)(2,1)S(1)}, bf16[384,256]{1,0:T(8,128)(2,1)S(1)}, u32[]{:S(2)}, u32[]{:S(2)}) collective-permute-start(bf16[384,256]{1,0:T(8,128)(2,1)S(1)} %cut.3), channel_id=1, source_target_pairs={{0,2},{1,3},{2,0},{3,1},{4,6},{5,7},{6,4},{7,5},{8,10},{9,11},{10,... | collective-permute-start | bytes 589832 | tf_op jit(solution)/shard_map/ppermute | solution.py:64
  19.8 0.0 collective-permute-done.3.refs_2_
  19.8 1.3 %gather_own.1.refs_3_ = f32[1024,256]{1,0:T(8,128)S(1)} custom-call(bf16[6,1024,1024]{2,1,0:T(8,128)(2,1)S(1)} %dense_adjacency.1.refs_0_.a_ref, bf16[1024,256]{1,0:T(8,128)(2,1)S(1)} %copy-done, bf16[1024,256]{1,0:T(8,128)(2,1)S(1)} %collective-permute-done.3.refs_2_), custom_call_target="tpu_custom_call" | custom-call | tf_op jit(solution)/shard_map/gather_own/pallas_call | solution.py:48
  21.0 0.0 collective-permute-done.2.refs_2_
  21.1 1.0 %gather_side.1.refs_3_ = f32[1024,256]{1,0:T(8,128)S(1)} custom-call(bf16[6,1024,1024]{2,1,0:T(8,128)(2,1)S(1)} %dense_adjacency.1.refs_0_.a_ref, bf16[640,256]{1,0:T(8,128)(2,1)S(1)} %collective-permute-done.refs_1_, bf16[640,256]{1,0:T(8,128)(2,1)S(1)} %collective-permute-done.2.refs_2_, f32[1024,256]{1,0:T(8,128)S(1)} %gather_own.1.refs_3_), custom_call_target="tpu_custom_call" | custom-call | tf_op jit(solution)/shard_map/gather_side/pallas_call | solution.py:48
  22.0 0.0 copy-start.1
  22.0 0.0 copy-start.2
  22.1 0.0 copy-start.3
  22.1 1.5 %collective-permute-done.1.refs_1_ = bf16[640,256]{1,0:T(8,128)(2,1)S(1)} collective-permute-done((bf16[640,256]{1,0:T(8,128)(2,1)S(1)}, bf16[640,256]{1,0:T(8,128)(2,1)S(1)}, u32[]{:S(2)}, u32[]{:S(2)}) %collective-permute-start.1) | collective-permute-done | bytes 327712 | tf_op jit(solution)/shard_map/ppermute | solution.py:75
  23.6 0.0 collective-permute-start.4
  23.6 0.0 collective-permute-done.6.refs_2_
  23.6 0.5 collective-permute-start.8
  24.1 2.7 %collective-permute-done.5.refs_1_ = bf16[384,256]{1,0:T(8,128)(2,1)S(1)} collective-permute-done((bf16[384,256]{1,0:T(8,128)(2,1)S(1)}, bf16[384,256]{1,0:T(8,128)(2,1)S(1)}, u32[]{:S(2)}, u32[]{:S(2)}) %collective-permute-start.5) | collective-permute-done | bytes 196640 | tf_op jit(solution)/shard_map/ppermute | solution.py:64
  26.8 0.0 collective-permute-start.7
  26.8 0.7 %gather_high.1.refs_3_ = f32[1024,256]{1,0:T(8,128)S(1)} custom-call(bf16[6,1024,1024]{2,1,0:T(8,128)(2,1)S(1)} %dense_adjacency.1.refs_0_.a_ref, bf16[384,256]{1,0:T(8,128)(2,1)S(1)} %collective-permute-done.5.refs_1_, bf16[384,256]{1,0:T(8,128)(2,1)S(1)} %collective-permute-done.6.refs_2_, f32[1024,256]{1,0:T(8,128)S(1)} %gather_side.1.refs_3_), custom_call_target="tpu_custom_call" | custom-call | tf_op jit(solution)/shard_map/gather_high/pallas_call | solution.py:48
  27.5 0.0 collective-permute-done.4.refs_2_
  27.5 1.0 %gather_plane.1.total_ref = f32[1024,256]{1,0:T(8,128)S(1)} custom-call(bf16[6,1024,1024]{2,1,0:T(8,128)(2,1)S(1)} %dense_adjacency.1.refs_0_.a_ref, bf16[640,256]{1,0:T(8,128)(2,1)S(1)} %collective-permute-done.1.refs_1_, bf16[640,256]{1,0:T(8,128)(2,1)S(1)} %collective-permute-done.4.refs_2_, f32[1024,256]{1,0:T(8,128)S(1)} %gather_high.1.refs_3_), custom_call_target="tpu_custom_call" | custom-call | tf_op jit(solution)/shard_map/gather_plane/pallas_call | solution.py:48
  28.5 0.0 collective-permute-done.8.refs_1_
  28.5 0.0 collective-permute-done.7.refs_0_
  28.5 0.0 copy-done.1
  28.5 0.0 copy-done.2
  28.5 3.3 %middle.1 = (bf16[1024,256]{1,0:T(8,128)(2,1)}, bf16[1024,256]{1,0:T(8,128)(2,1)S(1)}, bf16[1024,256]{1,0:T(8,128)(2,1)S(1)}, bf16[256,1024]{1,0:T(8,128)(2,1)S(1)}, bf16[1024,256]{1,0:T(8,128)(2,1)S(1)}) custom-call(bf16[6,1024,1024]{2,1,0:T(8,128)(2,1)S(1)} %dense_adjacency.1.refs_0_.a_ref, f32[1024,256]{1,0:T(8,128)S(1)} %gather_plane.1.total_ref, ...), custom_call_target="tpu_custom_call" | custom-call | tf_op jit(solution)/shard_map/middle/pallas_call | solution.py:243
  31.8 0.6 collective-permute-start.9
  32.4 0.8 %spread_plane.1 = bf16[1024,256]{1,0:T(8,128)(2,1)S(1)} custom-call(bf16[6,1024,1024]{2,1,0:T(8,128)(2,1)S(1)} %dense_adjacency.1.refs_0_.a_ref, bf16[256,1024]{1,0:T(8,128)(2,1)S(1)} %get-tuple-element.30.ht_ref), custom_call_target="tpu_custom_call" | custom-call | tf_op jit(solution)/shard_map/spread_plane/pallas_call | solution.py:48
  33.2 0.5 weight_products.1
  33.7 0.1 collective-permute-start.14
  33.8 0.2 collective-permute-done.9
  34.0 0.1 add_convert_fusion.1
  34.1 4.3 %collective-permute-start.11 = (bf16[1024,256]{1,0:T(8,128)(2,1)S(1)}, bf16[1024,256]{1,0:T(8,128)(2,1)S(1)}, u32[]{:S(2)}, u32[]{:S(2)}) collective-permute-start(bf16[1024,256]{1,0:T(8,128)(2,1)S(1)} %add_convert_fusion.1), channel_id=1, source_target_pairs={{4,0},{5,1},{8,4},{9,5},{12,8},{13,9},{2,6},{3,7},{6,10},{7,11},{1... | collective-permute-start | bytes 1572872 | tf_op jit(solution)/shard_map/ppermute | solution.py:75
  38.4 0.0 collective-permute-done.14
  38.5 0.1 collective-permute-start.15
  38.6 5.5 %collective-permute-done.15 = bf16[256,256]{1,0:T(8,128)(2,1)S(1)} collective-permute-done((bf16[256,256]{1,0:T(8,128)(2,1)S(1)}, bf16[256,256]{1,0:T(8,128)(2,1)S(1)}, u32[]{:S(2)}, u32[]{:S(2)}) %collective-permute-start.15) | collective-permute-done | bytes 131104 | tf_op jit(solution)/shard_map/ppermute | solution.py:327
  44.1 0.8 %spread_own_x.1 = bf16[1024,256]{1,0:T(8,128)(2,1)S(1)} custom-call(bf16[6,1024,1024]{2,1,0:T(8,128)(2,1)S(1)} %dense_adjacency.1.refs_0_.a_ref, bf16[256,1024]{1,0:T(8,128)(2,1)S(1)} %get-tuple-element.30.ht_ref), custom_call_target="tpu_custom_call" | custom-call | tf_op jit(solution)/shard_map/spread_own_x/pallas_call | solution.py:48
  44.8 0.9 %spread_own.1.own_ref = f32[1024,256]{1,0:T(8,128)S(1)} custom-call(bf16[6,1024,1024]{2,1,0:T(8,128)(2,1)S(1)} %dense_adjacency.1.refs_0_.a_ref, bf16[256,1024]{1,0:T(8,128)(2,1)S(1)} %get-tuple-element.30.ht_ref, bf16[1024,256]{1,0:T(8,128)(2,1)S(1)} %get-tuple-element.31.grad_ref, bf16[256,256]{1,0:T(8,128)(2,1)S(1)} %copy-done.1), custom_call_target="tpu_custom_call" | custom-call | tf_op jit(solution)/shard_map/spread_own/pallas_call | solution.py:48
  45.8 0.8 %spread_side_x.1 = bf16[1024,256]{1,0:T(8,128)(2,1)S(1)} custom-call(bf16[6,1024,1024]{2,1,0:T(8,128)(2,1)S(1)} %dense_adjacency.1.refs_0_.a_ref, bf16[256,1024]{1,0:T(8,128)(2,1)S(1)} %get-tuple-element.30.ht_ref), custom_call_target="tpu_custom_call" | custom-call | tf_op jit(solution)/shard_map/spread_side_x/pallas_call | solution.py:48
  46.6 0.8 %spread_side.1.own_ref = f32[1024,256]{1,0:T(8,128)S(1)} custom-call(bf16[6,1024,1024]{2,1,0:T(8,128)(2,1)S(1)} %dense_adjacency.1.refs_0_.a_ref, bf16[256,1024]{1,0:T(8,128)(2,1)S(1)} %get-tuple-element.30.ht_ref), custom_call_target="tpu_custom_call" | custom-call | tf_op jit(solution)/shard_map/spread_side/pallas_call | solution.py:48
  47.4 0.1 collective-permute-start.12
  47.5 2.7 %collective-permute-done.11.arrived_ref = bf16[1024,256]{1,0:T(8,128)(2,1)S(1)} collective-permute-done((bf16[1024,256]{1,0:T(8,128)(2,1)S(1)}, bf16[1024,256]{1,0:T(8,128)(2,1)S(1)}, u32[]{:S(2)}, u32[]{:S(2)}) %collective-permute-start.11) | collective-permute-done | bytes 524320 | tf_op jit(solution)/shard_map/ppermute | solution.py:75
  50.1 0.1 relay.1
  50.2 0.0 collective-permute-done.12
  50.2 0.1 add_convert_fusion
  50.4 1.3 %collective-permute-start.16 = (bf16[256,256]{1,0:T(8,128)(2,1)S(1)}, bf16[256,256]{1,0:T(8,128)(2,1)S(1)}, u32[]{:S(2)}, u32[]{:S(2)}) collective-permute-start(bf16[256,256]{1,0:T(8,128)(2,1)S(1)} %convert_add_fusion.1), channel_id=1, source_target_pairs={{0,4},{1,5},{2,6},{3,7},{4,0},{5,1},{6,2},{7,3},{8,12},{9,13},{10,... | collective-permute-start | bytes 393224 | tf_op jit(solution)/shard_map/ppermute | solution.py:327
  51.7 0.0 collective-permute-start.10
  51.7 0.8 %collective-permute-start.13 = (bf16[1024,256]{1,0:T(8,128)(2,1)S(1)}, bf16[1024,256]{1,0:T(8,128)(2,1)S(1)}, u32[]{:S(2)}, u32[]{:S(2)}) collective-permute-start(bf16[1024,256]{1,0:T(8,128)(2,1)S(1)} %add_convert_fusion), channel_id=1, source_target_pairs={{0,2},{1,3},{2,0},{3,1},{4,6},{5,7},{6,4},{7,5},{8,10},{9,11},{10,... | collective-permute-start | bytes 1572872 | tf_op jit(solution)/shard_map/ppermute | solution.py:64
  52.5 2.9 %collective-permute-done.16 = bf16[256,256]{1,0:T(8,128)(2,1)S(1)} collective-permute-done((bf16[256,256]{1,0:T(8,128)(2,1)S(1)}, bf16[256,256]{1,0:T(8,128)(2,1)S(1)}, u32[]{:S(2)}, u32[]{:S(2)}) %collective-permute-start.16) | collective-permute-done | bytes 131104 | tf_op jit(solution)/shard_map/ppermute | solution.py:327
  55.4 3.2 %collective-permute-start.17 = (bf16[256,256]{1,0:T(8,128)(2,1)S(1)}, bf16[256,256]{1,0:T(8,128)(2,1)S(1)}, u32[]{:S(2)}, u32[]{:S(2)}) collective-permute-start(bf16[256,256]{1,0:T(8,128)(2,1)S(1)} %add_convert_fusion.2), channel_id=1, source_target_pairs={{0,8},{1,9},{2,10},{3,11},{4,12},{5,13},{6,14},{7,15},{8,0},{9,1},... | collective-permute-start | bytes 393224 | tf_op jit(solution)/shard_map/ppermute | solution.py:327
  58.6 5.4 %collective-permute-done.17 = bf16[256,256]{1,0:T(8,128)(2,1)S(1)} collective-permute-done((bf16[256,256]{1,0:T(8,128)(2,1)S(1)}, bf16[256,256]{1,0:T(8,128)(2,1)S(1)}, u32[]{:S(2)}, u32[]{:S(2)}) %collective-permute-start.17) | collective-permute-done | bytes 131104 | tf_op jit(solution)/shard_map/ppermute | solution.py:327
  64.1 0.1 collective-permute-start.18
  64.1 0.0 collective-permute-done.10.other_ref
  64.1 1.9 %collective-permute-done.13.arrived_ref = bf16[1024,256]{1,0:T(8,128)(2,1)S(1)} collective-permute-done((bf16[1024,256]{1,0:T(8,128)(2,1)S(1)}, bf16[1024,256]{1,0:T(8,128)(2,1)S(1)}, u32[]{:S(2)}, u32[]{:S(2)}) %collective-permute-start.13) | collective-permute-done | bytes 524320 | tf_op jit(solution)/shard_map/ppermute | solution.py:64
  66.0 0.2 final.1.out_ref
  66.2 0.0 collective-permute-done.18.other_ref
  66.2 1.0 %scaled.1 = (bf16[1024,256]{1,0:T(8,128)(2,1)}, f32[256,256]{1,0:T(8,128)}, f32[256,256]{1,0:T(8,128)}) custom-call(bf16[1024,256]{1,0:T(8,128)(2,1)S(1)} %final.1.out_ref, f32[256,256]{1,0:T(8,128)S(1)} %convert_add_fusion.kept_ref, f32[256,256]{1,0:T(8,128)S(1)} %collective-permute-done.18.other_ref), custom_call_target="tpu_custom_call" | custom-call | tf_op jit(solution)/shard_map/scaled/pallas_call | solution.py:297
  (5 shorter events, 0.1 us)
Async XLA Ops:
  0.6 11.8 %copy-start = (bf16[1024,256]{1,0:T(8,128)(2,1)S(1)}, bf16[1024,256]{1,0:T(8,128)(2,1)}, u32[]{:S(2)}) copy-start(bf16[1024,256]{1,0:T(8,128)(2,1)} %x_ref.3) | copy-start | bytes 1572868
  1.7 10.7 %collective-permute-start = (bf16[640,256]{1,0:T(8,128)(2,1)S(1)}, bf16[640,256]{1,0:T(8,128)(2,1)S(1)}, u32[]{:S(2)}, u32[]{:S(2)}) collective-permute-start(bf16[640,256]{1,0:T(8,128)(2,1)S(1)} %cut.2), channel_id=1, source_target_pairs={{0,2},{1,3},{2,0},{3,1},{4,6},{5,7},{6,4},{7,5},{8,10},{9,11},{10,... | collective-permute-start | bytes 983048 | tf_op jit(solution)/shard_map/ppermute | solution.py:64
  12.5 7.3 %collective-permute-start.3 = (bf16[1024,256]{1,0:T(8,128)(2,1)S(1)}, bf16[1024,256]{1,0:T(8,128)(2,1)S(1)}, u32[]{:S(2)}, u32[]{:S(2)}) collective-permute-start(bf16[1024,256]{1,0:T(8,128)(2,1)S(1)} %copy-done), channel_id=1, source_target_pairs={{0,1},{1,0},{2,3},{3,2},{4,5},{5,4},{6,7},{7,6},{8,9},{9,8},{10,11... | collective-permute-start | bytes 1572872 | tf_op jit(solution)/shard_map/ppermute | solution.py:60
  12.5 8.6 %collective-permute-start.2 = (bf16[640,256]{1,0:T(8,128)(2,1)S(1)}, bf16[640,256]{1,0:T(8,128)(2,1)S(1)}, u32[]{:S(2)}, u32[]{:S(2)}) collective-permute-start(bf16[640,256]{1,0:T(8,128)(2,1)S(1)} %collective-permute-done.refs_1_), channel_id=1, source_target_pairs={{0,1},{1,0},{2,3},{3,2},{4,5},{5,4},{6,7},{7,6},{8,9},{9,8},{10,11... | collective-permute-start | bytes 983048 | tf_op jit(solution)/shard_map/ppermute | solution.py:60
  13.0 10.6 %collective-permute-start.1 = (bf16[640,256]{1,0:T(8,128)(2,1)S(1)}, bf16[640,256]{1,0:T(8,128)(2,1)S(1)}, u32[]{:S(2)}, u32[]{:S(2)}) collective-permute-start(bf16[640,256]{1,0:T(8,128)(2,1)S(1)} %collective-permute-done.refs_1_), channel_id=1, source_target_pairs={{0,4},{1,5},{4,8},{5,9},{8,12},{9,13},{6,2},{7,3},{10,6},{11,7},{1... | collective-permute-start | bytes 983048 | tf_op jit(solution)/shard_map/ppermute | solution.py:75
  14.8 8.8 %collective-permute-start.6 = (bf16[384,256]{1,0:T(8,128)(2,1)S(1)}, bf16[384,256]{1,0:T(8,128)(2,1)S(1)}, u32[]{:S(2)}, u32[]{:S(2)}) collective-permute-start(bf16[384,256]{1,0:T(8,128)(2,1)S(1)} %cut.3), channel_id=1, source_target_pairs={{2,4},{3,5},{6,8},{7,9},{10,12},{11,13},{4,2},{5,3},{8,6},{9,7},{1... | collective-permute-start | bytes 589832 | tf_op jit(solution)/shard_map/ppermute | solution.py:81
  15.4 11.4 %collective-permute-start.5 = (bf16[384,256]{1,0:T(8,128)(2,1)S(1)}, bf16[384,256]{1,0:T(8,128)(2,1)S(1)}, u32[]{:S(2)}, u32[]{:S(2)}) collective-permute-start(bf16[384,256]{1,0:T(8,128)(2,1)S(1)} %cut.3), channel_id=1, source_target_pairs={{0,2},{1,3},{2,0},{3,1},{4,6},{5,7},{6,4},{7,5},{8,10},{9,11},{10,... | collective-permute-start | bytes 589832 | tf_op jit(solution)/shard_map/ppermute | solution.py:64
  22.0 6.5 %copy-start.1 = (bf16[256,256]{1,0:T(8,128)(2,1)S(1)}, bf16[256,256]{1,0:T(8,128)(2,1)}, u32[]{:S(2)}) copy-start(bf16[256,256]{1,0:T(8,128)(2,1)} %r_ref.3) | copy-start | bytes 393220
  22.0 6.5 %copy-start.2 = (bf16[1024,256]{1,0:T(8,128)(2,1)S(1)}, bf16[1024,256]{1,0:T(8,128)(2,1)}, u32[]{:S(2)}) copy-start(bf16[1024,256]{1,0:T(8,128)(2,1)} %cot_ref.1) | copy-start | bytes 1572868
  22.1 6.5 %copy-start.3 = (bf16[256,256]{1,0:T(8,128)(2,1)S(1)}, bf16[256,256]{1,0:T(8,128)(2,1)}, u32[]{:S(2)}) copy-start(bf16[256,256]{1,0:T(8,128)(2,1)} %w_ref.1) | copy-start | bytes 393220
  23.6 4.0 %collective-permute-start.4 = (bf16[640,256]{1,0:T(8,128)(2,1)S(1)}, bf16[640,256]{1,0:T(8,128)(2,1)S(1)}, u32[]{:S(2)}, u32[]{:S(2)}) collective-permute-start(bf16[640,256]{1,0:T(8,128)(2,1)S(1)} %collective-permute-done.1.refs_1_), channel_id=1, source_target_pairs={{0,1},{1,0},{2,3},{3,2},{4,5},{5,4},{6,7},{7,6},{8,9},{9,8},{10,11... | collective-permute-start | bytes 983048 | tf_op jit(solution)/shard_map/ppermute | solution.py:60
  23.6 4.9 %collective-permute-start.8 = (bf16[384,256]{1,0:T(8,128)(2,1)S(1)}, bf16[384,256]{1,0:T(8,128)(2,1)S(1)}, u32[]{:S(2)}, u32[]{:S(2)}) collective-permute-start(bf16[384,256]{1,0:T(8,128)(2,1)S(1)} %collective-permute-done.6.refs_2_), channel_id=1, source_target_pairs={{0,1},{1,0},{2,3},{3,2},{4,5},{5,4},{6,7},{7,6},{8,9},{9,8},{10,11... | collective-permute-start | bytes 589832 | tf_op jit(solution)/shard_map/ppermute | solution.py:60
  26.8 1.7 %collective-permute-start.7 = (bf16[384,256]{1,0:T(8,128)(2,1)S(1)}, bf16[384,256]{1,0:T(8,128)(2,1)S(1)}, u32[]{:S(2)}, u32[]{:S(2)}) collective-permute-start(bf16[384,256]{1,0:T(8,128)(2,1)S(1)} %collective-permute-done.5.refs_1_), channel_id=1, source_target_pairs={{0,1},{1,0},{2,3},{3,2},{4,5},{5,4},{6,7},{7,6},{8,9},{9,8},{10,11... | collective-permute-start | bytes 589832 | tf_op jit(solution)/shard_map/ppermute | solution.py:60
  31.8 2.1 %collective-permute-start.9 = (bf16[1024,256]{1,0:T(8,128)(2,1)S(1)}, bf16[1024,256]{1,0:T(8,128)(2,1)S(1)}, u32[]{:S(2)}, u32[]{:S(2)}) collective-permute-start(bf16[1024,256]{1,0:T(8,128)(2,1)S(1)} %get-tuple-element.29), channel_id=1, source_target_pairs={{0,1},{1,0},{2,3},{3,2},{4,5},{5,4},{6,7},{7,6},{8,9},{9,8},{10,11... | collective-permute-start | bytes 1572872 | tf_op jit(solution)/shard_map/ppermute | solution.py:60
  33.7 4.7 %collective-permute-start.14 = (f32[256,256]{1,0:T(8,128)S(1)}, f32[256,256]{1,0:T(8,128)S(1)}, u32[]{:S(2)}, u32[]{:S(2)}) collective-permute-start(f32[256,256]{1,0:T(8,128)S(1)} %get-tuple-element.35), channel_id=1, source_target_pairs={{0,1},{1,0},{2,3},{3,2},{4,5},{5,4},{6,7},{7,6},{8,9},{9,8},{10,11... | collective-permute-start | bytes 786440 | tf_op jit(solution)/shard_map/ppermute | solution.py:60
  34.1 16.0 %collective-permute-start.11 = (bf16[1024,256]{1,0:T(8,128)(2,1)S(1)}, bf16[1024,256]{1,0:T(8,128)(2,1)S(1)}, u32[]{:S(2)}, u32[]{:S(2)}) collective-permute-start(bf16[1024,256]{1,0:T(8,128)(2,1)S(1)} %add_convert_fusion.1), channel_id=1, source_target_pairs={{4,0},{5,1},{8,4},{9,5},{12,8},{13,9},{2,6},{3,7},{6,10},{7,11},{1... | collective-permute-start | bytes 1572872 | tf_op jit(solution)/shard_map/ppermute | solution.py:75
  38.5 5.5 %collective-permute-start.15 = (bf16[256,256]{1,0:T(8,128)(2,1)S(1)}, bf16[256,256]{1,0:T(8,128)(2,1)S(1)}, u32[]{:S(2)}, u32[]{:S(2)}) collective-permute-start(bf16[256,256]{1,0:T(8,128)(2,1)S(1)} %add_convert_fusion.3), channel_id=1, source_target_pairs={{0,2},{1,3},{2,0},{3,1},{4,6},{5,7},{6,4},{7,5},{8,10},{9,11},{10,... | collective-permute-start | bytes 393224 | tf_op jit(solution)/shard_map/ppermute | solution.py:327
  47.4 2.8 %collective-permute-start.12 = (bf16[1024,256]{1,0:T(8,128)(2,1)S(1)}, bf16[1024,256]{1,0:T(8,128)(2,1)S(1)}, u32[]{:S(2)}, u32[]{:S(2)}) collective-permute-start(bf16[1024,256]{1,0:T(8,128)(2,1)S(1)} %spread_side_x.1), channel_id=1, source_target_pairs={{0,1},{1,0},{2,3},{3,2},{4,5},{5,4},{6,7},{7,6},{8,9},{9,8},{10,11... | collective-permute-start | bytes 1572872 | tf_op jit(solution)/shard_map/ppermute | solution.py:60
  50.4 5.0 %collective-permute-start.16 = (bf16[256,256]{1,0:T(8,128)(2,1)S(1)}, bf16[256,256]{1,0:T(8,128)(2,1)S(1)}, u32[]{:S(2)}, u32[]{:S(2)}) collective-permute-start(bf16[256,256]{1,0:T(8,128)(2,1)S(1)} %convert_add_fusion.1), channel_id=1, source_target_pairs={{0,4},{1,5},{2,6},{3,7},{4,0},{5,1},{6,2},{7,3},{8,12},{9,13},{10,... | collective-permute-start | bytes 393224 | tf_op jit(solution)/shard_map/ppermute | solution.py:327
  51.7 12.4 %collective-permute-start.10 = (bf16[1024,256]{1,0:T(8,128)(2,1)S(1)}, bf16[1024,256]{1,0:T(8,128)(2,1)S(1)}, u32[]{:S(2)}, u32[]{:S(2)}) collective-permute-start(bf16[1024,256]{1,0:T(8,128)(2,1)S(1)} %spread_own_x.1), channel_id=1, source_target_pairs={{0,1},{1,0},{2,3},{3,2},{4,5},{5,4},{6,7},{7,6},{8,9},{9,8},{10,11... | collective-permute-start | bytes 1572872 | tf_op jit(solution)/shard_map/ppermute | solution.py:60
  51.7 14.3 %collective-permute-start.13 = (bf16[1024,256]{1,0:T(8,128)(2,1)S(1)}, bf16[1024,256]{1,0:T(8,128)(2,1)S(1)}, u32[]{:S(2)}, u32[]{:S(2)}) collective-permute-start(bf16[1024,256]{1,0:T(8,128)(2,1)S(1)} %add_convert_fusion), channel_id=1, source_target_pairs={{0,2},{1,3},{2,0},{3,1},{4,6},{5,7},{6,4},{7,5},{8,10},{9,11},{10,... | collective-permute-start | bytes 1572872 | tf_op jit(solution)/shard_map/ppermute | solution.py:64
  55.4 8.6 %collective-permute-start.17 = (bf16[256,256]{1,0:T(8,128)(2,1)S(1)}, bf16[256,256]{1,0:T(8,128)(2,1)S(1)}, u32[]{:S(2)}, u32[]{:S(2)}) collective-permute-start(bf16[256,256]{1,0:T(8,128)(2,1)S(1)} %add_convert_fusion.2), channel_id=1, source_target_pairs={{0,8},{1,9},{2,10},{3,11},{4,12},{5,13},{6,14},{7,15},{8,0},{9,1},... | collective-permute-start | bytes 393224 | tf_op jit(solution)/shard_map/ppermute | solution.py:327
  64.1 2.2 %collective-permute-start.18 = (f32[256,256]{1,0:T(8,128)S(1)}, f32[256,256]{1,0:T(8,128)S(1)}, u32[]{:S(2)}, u32[]{:S(2)}) collective-permute-start(f32[256,256]{1,0:T(8,128)S(1)} %convert_add_fusion.kept_ref), channel_id=1, source_target_pairs={{0,1},{1,0},{2,3},{3,2},{4,5},{5,4},{6,7},{7,6},{8,9},{9,8},{10,11... | collective-permute-start | bytes 786440 | tf_op jit(solution)/shard_map/ppermute | solution.py:60

commit v4 on v3

--- a/solution.py
+++ b/solution.py
@@ -14,10 +14,12 @@
 OWN, OWN_X, SIDE, SIDE_X, PLANE, PLANE_X = range(6)
 PARTS = 6
 LIMIT = 4 << 20
-CUT = 128
+CUT = 64
 SHORT = pl.CostEstimate(flops=0, bytes_accessed=0, transcendentals=0)
+RELAY = pl.CostEstimate(flops=10**10, bytes_accessed=0, transcendentals=0)
 LONG = pl.CostEstimate(flops=10**10, bytes_accessed=0, transcendentals=0)
-FORWARD = 10
+FORWARD = 11
+BACKWARD = 12
 
 
 def vmem_spec():
@@ -64,20 +66,13 @@
     return lax.ppermute(array, "row", [(i, i ^ 2) for i in range(count)])
 
 
-def over_planes(array, count, back):
+def over_planes(array, count, back, ends):
     step = [(i, i + 4) for i in range(count) if i % 4 < 2 and i + 4 < count]
     step += [(i, i - 4) for i in range(count) if i % 4 >= 2 and i >= 4]
-    if back:
-        step = [(b, a) for a, b in step]
-        step += [(0, count - 4), (1, count - 3), (count - 2, 2), (count - 1, 3)]
-    else:
+    if ends == "around":
+        step += [(count - 4, 0), (count - 3, 1), (2, count - 2), (3, count - 1)]
+    elif ends == "side":
         step += [(count - 4, count - 2), (count - 3, count - 1), (2, 0), (3, 1)]
-    return lax.ppermute(array, "row", step)
-
-
-def past_side(array, count, back):
-    step = [(i, (i ^ 2) + 4) for i in range(count) if i % 4 >= 2 and i + 4 < count]
-    step += [(i, (i ^ 2) - 4) for i in range(count) if i % 4 < 2 and i >= 4]
     return lax.ppermute(array, "row", [(b, a) for a, b in step] if back else step)
 
 
@@ -166,8 +161,8 @@
     a_ref, out_ref = refs[0], refs[-1]
     sources = refs[1:-1]
     total = sources[-1][...] if started else None
-    for (part, low), source in zip(terms, sources):
-        product = dot(a_ref[part, :, low : low + source.shape[0]], source[...])
+    for (part, low, high, at), source in zip(terms, sources):
+        product = dot(a_ref[part, :, low:high], source[at : at + high - low, :])
         total = product if total is None else total + product
     out_ref[...] = total
 
@@ -180,44 +175,50 @@
     )[0]
 
 
-def cut_kernel(at, src_ref, out_ref, sems):
+def cut_kernel(split, src_ref, low_ref, high_ref, sems):
     copies = []
-    rows = out_ref.shape[0]
-    for i, low in enumerate(range(0, rows, CUT)):
-        size = min(CUT, rows - low)
-        copies.append(
-            pltpu.make_async_copy(src_ref.at[pl.ds(at + low, size)], out_ref.at[pl.ds(low, size)], sems.at[i])
-        )
+    for i, low in enumerate(range(0, src_ref.shape[0], CUT)):
+        target = low_ref.at[pl.ds(low, CUT)] if low < split else high_ref.at[pl.ds(low - split, CUT)]
+        copies.append(pltpu.make_async_copy(src_ref.at[pl.ds(low, CUT)], target, sems.at[i]))
     for copy in copies:
         copy.start()
     for copy in copies:
         copy.wait()
 
 
-def cut(array, at, end):
+def cut(array, split):
+    rows, width = array.shape
     return pl.pallas_call(
-        functools.partial(cut_kernel, at),
-        out_shape=pltpu.VMEM((end - at, array.shape[1]), array.dtype),
+        functools.partial(cut_kernel, split),
+        out_shape=[pltpu.VMEM((split, width), array.dtype), pltpu.VMEM((rows - split, width), array.dtype)],
         in_specs=[hbm_spec()],
-        out_specs=vmem_spec(),
-        scratch_shapes=[pltpu.SemaphoreType.DMA((pl.cdiv(end - at, CUT),))],
+        out_specs=[vmem_spec()] * 2,
+        scratch_shapes=[pltpu.SemaphoreType.DMA((rows // CUT,))],
         compiler_params=pltpu.CompilerParams(vmem_limit_bytes=LIMIT),
         cost_estimate=SHORT,
         name="cut",
     )(in_hbm(array))
 
 
-def middle_kernel(terms, a_ref, total_ref, x_ref, w_ref, r_ref, cot_ref, *refs):
-    last_refs, refs = refs[: len(terms)], refs[len(terms) :]
-    out_hbm, grad_ref, ax_ref, ht_ref, px_ref, out_ref, sems = refs
+def join_kernel(a_ref, b_ref, out_ref):
+    rows = a_ref.shape[0]
+    out_ref[:rows, :] = a_ref[...]
+    out_ref[rows:, :] = b_ref[...]
+
+
+def middle_kernel(terms, end, a_ref, total_ref, x_ref, w_ref, r_ref, cot_ref, *refs):
+    last_ref, *refs = refs
+    out_hbm, grad_ref, ax_ref, ht_ref, low_ref, high_ref, out_ref, sems = refs
     rows = x_ref.shape[0]
     step = rows // sems.shape[0]
     copies = []
     for i in range(sems.shape[0]):
         here = slice(i * step, (i + 1) * step)
         ax = total_ref[here, :]
-        for (part, low, high), last_ref in zip(terms, last_refs):
-            ax = ax + dot(a_ref[part, here, low:high], last_ref[...])
+        at = 0
+        for part, low, high in terms:
+            ax = ax + dot(a_ref[part, here, low:high], last_ref[at : at + high - low, :])
+            at += high - low
         ax = ax.astype(BF16)
         ax_ref[here, :] = ax
         pre = dot(ax, w_ref[...]) + dot(x_ref[here, :], r_ref[...])
@@ -232,21 +233,23 @@
         grad = (cot_ref[here, :].astype(F32) * (gate * (1.0 + pre * (1.0 - gate)))).astype(BF16)
         grad_ref[here, :] = grad
         ht_ref[:, here] = dot_nt(w_ref[...], grad).astype(BF16)
-    px_ref[...] = dot(ht_ref[...], a_ref[PLANE_X, :, :]).T.astype(BF16)
+    low_ref[...] = dot(ht_ref[...], a_ref[PLANE_X, :, :end]).T.astype(BF16)
+    high_ref[...] = dot(ht_ref[...], a_ref[PLANE_X, :, end:]).T.astype(BF16)
     for copy in copies:
         copy.wait()
 
 
-def middle(terms, *args):
+def middle(terms, end, *args):
     rows, width = args[2].shape
     wide = pltpu.VMEM((rows, width), BF16)
     return pl.pallas_call(
-        functools.partial(middle_kernel, terms),
+        functools.partial(middle_kernel, terms, end),
         out_shape=[
-            pltpu.HBM((rows, width), BF16), wide, wide, pltpu.VMEM((width, rows), BF16), wide
+            pltpu.HBM((rows, width), BF16), wide, wide, pltpu.VMEM((width, rows), BF16),
+            pltpu.VMEM((end, width), BF16), pltpu.VMEM((rows - end, width), BF16),
         ],
         in_specs=[vmem_spec()] * len(args),
-        out_specs=[hbm_spec()] + [vmem_spec()] * 4,
+        out_specs=[hbm_spec()] + [vmem_spec()] * 5,
         scratch_shapes=[wide, pltpu.SemaphoreType.DMA((4,))],
         compiler_params=pltpu.CompilerParams(vmem_limit_bytes=LIMIT),
         cost_estimate=SHORT,
@@ -254,15 +257,26 @@
     )(*[in_vmem(a) for a in args])
 
 
-def spread_kernel(part, a_ref, ht_ref, out_ref):
-    half = out_ref.shape[0] // 2
-    for here in (slice(0, half), slice(half, None)):
-        out_ref[here, :] = dot(ht_ref[...], a_ref[part, :, here]).T.astype(out_ref.dtype)
-
-
-def spread(dense, ht, part, dtype, name):
-    shape = (dense.shape[1], ht.shape[0])
-    return kernel_call(functools.partial(spread_kernel, part), name, [(shape, dtype)], [dense, ht])[0]
+def spread_kernel(part, cuts, a_ref, ht_ref, *out_refs):
+    for (low, high), out_ref in zip(cuts, out_refs):
+        out_ref[...] = dot(ht_ref[...], a_ref[part, :, low:high]).T.astype(out_ref.dtype)
+
+
+def spread(dense, ht, part, cuts, dtype, name):
+    outs = [((high - low, ht.shape[0]), dtype) for low, high in cuts]
+    return kernel_call(functools.partial(spread_kernel, part, cuts), name, outs, [dense, ht])
+
+
+def pack_kernel(share_ref, other_ref, kept_ref, arrived_ref, out_ref):
+    rows = share_ref.shape[0]
+    out_ref[:rows, :] = (share_ref[...].astype(F32) + other_ref[...].astype(F32)).astype(BF16)
+    out_ref[rows:, :] = (kept_ref[...] + arrived_ref[...]).astype(BF16)
+
+
+def unpack_kernel(packed_ref, arrived_ref, share_ref, sum_ref):
+    rows = share_ref.shape[0]
+    share_ref[...] = arrived_ref[:rows, :]
+    sum_ref[...] = (packed_ref[rows:, :].astype(F32) + arrived_ref[rows:, :].astype(F32)).astype(BF16)
 
 
 def own_kernel(a_ref, ht_ref, grad_ref, r_ref, out_ref):
@@ -271,8 +285,12 @@
         out_ref[here, :] = dot(ht_ref[...], a_ref[OWN, :, here]).T + dot_nt(grad_ref[here, :], r_ref[...])
 
 
-def final_kernel(own_ref, other_ref, arrived_ref, out_ref):
-    out_ref[...] = (own_ref[...] + other_ref[...].astype(F32) + arrived_ref[...].astype(F32)).astype(BF16)
+def final_kernel(split, own_ref, other_ref, low_ref, high_ref, direct_ref, out_ref):
+    for rows, refs in ((slice(0, split), (low_ref,)), (slice(split, None), (high_ref, direct_ref))):
+        total = own_ref[rows, :] + other_ref[rows, :].astype(F32)
+        for ref in refs:
+            total = total + ref[...].astype(F32)
+        out_ref[rows, :] = total.astype(BF16)
 
 
 def scaled_kernel(
@@ -311,7 +329,7 @@
 
 
 def relayed(own, arrived):
-    return kernel_call(relay_kernel, "relay", [(own.shape, F32)], [own, arrived], LONG)[0]
+    return kernel_call(relay_kernel, "relay", [(own.shape, F32)], [own, arrived], RELAY)[0]
 
 
 def weight_kernel(ax_ref, x_ref, grad_ref, kept_ref, sent_ref):
@@ -336,50 +354,68 @@
     rows, width = features.shape
     split = rows * FORWARD // 16
 
-    side_low = flip_side(cut(features, 0, split), count)
+    low, high = cut(features, split)
+    side_low = flip_side(low, count)
+    passing = over_planes(high, count, True, "around")
     dense = dense_adjacency(tile_rows, tile_cols, tile_count, block_tiles, rows)
-    high = cut(after(features, dense), split, rows)
-    side_low, high = lax.optimization_barrier((side_low, high))
-    side_high = flip_side(high, count)
-    plane_high = past_side(high, count, False)
-    plane_low = over_planes(side_low, count, False)
+    joined = kernel_call(join_kernel, "join", [((2 * (rows - split), width), BF16)], [high, after(passing, dense)])[0]
+    highs = flip_side(joined, count)
+    side_low = after(side_low, joined)
+    plane_low = over_planes(side_low, count, False, "around")
     side_x_low = flip_core(side_low, count)
     own_x = flip_core(after(features, side_low), count)
-    total = gathered(dense, [(OWN, 0), (OWN_X, 0)], [features, own_x], None, "gather_own")
-    total = gathered(dense, [(SIDE, 0), (SIDE_X, 0)], [side_low, side_x_low], total, "gather_side")
+    whole, first, rest = (0, rows, 0), (0, split, 0), (split, rows, 0)
+    total = gathered(dense, [(OWN, *whole), (OWN_X, *whole)], [features, own_x], None, "gather_own")
+    total = gathered(dense, [(SIDE, *first), (SIDE_X, *first)], [side_low, side_x_low], total, "gather_side")
     plane_low = after(plane_low, total)
     plane_x_low = flip_core(plane_low, count)
-    side_x_high = flip_core(side_high, count)
-    plane_x_high = flip_core(plane_high, count)
-    total = gathered(dense, [(SIDE, split), (PLANE, split)], [side_high, plane_high], total, "gather_high")
-    total = gathered(dense, [(PLANE, 0), (PLANE_X, 0)], [plane_low, plane_x_low], total, "gather_plane")
-
-    layer_out, grad_pre, gathered_x, ht, px = middle(
-        [(SIDE_X, split, rows), (PLANE_X, split, rows)],
-        dense, total, features, weight, root_weight, cotangent, side_x_high, plane_x_high,
+    highs_x = flip_core(highs, count)
+    total = gathered(dense, [(SIDE, *rest), (PLANE, split, rows, rows - split)], [highs, highs], total, "gather_high")
+    total = gathered(dense, [(PLANE, *first), (PLANE_X, *first)], [plane_low, plane_x_low], total, "gather_plane")
+
+    split_back = rows * BACKWARD // 16
+    back = [(0, split_back), (split_back, rows)]
+    layer_out, grad_pre, gathered_x, ht, px_low, px_high = middle(
+        [(SIDE_X, split, rows), (PLANE_X, split, rows)], split_back,
+        dense, total, features, weight, root_weight, cotangent, highs_x,
     )
 
-    share = added(spread(dense, ht, PLANE, BF16, "spread_plane"), flip_core(px, count))
-    far = over_planes(share, count, True)
+    (p_low,) = spread(dense, ht, PLANE, back[:1], BF16, "spread_plane_low")
+    p_low = added(p_low, flip_core(px_low, count))
+    far = over_planes(p_low, count, True, "around")
+    (p_high,) = spread(dense, after(ht, p_low), PLANE, back[1:], BF16, "spread_plane_high")
 
     square = ((width, width), F32)
     kept, sent = kernel_call(weight_kernel, "weight_products", [square, square], [gathered_x, features, grad_pre])
-    kept = kept + flip_core(sent, count)
-    kept = exchanged(kept, 2, count)
-
-    ht = after(ht, share)
-    sx = flip_core(spread(dense, ht, SIDE_X, BF16, "spread_side_x"), count)
-    s = spread(dense, ht, SIDE, F32, "spread_side")
-    ox = spread(dense, ht, OWN_X, BF16, "spread_own_x")
+    high, wide = rows - split_back, (width, width)
+    packed = kernel_call(
+        pack_kernel, "pack", [((high + width, width), BF16)], [p_high, flip_core(px_high, count), kept, flip_core(sent, count)]
+    )[0]
+    passing, mine = kernel_call(
+        unpack_kernel, "unpack", [((high, width), BF16), (wide, BF16)], [packed, flip_side(packed, count)]
+    )
+
+    ht = after(ht, packed)
+    sx_low, sx_high = [flip_core(part, count) for part in spread(dense, ht, SIDE_X, back, BF16, "spread_side_x")]
+    s_low, s_high = spread(dense, ht, SIDE, back, F32, "spread_side")
+    s_high = added(s_high, sx_high)
+    near_high = flip_side(s_high, count)
+    ht = after(ht, s_high)
+    (ox,) = spread(dense, ht, OWN_X, [(0, rows)], BF16, "spread_own_x")
     own = kernel_call(own_kernel, "spread_own", [((rows, width), F32)], [dense, ht, grad_pre, root_weight])[0]
-    through = added(relayed(after(s, own, ox), far), sx)
-    near = flip_side(through, count)
-    kept = after(kept, through)
-    hop = 4
+    through = added(relayed(after(s_low, own, ox, near_high), far), sx_low)
+    near_low = flip_side(through, count)
+    direct = over_planes(passing, count, False, None)
+    theirs = lax.ppermute(after(mine, own), "row", [(i, i ^ 4) for i in range(count)])
+    kept = added(mine, after(theirs, through), F32)
+    hop = 8
     while hop < count:
         kept = exchanged(kept, hop, count)
         hop *= 2
-    result = kernel_call(final_kernel, "final", [((rows, width), BF16)], [own, flip_core(ox, count), near], LONG)[0]
+    result = kernel_call(
+        functools.partial(final_kernel, split_back), "final", [((rows, width), BF16)],
+        [own, flip_core(ox, count), near_low, near_high, direct], LONG,
+    )[0]
     grad_features, total_weight, total_root = scaled(
         1.0 / math.sqrt(count * rows), result, kept, flip_core(kept, count)
     )

time: 67.7 us -> 62.8 us (0.928)
  waiting for transfers between devices: 23.6 us -> 17.5 us
  starting transfers between devices: 21.3 us -> 22.2 us
  Pallas kernels: 20.4 us -> 21.1 us
    ppermute x3 -> x1, waiting for transfers between devices: 13.8 us -> 3.05 us  [exchanged(): lax.ppermute(mine, 'row', [(i, i ^ hop) for i in range(count)])]
    ppermute x3 -> x5, waiting for transfers between devices: 4.15 us -> 8.72 us  [the longest x4 7.14 us: over_planes(): lax.ppermute(array, 'row', [(b, a) for a, b in step] if back else step)]
    ppermute x3 -> x1, starting transfers between devices: 4.57 us -> 1.22 us  [exchanged(): lax.ppermute(mine, 'row', [(i, i ^ hop) for i in range(count)])]
    ppermute x3 -> x5, starting transfers between devices: 6.8 us -> 8.77 us  [the longest x4 6.98 us: over_planes(): lax.ppermute(array, 'row', [(b, a) for a, b in step] if back else step)]
    ppermute x10 -> x11, waiting for transfers between devices: 0.19 us -> 1.75 us  [flip_core(): return lax.ppermute(array, 'row', [(i, i ^ 1) for i in range(count)])]
    ppermute x3 -> x5, waiting for transfers between devices: 5.4 us -> 3.99 us  [flip_side(): return lax.ppermute(array, 'row', [(i, i ^ 2) for i in range(count)])]
    ppermute x10 -> x11, starting transfers between devices: 1.82 us -> 2.95 us  [flip_core(): return lax.ppermute(array, 'row', [(i, i ^ 1) for i in range(count)])]
    ppermute x3 -> x5, starting transfers between devices: 8.15 us -> 9.26 us  [flip_side(): return lax.ppermute(array, 'row', [(i, i ^ 2) for i in range(count)])]
  transfers between devices with their start and end apart: 19 -> 22, of which waited for: 9 -> 9; matrix products, arithmetic and copies ran while one was open for 0% -> 0% of each run, Pallas kernels for 22% -> 23%
where the time goes in v4:
time: 62.8 us
  starting transfers between devices  22.2 us (35%)
  Pallas kernels  21.1 us (34%)
  waiting for transfers between devices  17.5 us (28%)
  between operations  1.62 us (3%)
    ppermute x5, starting transfers between devices, flip_side(): return lax.ppermute(array, 'row', [(i, i ^ 2) for i in range(count)])  9.26 us
    pallas_call x16, Pallas kernels, kernel_call(): pl.pallas_call(kernel, out_shape=[pltpu.VMEM(shape, dtype) for shape, dty...  9.22 us
    ppermute x4, waiting for transfers between devices, over_planes(): lax.ppermute(array, 'row', [(b, a) for a, b in step] if back else step)  7.14 us
    ppermute x4, starting transfers between devices, over_planes(): lax.ppermute(array, 'row', [(b, a) for a, b in step] if back else step)  6.98 us
    pallas_call x1, Pallas kernels, dense_adjacency(): pl.pallas_call(dense_kernel, out_shape=pltpu.VMEM((PARTS, width, width),...  6.33 us
    ppermute x5, waiting for transfers between devices, flip_side(): return lax.ppermute(array, 'row', [(i, i ^ 2) for i in range(count)])  3.99 us
    pallas_call x1, Pallas kernels, middle(): pl.pallas_call(functools.partial(middle_kernel, terms, end), out_shape=[p...  3.39 us
    ppermute x1, waiting for transfers between devices, exchanged(): lax.ppermute(mine, 'row', [(i, i ^ hop) for i in range(count)])  3.05 us
  transfers between devices with their start and end apart: 22, of which 9 were waited for; matrix products, arithmetic and copies ran while one was open for 0% of the time, Pallas kernels for 23%

profile of v4, /device:TPU:0, one launch (start us, length us, event | category | flops | bytes accessed | tf_op | source)
XLA Modules:
  0.0 62.8 jit_solution(11638547579892603507)
XLA Ops:
  0.6 1.2 %cut.1 = (bf16[704,256]{1,0:T(8,128)(2,1)S(1)}, bf16[320,256]{1,0:T(8,128)(2,1)S(1)}) custom-call(bf16[1024,256]{1,0:T(8,128)(2,1)} %x_ref.3), custom_call_target="tpu_custom_call" | custom-call | tf_op jit(solution)/shard_map/cut/pallas_call | solution.py:191
  1.8 3.0 %collective-permute-start = (bf16[704,256]{1,0:T(8,128)(2,1)S(1)}, bf16[704,256]{1,0:T(8,128)(2,1)S(1)}, u32[]{:S(2)}, u32[]{:S(2)}) collective-permute-start(bf16[704,256]{1,0:T(8,128)(2,1)S(1)} %get-tuple-element.33), channel_id=1, source_target_pairs={{0,2},{1,3},{2,0},{3,1},{4,6},{5,7},{6,4},{7,5},{8,10},{9,11},{10,... | collective-permute-start | bytes 1081352 | tf_op jit(solution)/shard_map/ppermute | solution.py:66
  4.9 3.6 %collective-permute-start.1 = (bf16[320,256]{1,0:T(8,128)(2,1)S(1)}, bf16[320,256]{1,0:T(8,128)(2,1)S(1)}, u32[]{:S(2)}, u32[]{:S(2)}) collective-permute-start(bf16[320,256]{1,0:T(8,128)(2,1)S(1)} %get-tuple-element.34.a_ref), channel_id=1, source_target_pairs={{4,0},{5,1},{8,4},{9,5},{12,8},{13,9},{2,6},{3,7},{6,10},{7,11},{1... | collective-permute-start | bytes 491528 | tf_op jit(solution)/shard_map/ppermute | solution.py:76
  9.1 6.3 %dense_adjacency.1.refs_0_.a_ref = bf16[6,1024,1024]{2,1,0:T(8,128)(2,1)S(1)} custom-call(s32[1]{0:T(128)S(6)} %copy.12.count_ref, s32[192]{0:T(256)} %rows_hbm.1, s32[192]{0:T(256)} %cols_hbm.1, bf16[192,128,128]{2,1,0:T(8,128)(2,1)} %tiles_ref.1), custom_call_target="tpu_custom_call" | custom-call | tf_op jit(solution)/shard_map/dense_adjacency/pallas_call | solution.py:131
  15.5 0.0 collective-permute-done.1.b_ref
  15.5 0.0 collective-permute-done.refs_1_
  15.5 0.1 collective-permute-start.4
  15.6 0.5 collective-permute-start.3
  16.1 0.0 collective-permute-start.2
  16.1 3.0 %collective-permute-start.6 = (bf16[640,256]{1,0:T(8,128)(2,1)S(1)}, bf16[640,256]{1,0:T(8,128)(2,1)S(1)}, u32[]{:S(2)}, u32[]{:S(2)}) collective-permute-start(bf16[640,256]{1,0:T(8,128)(2,1)S(1)} %join.1), channel_id=1, source_target_pairs={{0,2},{1,3},{2,0},{3,1},{4,6},{5,7},{6,4},{7,5},{8,10},{9,11},{10,... | collective-permute-start | bytes 983048 | tf_op jit(solution)/shard_map/ppermute | solution.py:66
  19.1 0.0 collective-permute-done.4.refs_2_
  19.1 1.3 %gather_own.1.refs_3_ = f32[1024,256]{1,0:T(8,128)S(1)} custom-call(bf16[6,1024,1024]{2,1,0:T(8,128)(2,1)S(1)} %dense_adjacency.1.refs_0_.a_ref, bf16[1024,256]{1,0:T(8,128)(2,1)S(1)} %copy-done, bf16[1024,256]{1,0:T(8,128)(2,1)S(1)} %collective-permute-done.4.refs_2_), custom_call_target="tpu_custom_call" | custom-call | tf_op jit(solution)/shard_map/gather_own/pallas_call | solution.py:50
  20.4 0.0 collective-permute-done.3.refs_2_
  20.4 1.0 %gather_side.1.refs_3_ = f32[1024,256]{1,0:T(8,128)S(1)} custom-call(bf16[6,1024,1024]{2,1,0:T(8,128)(2,1)S(1)} %dense_adjacency.1.refs_0_.a_ref, bf16[704,256]{1,0:T(8,128)(2,1)S(1)} %collective-permute-done.refs_1_, bf16[704,256]{1,0:T(8,128)(2,1)S(1)} %collective-permute-done.3.refs_2_, f32[1024,256]{1,0:T(8,128)S(1)} %gather_own.1.refs_3_), custom_call_target="tpu_custom_call" | custom-call | tf_op jit(solution)/shard_map/gather_side/pallas_call | solution.py:50
  21.4 0.0 copy-start.1
  21.4 0.0 copy-start.2
  21.4 0.0 copy-start.3
  21.4 6.9 %collective-permute-done.2.refs_1_ = bf16[704,256]{1,0:T(8,128)(2,1)S(1)} collective-permute-done((bf16[704,256]{1,0:T(8,128)(2,1)S(1)}, bf16[704,256]{1,0:T(8,128)(2,1)S(1)}, u32[]{:S(2)}, u32[]{:S(2)}) %collective-permute-start.2) | collective-permute-done | bytes 360480 | tf_op jit(solution)/shard_map/ppermute | solution.py:76
  28.3 0.0 collective-permute-start.5
  28.3 0.0 collective-permute-done.6.refs_1_.refs_2_
  28.3 0.5 collective-permute-start.7
  28.8 0.8 %gather_high.1.refs_3_ = f32[1024,256]{1,0:T(8,128)S(1)} custom-call(bf16[6,1024,1024]{2,1,0:T(8,128)(2,1)S(1)} %dense_adjacency.1.refs_0_.a_ref, bf16[640,256]{1,0:T(8,128)(2,1)S(1)} %collective-permute-done.6.refs_1_.refs_2_, bf16[640,256]{1,0:T(8,128)(2,1)S(1)} %collective-permute-done.6.refs_1_.refs_2_, f32[1024,256]{1,0:T(8,128)S(1)} %gather_side.1.refs_3_), custom_call_target="tpu_custom_call" | custom-call | tf_op jit(solution)/shard_map/gather_high/pallas_call | solution.py:50
  29.6 0.4 collective-permute-done.5.refs_2_
  30.0 1.0 %gather_plane.1.total_ref = f32[1024,256]{1,0:T(8,128)S(1)} custom-call(bf16[6,1024,1024]{2,1,0:T(8,128)(2,1)S(1)} %dense_adjacency.1.refs_0_.a_ref, bf16[704,256]{1,0:T(8,128)(2,1)S(1)} %collective-permute-done.2.refs_1_, bf16[704,256]{1,0:T(8,128)(2,1)S(1)} %collective-permute-done.5.refs_2_, f32[1024,256]{1,0:T(8,128)S(1)} %gather_high.1.refs_3_), custom_call_target="tpu_custom_call" | custom-call | tf_op jit(solution)/shard_map/gather_plane/pallas_call | solution.py:50
  31.0 0.0 collective-permute-done.7.refs_0_
  31.0 3.4 %middle.1 = (bf16[1024,256]{1,0:T(8,128)(2,1)}, bf16[1024,256]{1,0:T(8,128)(2,1)S(1)}, bf16[1024,256]{1,0:T(8,128)(2,1)S(1)}, bf16[256,1024]{1,0:T(8,128)(2,1)S(...) custom-call(bf16[6,1024,1024]{2,1,0:T(8,128)(2,1)S(1)} %dense_adjacency.1.refs_0_.a_ref, ...), custom_call_target="tpu_custom_call" | custom-call | tf_op jit(solution)/shard_map/middle/pallas_call | solution.py:245
  34.4 0.2 collective-permute-start.8
  34.6 0.5 weight_products.1
  35.1 0.4 collective-permute-start.10
  35.5 0.1 collective-permute-start.9
  35.7 0.6 %spread_plane_low.1 = bf16[768,256]{1,0:T(8,128)(2,1)S(1)} custom-call(bf16[6,1024,1024]{2,1,0:T(8,128)(2,1)S(1)} %dense_adjacency.1.refs_0_.a_ref, bf16[256,1024]{1,0:T(8,128)(2,1)S(1)} %get-tuple-element.51.ht_ref), custom_call_target="tpu_custom_call" | custom-call | tf_op jit(solution)/shard_map/spread_plane_low/pallas_call | solution.py:50
  36.3 0.0 collective-permute-done.8
  36.4 0.1 add_convert_fusion.1
  36.5 0.4 spread_plane_high.1.share_ref
  36.8 0.1 collective-permute-done.9.other_ref
  36.9 0.0 collective-permute-done.10.arrived_ref
  37.0 0.8 %spread_side_x.1 = (bf16[768,256]{1,0:T(8,128)(2,1)S(1)}, bf16[256,256]{1,0:T(8,128)(2,1)S(1)}) custom-call(bf16[6,1024,1024]{2,1,0:T(8,128)(2,1)S(1)} %dense_adjacency.1.refs_0_.a_ref, bf16[256,1024]{1,0:T(8,128)(2,1)S(1)} %get-tuple-element.51.ht_ref), custom_call_target="tpu_custom_call" | custom-call | tf_op jit(solution)/shard_map/spread_side_x/pallas_call | solution.py:50
  37.8 0.4 collective-permute-start.11
  38.2 0.3 collective-permute-start.14
  38.5 0.0 collective-permute-start.17
  38.5 0.8 %spread_side.1 = (f32[768,256]{1,0:T(8,128)S(1)}, f32[256,256]{1,0:T(8,128)S(1)}) custom-call(bf16[6,1024,1024]{2,1,0:T(8,128)(2,1)S(1)} %dense_adjacency.1.refs_0_.a_ref, bf16[256,1024]{1,0:T(8,128)(2,1)S(1)} %get-tuple-element.51.ht_ref), custom_call_target="tpu_custom_call" | custom-call | tf_op jit(solution)/shard_map/spread_side/pallas_call | solution.py:50
  39.4 0.0 collective-permute-done.11
  39.4 2.1 %collective-permute-start.13 = (bf16[256,256]{1,0:T(8,128)(2,1)S(1)}, bf16[256,256]{1,0:T(8,128)(2,1)S(1)}, u32[]{:S(2)}, u32[]{:S(2)}) collective-permute-start(bf16[256,256]{1,0:T(8,128)(2,1)S(1)} %add_convert_fusion.3), channel_id=1, source_target_pairs={{0,2},{1,3},{2,0},{3,1},{4,6},{5,7},{6,4},{7,5},{8,10},{9,11},{10,... | collective-permute-start | bytes 393224 | tf_op jit(solution)/shard_map/ppermute | solution.py:66
  41.5 0.0 collective-permute-start.15
  41.5 0.9 %spread_own.1.own_ref = f32[1024,256]{1,0:T(8,128)S(1)} custom-call(bf16[6,1024,1024]{2,1,0:T(8,128)(2,1)S(1)} %dense_adjacency.1.refs_0_.a_ref, bf16[256,1024]{1,0:T(8,128)(2,1)S(1)} %get-tuple-element.51.ht_ref, bf16[1024,256]{1,0:T(8,128)(2,1)S(1)} %get-tuple-element.45.grad_ref, bf16[256,256]{1,0:T(8,128)(2,1)S(1)} %copy-done.1), custom_call_target="tpu_custom_call" | custom-call | tf_op jit(solution)/shard_map/spread_own/pallas_call | solution.py:50
  42.4 0.8 %spread_own_x.1 = bf16[1024,256]{1,0:T(8,128)(2,1)S(1)} custom-call(bf16[6,1024,1024]{2,1,0:T(8,128)(2,1)S(1)} %dense_adjacency.1.refs_0_.a_ref, bf16[256,1024]{1,0:T(8,128)(2,1)S(1)} %get-tuple-element.51.ht_ref), custom_call_target="tpu_custom_call" | custom-call | tf_op jit(solution)/shard_map/spread_own_x/pallas_call | solution.py:50
  43.2 0.6 collective-permute-start.12
  43.8 3.9 %collective-permute-done.17.arrived_ref = bf16[512,256]{1,0:T(8,128)(2,1)S(1)} collective-permute-done((bf16[512,256]{1,0:T(8,128)(2,1)S(1)}, bf16[512,256]{1,0:T(8,128)(2,1)S(1)}, u32[]{:S(2)}, u32[]{:S(2)}) %collective-permute-start.17) | collective-permute-done | bytes 262176 | tf_op jit(solution)/shard_map/ppermute | solution.py:66
  47.7 1.8 %collective-permute-start.19 = (bf16[256,256]{1,0:T(8,128)(2,1)S(1)}, bf16[256,256]{1,0:T(8,128)(2,1)S(1)}, u32[]{:S(2)}, u32[]{:S(2)}) collective-permute-start(bf16[256,256]{1,0:T(8,128)(2,1)S(1)} %get-tuple-element.57), channel_id=1, source_target_pairs={{0,4},{1,5},{2,6},{3,7},{4,0},{5,1},{6,2},{7,3},{8,12},{9,13},{10,... | collective-permute-start | bytes 393224 | tf_op jit(solution)/shard_map/ppermute | solution.py:409
  49.5 0.1 collective-permute-done.13.high_ref
  49.6 0.3 collective-permute-done.14.arrived_ref
  49.9 0.1 relay.1
  50.0 0.0 collective-permute-done.15
  50.0 0.1 add_convert_fusion
  50.1 1.1 %collective-permute-start.16 = (bf16[768,256]{1,0:T(8,128)(2,1)S(1)}, bf16[768,256]{1,0:T(8,128)(2,1)S(1)}, u32[]{:S(2)}, u32[]{:S(2)}) collective-permute-start(bf16[768,256]{1,0:T(8,128)(2,1)S(1)} %add_convert_fusion), channel_id=1, source_target_pairs={{0,2},{1,3},{2,0},{3,1},{4,6},{5,7},{6,4},{7,5},{8,10},{9,11},{10,... | collective-permute-start | bytes 1179656 | tf_op jit(solution)/shard_map/ppermute | solution.py:66
  51.2 1.6 %collective-permute-done.19 = bf16[256,256]{1,0:T(8,128)(2,1)S(1)} collective-permute-done((bf16[256,256]{1,0:T(8,128)(2,1)S(1)}, bf16[256,256]{1,0:T(8,128)(2,1)S(1)}, u32[]{:S(2)}, u32[]{:S(2)}) %collective-permute-start.19) | collective-permute-done | bytes 131104 | tf_op jit(solution)/shard_map/ppermute | solution.py:409
  52.8 1.2 %collective-permute-start.20 = (bf16[256,256]{1,0:T(8,128)(2,1)S(1)}, bf16[256,256]{1,0:T(8,128)(2,1)S(1)}, u32[]{:S(2)}, u32[]{:S(2)}) collective-permute-start(bf16[256,256]{1,0:T(8,128)(2,1)S(1)} %add_convert_fusion.2), channel_id=1, source_target_pairs={{0,8},{1,9},{2,10},{3,11},{4,12},{5,13},{6,14},{7,15},{8,0},{9,1},... | collective-permute-start | bytes 393224 | tf_op jit(solution)/shard_map/ppermute | solution.py:345
  54.0 3.0 %collective-permute-start.18 = (bf16[256,256]{1,0:T(8,128)(2,1)S(1)}, bf16[256,256]{1,0:T(8,128)(2,1)S(1)}, u32[]{:S(2)}, u32[]{:S(2)}) collective-permute-start(bf16[256,256]{1,0:T(8,128)(2,1)S(1)} %get-tuple-element.55), channel_id=1, source_target_pairs={{0,4},{1,5},{4,8},{5,9},{8,12},{9,13},{6,2},{7,3},{10,6},{11,7},{1... | collective-permute-start | bytes 393224 | tf_op jit(solution)/shard_map/ppermute | solution.py:76
  57.1 3.1 %collective-permute-done.20 = bf16[256,256]{1,0:T(8,128)(2,1)S(1)} collective-permute-done((bf16[256,256]{1,0:T(8,128)(2,1)S(1)}, bf16[256,256]{1,0:T(8,128)(2,1)S(1)}, u32[]{:S(2)}, u32[]{:S(2)}) %collective-permute-start.20) | collective-permute-done | bytes 131104 | tf_op jit(solution)/shard_map/ppermute | solution.py:345
  60.2 0.1 collective-permute-start.21
  60.3 0.0 collective-permute-done.16.low_ref
  60.3 0.2 final.1.out_ref
  60.5 1.3 %collective-permute-done.21.other_ref = f32[256,256]{1,0:T(8,128)S(1)} collective-permute-done((f32[256,256]{1,0:T(8,128)S(1)}, f32[256,256]{1,0:T(8,128)S(1)}, u32[]{:S(2)}, u32[]{:S(2)}) %collective-permute-start.21) | collective-permute-done | bytes 262176 | tf_op jit(solution)/shard_map/ppermute | solution.py:62
  61.8 1.0 %scaled.1 = (bf16[1024,256]{1,0:T(8,128)(2,1)}, f32[256,256]{1,0:T(8,128)}, f32[256,256]{1,0:T(8,128)}) custom-call(bf16[1024,256]{1,0:T(8,128)(2,1)S(1)} %final.1.out_ref, f32[256,256]{1,0:T(8,128)S(1)} %convert_add_fusion.kept_ref, f32[256,256]{1,0:T(8,128)S(1)} %collective-permute-done.21.other_ref), custom_call_target="tpu_custom_call" | custom-call | tf_op jit(solution)/shard_map/scaled/pallas_call | solution.py:315
  (13 shorter events, 0.2 us)
Async XLA Ops:
  0.6 14.9 %copy-start = (bf16[1024,256]{1,0:T(8,128)(2,1)S(1)}, bf16[1024,256]{1,0:T(8,128)(2,1)}, u32[]{:S(2)}) copy-start(bf16[1024,256]{1,0:T(8,128)(2,1)} %x_ref.3) | copy-start | bytes 1572868
  1.8 13.7 %collective-permute-start = (bf16[704,256]{1,0:T(8,128)(2,1)S(1)}, bf16[704,256]{1,0:T(8,128)(2,1)S(1)}, u32[]{:S(2)}, u32[]{:S(2)}) collective-permute-start(bf16[704,256]{1,0:T(8,128)(2,1)S(1)} %get-tuple-element.33), channel_id=1, source_target_pairs={{0,2},{1,3},{2,0},{3,1},{4,6},{5,7},{6,4},{7,5},{8,10},{9,11},{10,... | collective-permute-start | bytes 1081352 | tf_op jit(solution)/shard_map/ppermute | solution.py:66
  4.9 10.6 %collective-permute-start.1 = (bf16[320,256]{1,0:T(8,128)(2,1)S(1)}, bf16[320,256]{1,0:T(8,128)(2,1)S(1)}, u32[]{:S(2)}, u32[]{:S(2)}) collective-permute-start(bf16[320,256]{1,0:T(8,128)(2,1)S(1)} %get-tuple-element.34.a_ref), channel_id=1, source_target_pairs={{4,0},{5,1},{8,4},{9,5},{12,8},{13,9},{2,6},{3,7},{6,10},{7,11},{1... | collective-permute-start | bytes 491528 | tf_op jit(solution)/shard_map/ppermute | solution.py:76
  15.5 3.6 %collective-permute-start.4 = (bf16[1024,256]{1,0:T(8,128)(2,1)S(1)}, bf16[1024,256]{1,0:T(8,128)(2,1)S(1)}, u32[]{:S(2)}, u32[]{:S(2)}) collective-permute-start(bf16[1024,256]{1,0:T(8,128)(2,1)S(1)} %copy-done), channel_id=1, source_target_pairs={{0,1},{1,0},{2,3},{3,2},{4,5},{5,4},{6,7},{7,6},{8,9},{9,8},{10,11... | collective-permute-start | bytes 1572872 | tf_op jit(solution)/shard_map/ppermute | solution.py:62
  15.6 4.8 %collective-permute-start.3 = (bf16[704,256]{1,0:T(8,128)(2,1)S(1)}, bf16[704,256]{1,0:T(8,128)(2,1)S(1)}, u32[]{:S(2)}, u32[]{:S(2)}) collective-permute-start(bf16[704,256]{1,0:T(8,128)(2,1)S(1)} %collective-permute-done.refs_1_), channel_id=1, source_target_pairs={{0,1},{1,0},{2,3},{3,2},{4,5},{5,4},{6,7},{7,6},{8,9},{9,8},{10,11... | collective-permute-start | bytes 1081352 | tf_op jit(solution)/shard_map/ppermute | solution.py:62
  16.1 12.2 %collective-permute-start.2 = (bf16[704,256]{1,0:T(8,128)(2,1)S(1)}, bf16[704,256]{1,0:T(8,128)(2,1)S(1)}, u32[]{:S(2)}, u32[]{:S(2)}) collective-permute-start(bf16[704,256]{1,0:T(8,128)(2,1)S(1)} %collective-permute-done.refs_1_), channel_id=1, source_target_pairs={{0,4},{1,5},{4,8},{5,9},{8,12},{9,13},{6,2},{7,3},{10,6},{11,7},{1... | collective-permute-start | bytes 1081352 | tf_op jit(solution)/shard_map/ppermute | solution.py:76
  16.1 12.2 %collective-permute-start.6 = (bf16[640,256]{1,0:T(8,128)(2,1)S(1)}, bf16[640,256]{1,0:T(8,128)(2,1)S(1)}, u32[]{:S(2)}, u32[]{:S(2)}) collective-permute-start(bf16[640,256]{1,0:T(8,128)(2,1)S(1)} %join.1), channel_id=1, source_target_pairs={{0,2},{1,3},{2,0},{3,1},{4,6},{5,7},{6,4},{7,5},{8,10},{9,11},{10,... | collective-permute-start | bytes 983048 | tf_op jit(solution)/shard_map/ppermute | solution.py:66
  21.4 9.6 %copy-start.1 = (bf16[256,256]{1,0:T(8,128)(2,1)S(1)}, bf16[256,256]{1,0:T(8,128)(2,1)}, u32[]{:S(2)}) copy-start(bf16[256,256]{1,0:T(8,128)(2,1)} %r_ref.3) | copy-start | bytes 393220
  21.4 9.6 %copy-start.2 = (bf16[1024,256]{1,0:T(8,128)(2,1)S(1)}, bf16[1024,256]{1,0:T(8,128)(2,1)}, u32[]{:S(2)}) copy-start(bf16[1024,256]{1,0:T(8,128)(2,1)} %cot_ref.1) | copy-start | bytes 1572868
  21.4 9.6 %copy-start.3 = (bf16[256,256]{1,0:T(8,128)(2,1)S(1)}, bf16[256,256]{1,0:T(8,128)(2,1)}, u32[]{:S(2)}) copy-start(bf16[256,256]{1,0:T(8,128)(2,1)} %w_ref.1) | copy-start | bytes 393220
  28.3 1.7 %collective-permute-start.5 = (bf16[704,256]{1,0:T(8,128)(2,1)S(1)}, bf16[704,256]{1,0:T(8,128)(2,1)S(1)}, u32[]{:S(2)}, u32[]{:S(2)}) collective-permute-start(bf16[704,256]{1,0:T(8,128)(2,1)S(1)} %collective-permute-done.2.refs_1_), channel_id=1, source_target_pairs={{0,1},{1,0},{2,3},{3,2},{4,5},{5,4},{6,7},{7,6},{8,9},{9,8},{10,11... | collective-permute-start | bytes 1081352 | tf_op jit(solution)/shard_map/ppermute | solution.py:62
  28.3 2.7 %collective-permute-start.7 = (bf16[640,256]{1,0:T(8,128)(2,1)S(1)}, bf16[640,256]{1,0:T(8,128)(2,1)S(1)}, u32[]{:S(2)}, u32[]{:S(2)}) collective-permute-start(bf16[640,256]{1,0:T(8,128)(2,1)S(1)} %collective-permute-done.6.refs_1_.refs_2_), channel_id=1, source_target_pairs={{0,1},{1,0},{2,3},{3,2},{4,5},{5,4},{6,7},{7,6},{8,9},{9,8},{10,11... | collective-permute-start | bytes 983048 | tf_op jit(solution)/shard_map/ppermute | solution.py:62
  34.4 1.9 %collective-permute-start.8 = (bf16[768,256]{1,0:T(8,128)(2,1)S(1)}, bf16[768,256]{1,0:T(8,128)(2,1)S(1)}, u32[]{:S(2)}, u32[]{:S(2)}) collective-permute-start(bf16[768,256]{1,0:T(8,128)(2,1)S(1)} %get-tuple-element.41), channel_id=1, source_target_pairs={{0,1},{1,0},{2,3},{3,2},{4,5},{5,4},{6,7},{7,6},{8,9},{9,8},{10,11... | collective-permute-start | bytes 1179656 | tf_op jit(solution)/shard_map/ppermute | solution.py:62
  35.1 1.8 %collective-permute-start.10 = (f32[256,256]{1,0:T(8,128)S(1)}, f32[256,256]{1,0:T(8,128)S(1)}, u32[]{:S(2)}, u32[]{:S(2)}) collective-permute-start(f32[256,256]{1,0:T(8,128)S(1)} %get-tuple-element.47), channel_id=1, source_target_pairs={{0,1},{1,0},{2,3},{3,2},{4,5},{5,4},{6,7},{7,6},{8,9},{9,8},{10,11... | collective-permute-start | bytes 786440 | tf_op jit(solution)/shard_map/ppermute | solution.py:62
  35.5 1.4 %collective-permute-start.9 = (bf16[256,256]{1,0:T(8,128)(2,1)S(1)}, bf16[256,256]{1,0:T(8,128)(2,1)S(1)}, u32[]{:S(2)}, u32[]{:S(2)}) collective-permute-start(bf16[256,256]{1,0:T(8,128)(2,1)S(1)} %get-tuple-element.43), channel_id=1, source_target_pairs={{0,1},{1,0},{2,3},{3,2},{4,5},{5,4},{6,7},{7,6},{8,9},{9,8},{10,11... | collective-permute-start | bytes 393224 | tf_op jit(solution)/shard_map/ppermute | solution.py:62
  37.8 1.6 %collective-permute-start.11 = (bf16[256,256]{1,0:T(8,128)(2,1)S(1)}, bf16[256,256]{1,0:T(8,128)(2,1)S(1)}, u32[]{:S(2)}, u32[]{:S(2)}) collective-permute-start(bf16[256,256]{1,0:T(8,128)(2,1)S(1)} %get-tuple-element.50), channel_id=1, source_target_pairs={{0,1},{1,0},{2,3},{3,2},{4,5},{5,4},{6,7},{7,6},{8,9},{9,8},{10,11... | collective-permute-start | bytes 393224 | tf_op jit(solution)/shard_map/ppermute | solution.py:62
  38.2 11.7 %collective-permute-start.14 = (bf16[768,256]{1,0:T(8,128)(2,1)S(1)}, bf16[768,256]{1,0:T(8,128)(2,1)S(1)}, u32[]{:S(2)}, u32[]{:S(2)}) collective-permute-start(bf16[768,256]{1,0:T(8,128)(2,1)S(1)} %add_convert_fusion.1), channel_id=1, source_target_pairs={{4,0},{5,1},{8,4},{9,5},{12,8},{13,9},{2,6},{3,7},{6,10},{7,11},{1... | collective-permute-start | bytes 1179656 | tf_op jit(solution)/shard_map/ppermute | solution.py:76
  38.5 9.2 %collective-permute-start.17 = (bf16[512,256]{1,0:T(8,128)(2,1)S(1)}, bf16[512,256]{1,0:T(8,128)(2,1)S(1)}, u32[]{:S(2)}, u32[]{:S(2)}) collective-permute-start(bf16[512,256]{1,0:T(8,128)(2,1)S(1)} %pack.1.packed_ref), channel_id=1, source_target_pairs={{0,2},{1,3},{2,0},{3,1},{4,6},{5,7},{6,4},{7,5},{8,10},{9,11},{10,... | collective-permute-start | bytes 786440 | tf_op jit(solution)/shard_map/ppermute | solution.py:66
  39.4 10.2 %collective-permute-start.13 = (bf16[256,256]{1,0:T(8,128)(2,1)S(1)}, bf16[256,256]{1,0:T(8,128)(2,1)S(1)}, u32[]{:S(2)}, u32[]{:S(2)}) collective-permute-start(bf16[256,256]{1,0:T(8,128)(2,1)S(1)} %add_convert_fusion.3), channel_id=1, source_target_pairs={{0,2},{1,3},{2,0},{3,1},{4,6},{5,7},{6,4},{7,5},{8,10},{9,11},{10,... | collective-permute-start | bytes 393224 | tf_op jit(solution)/shard_map/ppermute | solution.py:66
  41.5 8.5 %collective-permute-start.15 = (bf16[768,256]{1,0:T(8,128)(2,1)S(1)}, bf16[768,256]{1,0:T(8,128)(2,1)S(1)}, u32[]{:S(2)}, u32[]{:S(2)}) collective-permute-start(bf16[768,256]{1,0:T(8,128)(2,1)S(1)} %get-tuple-element.54), channel_id=1, source_target_pairs={{0,1},{1,0},{2,3},{3,2},{4,5},{5,4},{6,7},{7,6},{8,9},{9,8},{10,11... | collective-permute-start | bytes 1179656 | tf_op jit(solution)/shard_map/ppermute | solution.py:62
  43.2 17.0 %collective-permute-start.12 = (bf16[1024,256]{1,0:T(8,128)(2,1)S(1)}, bf16[1024,256]{1,0:T(8,128)(2,1)S(1)}, u32[]{:S(2)}, u32[]{:S(2)}) collective-permute-start(bf16[1024,256]{1,0:T(8,128)(2,1)S(1)} %spread_own_x.1), channel_id=1, source_target_pairs={{0,1},{1,0},{2,3},{3,2},{4,5},{5,4},{6,7},{7,6},{8,9},{9,8},{10,11... | collective-permute-start | bytes 1572872 | tf_op jit(solution)/shard_map/ppermute | solution.py:62
  47.7 5.0 %collective-permute-start.19 = (bf16[256,256]{1,0:T(8,128)(2,1)S(1)}, bf16[256,256]{1,0:T(8,128)(2,1)S(1)}, u32[]{:S(2)}, u32[]{:S(2)}) collective-permute-start(bf16[256,256]{1,0:T(8,128)(2,1)S(1)} %get-tuple-element.57), channel_id=1, source_target_pairs={{0,4},{1,5},{2,6},{3,7},{4,0},{5,1},{6,2},{7,3},{8,12},{9,13},{10,... | collective-permute-start | bytes 393224 | tf_op jit(solution)/shard_map/ppermute | solution.py:409
  50.1 10.2 %collective-permute-start.16 = (bf16[768,256]{1,0:T(8,128)(2,1)S(1)}, bf16[768,256]{1,0:T(8,128)(2,1)S(1)}, u32[]{:S(2)}, u32[]{:S(2)}) collective-permute-start(bf16[768,256]{1,0:T(8,128)(2,1)S(1)} %add_convert_fusion), channel_id=1, source_target_pairs={{0,2},{1,3},{2,0},{3,1},{4,6},{5,7},{6,4},{7,5},{8,10},{9,11},{10,... | collective-permute-start | bytes 1179656 | tf_op jit(solution)/shard_map/ppermute | solution.py:66
  52.8 7.3 %collective-permute-start.20 = (bf16[256,256]{1,0:T(8,128)(2,1)S(1)}, bf16[256,256]{1,0:T(8,128)(2,1)S(1)}, u32[]{:S(2)}, u32[]{:S(2)}) collective-permute-start(bf16[256,256]{1,0:T(8,128)(2,1)S(1)} %add_convert_fusion.2), channel_id=1, source_target_pairs={{0,8},{1,9},{2,10},{3,11},{4,12},{5,13},{6,14},{7,15},{8,0},{9,1},... | collective-permute-start | bytes 393224 | tf_op jit(solution)/shard_map/ppermute | solution.py:345
  54.0 6.2 %collective-permute-start.18 = (bf16[256,256]{1,0:T(8,128)(2,1)S(1)}, bf16[256,256]{1,0:T(8,128)(2,1)S(1)}, u32[]{:S(2)}, u32[]{:S(2)}) collective-permute-start(bf16[256,256]{1,0:T(8,128)(2,1)S(1)} %get-tuple-element.55), channel_id=1, source_target_pairs={{0,4},{1,5},{4,8},{5,9},{8,12},{9,13},{6,2},{7,3},{10,6},{11,7},{1... | collective-permute-start | bytes 393224 | tf_op jit(solution)/shard_map/ppermute | solution.py:76
  60.2 1.6 %collective-permute-start.21 = (f32[256,256]{1,0:T(8,128)S(1)}, f32[256,256]{1,0:T(8,128)S(1)}, u32[]{:S(2)}, u32[]{:S(2)}) collective-permute-start(f32[256,256]{1,0:T(8,128)S(1)} %convert_add_fusion.kept_ref), channel_id=1, source_target_pairs={{0,1},{1,0},{2,3},{3,2},{4,5},{5,4},{6,7},{7,6},{8,9},{9,8},{10,11... | collective-permute-start | bytes 786440 | tf_op jit(solution)/shard_map/ppermute | solution.py:62

commit v5 on v4

--- a/solution.py
+++ b/solution.py
@@ -17,8 +17,9 @@
 CUT = 64
 SHORT = pl.CostEstimate(flops=0, bytes_accessed=0, transcendentals=0)
 RELAY = pl.CostEstimate(flops=10**10, bytes_accessed=0, transcendentals=0)
+BRIEF = pl.CostEstimate(flops=5 * 10**8, bytes_accessed=0, transcendentals=0)
 LONG = pl.CostEstimate(flops=10**10, bytes_accessed=0, transcendentals=0)
-FORWARD = 11
+FORWARD = 10
 BACKWARD = 12
 
 
@@ -206,9 +207,9 @@
     out_ref[rows:, :] = b_ref[...]
 
 
-def middle_kernel(terms, end, a_ref, total_ref, x_ref, w_ref, r_ref, cot_ref, *refs):
+def middle_kernel(terms, shares, a_ref, total_ref, x_ref, w_ref, r_ref, cot_ref, *refs):
     last_ref, *refs = refs
-    out_hbm, grad_ref, ax_ref, ht_ref, low_ref, high_ref, out_ref, sems = refs
+    out_hbm, grad_ref, ax_ref, ht_ref, *share_refs, out_ref, sems = refs
     rows = x_ref.shape[0]
     step = rows // sems.shape[0]
     copies = []
@@ -233,23 +234,23 @@
         grad = (cot_ref[here, :].astype(F32) * (gate * (1.0 + pre * (1.0 - gate)))).astype(BF16)
         grad_ref[here, :] = grad
         ht_ref[:, here] = dot_nt(w_ref[...], grad).astype(BF16)
-    low_ref[...] = dot(ht_ref[...], a_ref[PLANE_X, :, :end]).T.astype(BF16)
-    high_ref[...] = dot(ht_ref[...], a_ref[PLANE_X, :, end:]).T.astype(BF16)
+    for (part, low, high), share_ref in zip(shares, share_refs):
+        share_ref[...] = dot(ht_ref[...], a_ref[part, :, low:high]).T.astype(BF16)
     for copy in copies:
         copy.wait()
 
 
-def middle(terms, end, *args):
+def middle(terms, shares, *args):
     rows, width = args[2].shape
     wide = pltpu.VMEM((rows, width), BF16)
     return pl.pallas_call(
-        functools.partial(middle_kernel, terms, end),
+        functools.partial(middle_kernel, terms, shares),
         out_shape=[
             pltpu.HBM((rows, width), BF16), wide, wide, pltpu.VMEM((width, rows), BF16),
-            pltpu.VMEM((end, width), BF16), pltpu.VMEM((rows - end, width), BF16),
+            *[pltpu.VMEM((high - low, width), BF16) for _, low, high in shares],
         ],
         in_specs=[vmem_spec()] * len(args),
-        out_specs=[hbm_spec()] + [vmem_spec()] * 5,
+        out_specs=[hbm_spec()] + [vmem_spec()] * (3 + len(shares)),
         scratch_shapes=[wide, pltpu.SemaphoreType.DMA((4,))],
         compiler_params=pltpu.CompilerParams(vmem_limit_bytes=LIMIT),
         cost_estimate=SHORT,
@@ -358,26 +359,33 @@
     side_low = flip_side(low, count)
     passing = over_planes(high, count, True, "around")
     dense = dense_adjacency(tile_rows, tile_cols, tile_count, block_tiles, rows)
-    joined = kernel_call(join_kernel, "join", [((2 * (rows - split), width), BF16)], [high, after(passing, dense)])[0]
+    whole, first, rest = (0, rows, 0), (0, split, 0), (split, rows, 0)
+    own_x = flip_core(after(features, low), count)
+    total = gathered(dense, [(OWN, *whole), (OWN_X, *whole)], [features, own_x], None, "gather_own")
+    joined = kernel_call(join_kernel, "join", [((2 * (rows - split), width), BF16)], [high, after(passing, total, side_low)])[0]
     highs = flip_side(joined, count)
     side_low = after(side_low, joined)
     plane_low = over_planes(side_low, count, False, "around")
     side_x_low = flip_core(side_low, count)
-    own_x = flip_core(after(features, side_low), count)
-    whole, first, rest = (0, rows, 0), (0, split, 0), (split, rows, 0)
-    total = gathered(dense, [(OWN, *whole), (OWN_X, *whole)], [features, own_x], None, "gather_own")
     total = gathered(dense, [(SIDE, *first), (SIDE_X, *first)], [side_low, side_x_low], total, "gather_side")
     plane_low = after(plane_low, total)
     plane_x_low = flip_core(plane_low, count)
     highs_x = flip_core(highs, count)
     total = gathered(dense, [(SIDE, *rest), (PLANE, split, rows, rows - split)], [highs, highs], total, "gather_high")
-    total = gathered(dense, [(PLANE, *first), (PLANE_X, *first)], [plane_low, plane_x_low], total, "gather_plane")
+    total = gathered(
+        dense,
+        [(PLANE, *first), (SIDE_X, *rest), (PLANE_X, split, rows, rows - split)],
+        [plane_low, highs_x, highs_x],
+        total,
+        "gather_high_x",
+        BRIEF,
+    )
 
     split_back = rows * BACKWARD // 16
     back = [(0, split_back), (split_back, rows)]
-    layer_out, grad_pre, gathered_x, ht, px_low, px_high = middle(
-        [(SIDE_X, split, rows), (PLANE_X, split, rows)], split_back,
-        dense, total, features, weight, root_weight, cotangent, highs_x,
+    layer_out, grad_pre, gathered_x, ht, px_low, px_high, sx_high = middle(
+        [(PLANE_X, 0, split)], [(PLANE_X, *back[0]), (PLANE_X, *back[1]), (SIDE_X, *back[1])],
+        dense, total, features, weight, root_weight, cotangent, plane_x_low,
     )
 
     (p_low,) = spread(dense, ht, PLANE, back[:1], BF16, "spread_plane_low")
@@ -395,12 +403,13 @@
         unpack_kernel, "unpack", [((high, width), BF16), (wide, BF16)], [packed, flip_side(packed, count)]
     )
 
-    ht = after(ht, packed)
-    sx_low, sx_high = [flip_core(part, count) for part in spread(dense, ht, SIDE_X, back, BF16, "spread_side_x")]
-    s_low, s_high = spread(dense, ht, SIDE, back, F32, "spread_side")
-    s_high = added(s_high, sx_high)
+    (s_high,) = spread(dense, after(ht, packed), SIDE, back[1:], F32, "spread_side_high")
+    s_high = added(s_high, flip_core(sx_high, count))
     near_high = flip_side(s_high, count)
     ht = after(ht, s_high)
+    (sx_low,) = spread(dense, ht, SIDE_X, back[:1], BF16, "spread_side_x_low")
+    sx_low = flip_core(sx_low, count)
+    (s_low,) = spread(dense, after(ht, mine), SIDE, back[:1], F32, "spread_side_low")
     (ox,) = spread(dense, ht, OWN_X, [(0, rows)], BF16, "spread_own_x")
     own = kernel_call(own_kernel, "spread_own", [((rows, width), F32)], [dense, ht, grad_pre, root_weight])[0]
     through = added(relayed(after(s_low, own, ox, near_high), far), sx_low)

time: 62.8 us -> 61.5 us (0.979)
  starting transfers between devices: 22.2 us -> 18 us
  waiting for transfers between devices: 17.5 us -> 21.3 us
  Pallas kernels: 21.1 us -> 19.9 us
    ppermute x5, waiting for transfers between devices: 3.99 us -> 13.1 us  [flip_side(): return lax.ppermute(array, 'row', [(i, i ^ 2) for i in range(count)])]
    ppermute x4, waiting for transfers between devices: 7.14 us -> 1.1 us  [over_planes(): lax.ppermute(array, 'row', [(b, a) for a, b in step] if back else step)]
    ppermute x5, starting transfers between devices: 9.26 us -> 5.82 us  [flip_side(): return lax.ppermute(array, 'row', [(i, i ^ 2) for i in range(count)])]
    ppermute x4, starting transfers between devices: 6.98 us -> 8.07 us  [over_planes(): lax.ppermute(array, 'row', [(b, a) for a, b in step] if back else step)]
    pallas_call x1, Pallas kernels: 3.39 us -> 2.6 us  [middle(): pl.pallas_call(functools.partial(middle_kernel, terms, shares), out_shape...]
    ppermute x1, starting transfers between devices: 1.22 us -> 0.55 us  [exchanged(): lax.ppermute(mine, 'row', [(i, i ^ hop) for i in range(count)])]
    ppermute x1, waiting for transfers between devices: 3.05 us -> 3.73 us  [exchanged(): lax.ppermute(mine, 'row', [(i, i ^ hop) for i in range(count)])]
    ppermute x1, starting transfers between devices: 1.79 us -> 1.13 us  [body(): lax.ppermute(after(mine, own), 'row', [(i, i ^ 4) for i in range(count)])]
  transfers between devices with their start and end apart: 22 -> 22, of which waited for: 9 -> 7; matrix products, arithmetic and copies ran while one was open for 0% -> 0% of each run, Pallas kernels for 23% -> 25%
where the time goes in v5:
time: 61.5 us; the launch traced here: 61.2 us
  waiting for transfers between devices  21.3 us (35%)
  Pallas kernels  19.9 us (32%)
  starting transfers between devices  18 us (29%)
  between operations  1.66 us (3%)
    ppermute x5, waiting for transfers between devices, flip_side(): return lax.ppermute(array, 'row', [(i, i ^ 2) for i in range(count)])  13.1 us
    pallas_call x17, Pallas kernels, kernel_call(): pl.pallas_call(kernel, out_shape=[pltpu.VMEM(shape, dtype) for shape, dty...  9.34 us
    ppermute x4, starting transfers between devices, over_planes(): lax.ppermute(array, 'row', [(b, a) for a, b in step] if back else step)  8.07 us
    pallas_call x1, Pallas kernels, dense_adjacency(): pl.pallas_call(dense_kernel, out_shape=pltpu.VMEM((PARTS, width, width),...  5.82 us
    ppermute x5, starting transfers between devices, flip_side(): return lax.ppermute(array, 'row', [(i, i ^ 2) for i in range(count)])  5.82 us
    ppermute x1, waiting for transfers between devices, exchanged(): lax.ppermute(mine, 'row', [(i, i ^ hop) for i in range(count)])  3.73 us
    pallas_call x1, Pallas kernels, middle(): pl.pallas_call(functools.partial(middle_kernel, terms, shares), out_shape...  2.6 us
    ppermute x11, starting transfers between devices, flip_core(): return lax.ppermute(array, 'row', [(i, i ^ 1) for i in range(count)])  2.45 us
  transfers between devices with their start and end apart: 22, of which 7 were waited for; matrix products, arithmetic and copies ran while one was open for 0% of the time, Pallas kernels for 25%

profile of v5, /device:TPU:0, one launch (start us, length us, event | category | flops | bytes accessed | tf_op | source)
XLA Modules:
  0.0 61.2 jit_solution(9695004650945522225)
XLA Ops:
  0.6 0.0 copy-start
  0.6 1.2 %cut.1 = (bf16[640,256]{1,0:T(8,128)(2,1)S(1)}, bf16[384,256]{1,0:T(8,128)(2,1)S(1)}) custom-call(bf16[1024,256]{1,0:T(8,128)(2,1)} %x_ref.3), custom_call_target="tpu_custom_call" | custom-call | tf_op jit(solution)/shard_map/cut/pallas_call | solution.py:192
  1.8 0.5 collective-permute-start.2
  2.4 2.6 %collective-permute-start = (bf16[640,256]{1,0:T(8,128)(2,1)S(1)}, bf16[640,256]{1,0:T(8,128)(2,1)S(1)}, u32[]{:S(2)}, u32[]{:S(2)}) collective-permute-start(bf16[640,256]{1,0:T(8,128)(2,1)S(1)} %get-tuple-element.31), channel_id=1, source_target_pairs={{0,2},{1,3},{2,0},{3,1},{4,6},{5,7},{6,4},{7,5},{8,10},{9,11},{10,... | collective-permute-start | bytes 983048 | tf_op jit(solution)/shard_map/ppermute | solution.py:67
  5.0 3.6 %collective-permute-start.1 = (bf16[384,256]{1,0:T(8,128)(2,1)S(1)}, bf16[384,256]{1,0:T(8,128)(2,1)S(1)}, u32[]{:S(2)}, u32[]{:S(2)}) collective-permute-start(bf16[384,256]{1,0:T(8,128)(2,1)S(1)} %get-tuple-element.32.a_ref), channel_id=1, source_target_pairs={{4,0},{5,1},{8,4},{9,5},{12,8},{13,9},{2,6},{3,7},{6,10},{7,11},{1... | collective-permute-start | bytes 589832 | tf_op jit(solution)/shard_map/ppermute | solution.py:77
  9.2 5.8 %dense_adjacency.1.refs_0_.a_ref = bf16[6,1024,1024]{2,1,0:T(8,128)(2,1)S(1)} custom-call(s32[1]{0:T(128)S(6)} %copy.12.count_ref, s32[192]{0:T(256)} %rows_hbm.1, s32[192]{0:T(256)} %cols_hbm.1, bf16[192,128,128]{2,1,0:T(8,128)(2,1)} %tiles_ref.1), custom_call_target="tpu_custom_call" | custom-call | tf_op jit(solution)/shard_map/dense_adjacency/pallas_call | solution.py:132
  15.0 0.0 collective-permute-done.2.refs_2_
  15.1 1.3 %gather_own.1.refs_3_ = f32[1024,256]{1,0:T(8,128)S(1)} custom-call(bf16[6,1024,1024]{2,1,0:T(8,128)(2,1)S(1)} %dense_adjacency.1.refs_0_.a_ref, bf16[1024,256]{1,0:T(8,128)(2,1)S(1)} %copy-done, bf16[1024,256]{1,0:T(8,128)(2,1)S(1)} %collective-permute-done.2.refs_2_), custom_call_target="tpu_custom_call" | custom-call | tf_op jit(solution)/shard_map/gather_own/pallas_call | solution.py:51
  16.3 0.0 collective-permute-done.1.b_ref
  16.3 0.0 collective-permute-done.refs_1_
  16.4 0.1 collective-permute-start.5
  16.5 0.1 collective-permute-start.4
  16.5 0.4 collective-permute-start.3
  17.0 9.4 %collective-permute-done.5.refs_1_.refs_2_ = bf16[768,256]{1,0:T(8,128)(2,1)S(1)} collective-permute-done((bf16[768,256]{1,0:T(8,128)(2,1)S(1)}, bf16[768,256]{1,0:T(8,128)(2,1)S(1)}, u32[]{:S(2)}, u32[]{:S(2)}) %collective-permute-start.5) | collective-permute-done | bytes 393248 | tf_op jit(solution)/shard_map/ppermute | solution.py:67
  26.3 0.0 collective-permute-start.6
  26.3 0.0 collective-permute-done.4.refs_2_
  26.3 1.0 %gather_side.1.refs_3_ = f32[1024,256]{1,0:T(8,128)S(1)} custom-call(bf16[6,1024,1024]{2,1,0:T(8,128)(2,1)S(1)} %dense_adjacency.1.refs_0_.a_ref, bf16[640,256]{1,0:T(8,128)(2,1)S(1)} %collective-permute-done.refs_1_, bf16[640,256]{1,0:T(8,128)(2,1)S(1)} %collective-permute-done.4.refs_2_, f32[1024,256]{1,0:T(8,128)S(1)} %gather_own.1.refs_3_), custom_call_target="tpu_custom_call" | custom-call | tf_op jit(solution)/shard_map/gather_side/pallas_call | solution.py:51
  27.3 0.0 copy-start.1
  27.3 0.0 copy-start.2
  27.3 0.0 copy-start.3
  27.4 1.1 %collective-permute-done.3.refs_1_ = bf16[640,256]{1,0:T(8,128)(2,1)S(1)} collective-permute-done((bf16[640,256]{1,0:T(8,128)(2,1)S(1)}, bf16[640,256]{1,0:T(8,128)(2,1)S(1)}, u32[]{:S(2)}, u32[]{:S(2)}) %collective-permute-start.3) | collective-permute-done | bytes 327712 | tf_op jit(solution)/shard_map/ppermute | solution.py:77
  28.4 0.0 collective-permute-start.7
  28.5 0.7 %gather_high.1.refs_4_ = f32[1024,256]{1,0:T(8,128)S(1)} custom-call(bf16[6,1024,1024]{2,1,0:T(8,128)(2,1)S(1)} %dense_adjacency.1.refs_0_.a_ref, bf16[768,256]{1,0:T(8,128)(2,1)S(1)} %collective-permute-done.5.refs_1_.refs_2_, bf16[768,256]{1,0:T(8,128)(2,1)S(1)} %collective-permute-done.5.refs_1_.refs_2_, f32[1024,256]{1,0:T(8,128)S(1)} %gather_side.1.refs_3_), custom_call_target="tpu_custom_call" | custom-call | tf_op jit(solution)/shard_map/gather_high/pallas_call | solution.py:51
  29.2 0.0 collective-permute-done.6.refs_2_.refs_3_
  29.2 1.1 %gather_high_x.1.total_ref = f32[1024,256]{1,0:T(8,128)S(1)} custom-call(bf16[6,1024,1024]{2,1,0:T(8,128)(2,1)S(1)} %dense_adjacency.1.refs_0_.a_ref, bf16[640,256]{1,0:T(8,128)(2,1)S(1)} %collective-permute-done.3.refs_1_, bf16[768,256]{1,0:T(8,128)(2,1)S(1)} %collective-permute-done.6.refs_2_.refs_3_, ...), custom_call_target="tpu_custom_call" | custom-call | flops 500000000 | tf_op jit(solution)/shard_map/gather_high_x/pallas_call | solution.py:51
  30.3 2.6 %middle.1 = (bf16[1024,256]{1,0:T(8,128)(2,1)}, bf16[1024,256]{1,0:T(8,128)(2,1)S(1)}, bf16[1024,256]{1,0:T(8,128)(2,1)S(1)}, bf16[256,1024]{1,0:T(8,128)(2,1)S(...) custom-call(bf16[6,1024,1024]{2,1,0:T(8,128)(2,1)S(1)} %dense_adjacency.1.refs_0_.a_ref, ...), custom_call_target="tpu_custom_call" | custom-call | tf_op jit(solution)/shard_map/middle/pallas_call | solution.py:246
  32.9 0.6 collective-permute-start.8
  33.5 0.1 collective-permute-start.9
  33.6 0.4 collective-permute-start.11
  34.0 0.7 %spread_plane_low.1 = bf16[768,256]{1,0:T(8,128)(2,1)S(1)} custom-call(bf16[6,1024,1024]{2,1,0:T(8,128)(2,1)S(1)} %dense_adjacency.1.refs_0_.a_ref, bf16[256,1024]{1,0:T(8,128)(2,1)S(1)} %get-tuple-element.50.ht_ref), custom_call_target="tpu_custom_call" | custom-call | tf_op jit(solution)/shard_map/spread_plane_low/pallas_call | solution.py:51
  34.7 0.5 weight_products.1
  35.2 0.1 collective-permute-start.10
  35.3 0.0 collective-permute-done.8
  35.3 0.1 add_convert_fusion.1
  35.4 1.0 %collective-permute-start.15 = (bf16[768,256]{1,0:T(8,128)(2,1)S(1)}, bf16[768,256]{1,0:T(8,128)(2,1)S(1)}, u32[]{:S(2)}, u32[]{:S(2)}) collective-permute-start(bf16[768,256]{1,0:T(8,128)(2,1)S(1)} %add_convert_fusion.1), channel_id=1, source_target_pairs={{4,0},{5,1},{8,4},{9,5},{12,8},{13,9},{2,6},{3,7},{6,10},{7,11},{1... | collective-permute-start | bytes 1179656 | tf_op jit(solution)/shard_map/ppermute | solution.py:77
  36.4 0.4 spread_plane_high.1.share_ref
  36.8 0.0 collective-permute-done.9.other_ref
  36.8 0.0 collective-permute-done.10.arrived_ref
  36.8 0.1 pack.1.packed_ref
  36.9 0.2 collective-permute-start.13
  37.0 0.4 spread_side_high.1
  37.5 2.0 %collective-permute-start.14 = (bf16[256,256]{1,0:T(8,128)(2,1)S(1)}, bf16[256,256]{1,0:T(8,128)(2,1)S(1)}, u32[]{:S(2)}, u32[]{:S(2)}) collective-permute-start(bf16[256,256]{1,0:T(8,128)(2,1)S(1)} %add_convert_fusion.3), channel_id=1, source_target_pairs={{0,2},{1,3},{2,0},{3,1},{4,6},{5,7},{6,4},{7,5},{8,10},{9,11},{10,... | collective-permute-start | bytes 393224 | tf_op jit(solution)/shard_map/ppermute | solution.py:67
  39.5 0.6 %spread_side_x_low.1 = bf16[768,256]{1,0:T(8,128)(2,1)S(1)} custom-call(bf16[6,1024,1024]{2,1,0:T(8,128)(2,1)S(1)} %dense_adjacency.1.refs_0_.a_ref, bf16[256,1024]{1,0:T(8,128)(2,1)S(1)} %get-tuple-element.50.ht_ref), custom_call_target="tpu_custom_call" | custom-call | tf_op jit(solution)/shard_map/spread_side_x_low/pallas_call | solution.py:51
  40.1 0.9 %spread_own.1.own_ref = f32[1024,256]{1,0:T(8,128)S(1)} custom-call(bf16[6,1024,1024]{2,1,0:T(8,128)(2,1)S(1)} %dense_adjacency.1.refs_0_.a_ref, bf16[256,1024]{1,0:T(8,128)(2,1)S(1)} %get-tuple-element.50.ht_ref, bf16[1024,256]{1,0:T(8,128)(2,1)S(1)} %get-tuple-element.43.grad_ref, bf16[256,256]{1,0:T(8,128)(2,1)S(1)} %copy-done.1), custom_call_target="tpu_custom_call" | custom-call | tf_op jit(solution)/shard_map/spread_own/pallas_call | solution.py:51
  41.0 0.8 %spread_own_x.1 = bf16[1024,256]{1,0:T(8,128)(2,1)S(1)} custom-call(bf16[6,1024,1024]{2,1,0:T(8,128)(2,1)S(1)} %dense_adjacency.1.refs_0_.a_ref, bf16[256,1024]{1,0:T(8,128)(2,1)S(1)} %get-tuple-element.50.ht_ref), custom_call_target="tpu_custom_call" | custom-call | tf_op jit(solution)/shard_map/spread_own_x/pallas_call | solution.py:51
  41.8 0.1 collective-permute-start.16
  41.9 0.5 collective-permute-start.12
  42.4 3.7 %collective-permute-done.13.arrived_ref = bf16[512,256]{1,0:T(8,128)(2,1)S(1)} collective-permute-done((bf16[512,256]{1,0:T(8,128)(2,1)S(1)}, bf16[512,256]{1,0:T(8,128)(2,1)S(1)}, u32[]{:S(2)}, u32[]{:S(2)}) %collective-permute-start.13) | collective-permute-done | bytes 262176 | tf_op jit(solution)/shard_map/ppermute | solution.py:67
  46.1 1.1 %collective-permute-start.19 = (bf16[256,256]{1,0:T(8,128)(2,1)S(1)}, bf16[256,256]{1,0:T(8,128)(2,1)S(1)}, u32[]{:S(2)}, u32[]{:S(2)}) collective-permute-start(bf16[256,256]{1,0:T(8,128)(2,1)S(1)} %get-tuple-element.53), channel_id=1, source_target_pairs={{0,4},{1,5},{2,6},{3,7},{4,0},{5,1},{6,2},{7,3},{8,12},{9,13},{10,... | collective-permute-start | bytes 393224 | tf_op jit(solution)/shard_map/ppermute | solution.py:418
  47.3 0.7 %spread_side_low.1.own_ref = f32[768,256]{1,0:T(8,128)S(1)} custom-call(bf16[6,1024,1024]{2,1,0:T(8,128)(2,1)S(1)} %dense_adjacency.1.refs_0_.a_ref, bf16[256,1024]{1,0:T(8,128)(2,1)S(1)} %get-tuple-element.50.ht_ref), custom_call_target="tpu_custom_call" | custom-call | tf_op jit(solution)/shard_map/spread_side_low/pallas_call | solution.py:51
  48.0 0.1 collective-permute-done.14.high_ref
  48.0 0.0 collective-permute-done.15.arrived_ref
  48.1 0.1 relay.1
  48.1 0.1 add_convert_fusion
  48.2 1.0 %collective-permute-start.17 = (bf16[768,256]{1,0:T(8,128)(2,1)S(1)}, bf16[768,256]{1,0:T(8,128)(2,1)S(1)}, u32[]{:S(2)}, u32[]{:S(2)}) collective-permute-start(bf16[768,256]{1,0:T(8,128)(2,1)S(1)} %add_convert_fusion), channel_id=1, source_target_pairs={{0,2},{1,3},{2,0},{3,1},{4,6},{5,7},{6,4},{7,5},{8,10},{9,11},{10,... | collective-permute-start | bytes 1179656 | tf_op jit(solution)/shard_map/ppermute | solution.py:67
  49.2 2.0 %collective-permute-done.19 = bf16[256,256]{1,0:T(8,128)(2,1)S(1)} collective-permute-done((bf16[256,256]{1,0:T(8,128)(2,1)S(1)}, bf16[256,256]{1,0:T(8,128)(2,1)S(1)}, u32[]{:S(2)}, u32[]{:S(2)}) %collective-permute-start.19) | collective-permute-done | bytes 131104 | tf_op jit(solution)/shard_map/ppermute | solution.py:418
  51.2 0.5 collective-permute-start.20
  51.8 3.1 %collective-permute-start.18 = (bf16[256,256]{1,0:T(8,128)(2,1)S(1)}, bf16[256,256]{1,0:T(8,128)(2,1)S(1)}, u32[]{:S(2)}, u32[]{:S(2)}) collective-permute-start(bf16[256,256]{1,0:T(8,128)(2,1)S(1)} %get-tuple-element.52), channel_id=1, source_target_pairs={{0,4},{1,5},{4,8},{5,9},{8,12},{9,13},{6,2},{7,3},{10,6},{11,7},{1... | collective-permute-start | bytes 393224 | tf_op jit(solution)/shard_map/ppermute | solution.py:77
  54.8 3.7 %collective-permute-done.20 = bf16[256,256]{1,0:T(8,128)(2,1)S(1)} collective-permute-done((bf16[256,256]{1,0:T(8,128)(2,1)S(1)}, bf16[256,256]{1,0:T(8,128)(2,1)S(1)}, u32[]{:S(2)}, u32[]{:S(2)}) %collective-permute-start.20) | collective-permute-done | bytes 131104 | tf_op jit(solution)/shard_map/ppermute | solution.py:346
  58.6 0.1 collective-permute-start.21
  58.7 0.0 collective-permute-done.18.direct_ref
  58.7 0.2 final.1.out_ref
  58.9 1.3 %collective-permute-done.21.other_ref = f32[256,256]{1,0:T(8,128)S(1)} collective-permute-done((f32[256,256]{1,0:T(8,128)S(1)}, f32[256,256]{1,0:T(8,128)S(1)}, u32[]{:S(2)}, u32[]{:S(2)}) %collective-permute-start.21) | collective-permute-done | bytes 262176 | tf_op jit(solution)/shard_map/ppermute | solution.py:63
  60.2 1.0 %scaled.1 = (bf16[1024,256]{1,0:T(8,128)(2,1)}, f32[256,256]{1,0:T(8,128)}, f32[256,256]{1,0:T(8,128)}) custom-call(bf16[1024,256]{1,0:T(8,128)(2,1)S(1)} %final.1.out_ref, f32[256,256]{1,0:T(8,128)S(1)} %convert_add_fusion.kept_ref, f32[256,256]{1,0:T(8,128)S(1)} %collective-permute-done.21.other_ref), custom_call_target="tpu_custom_call" | custom-call | tf_op jit(solution)/shard_map/scaled/pallas_call | solution.py:316
  (14 shorter events, 0.2 us)
Async XLA Ops:
  0.6 14.4 %copy-start = (bf16[1024,256]{1,0:T(8,128)(2,1)S(1)}, bf16[1024,256]{1,0:T(8,128)(2,1)}, u32[]{:S(2)}) copy-start(bf16[1024,256]{1,0:T(8,128)(2,1)} %x_ref.3) | copy-start | bytes 1572868
  1.8 13.2 %collective-permute-start.2 = (bf16[1024,256]{1,0:T(8,128)(2,1)}, bf16[1024,256]{1,0:T(8,128)(2,1)S(1)}, u32[]{:S(2)}, u32[]{:S(2)}) collective-permute-start(bf16[1024,256]{1,0:T(8,128)(2,1)} %x_ref.3), channel_id=1, source_target_pairs={{0,1},{1,0},{2,3},{3,2},{4,5},{5,4},{6,7},{7,6},{8,9},{9,8},{10,11... | collective-permute-start | bytes 1572872 | tf_op jit(solution)/shard_map/ppermute | solution.py:63
  2.4 14.0 %collective-permute-start = (bf16[640,256]{1,0:T(8,128)(2,1)S(1)}, bf16[640,256]{1,0:T(8,128)(2,1)S(1)}, u32[]{:S(2)}, u32[]{:S(2)}) collective-permute-start(bf16[640,256]{1,0:T(8,128)(2,1)S(1)} %get-tuple-element.31), channel_id=1, source_target_pairs={{0,2},{1,3},{2,0},{3,1},{4,6},{5,7},{6,4},{7,5},{8,10},{9,11},{10,... | collective-permute-start | bytes 983048 | tf_op jit(solution)/shard_map/ppermute | solution.py:67
  5.0 11.4 %collective-permute-start.1 = (bf16[384,256]{1,0:T(8,128)(2,1)S(1)}, bf16[384,256]{1,0:T(8,128)(2,1)S(1)}, u32[]{:S(2)}, u32[]{:S(2)}) collective-permute-start(bf16[384,256]{1,0:T(8,128)(2,1)S(1)} %get-tuple-element.32.a_ref), channel_id=1, source_target_pairs={{4,0},{5,1},{8,4},{9,5},{12,8},{13,9},{2,6},{3,7},{6,10},{7,11},{1... | collective-permute-start | bytes 589832 | tf_op jit(solution)/shard_map/ppermute | solution.py:77
  16.4 10.0 %collective-permute-start.5 = (bf16[768,256]{1,0:T(8,128)(2,1)S(1)}, bf16[768,256]{1,0:T(8,128)(2,1)S(1)}, u32[]{:S(2)}, u32[]{:S(2)}) collective-permute-start(bf16[768,256]{1,0:T(8,128)(2,1)S(1)} %join.1), channel_id=1, source_target_pairs={{0,2},{1,3},{2,0},{3,1},{4,6},{5,7},{6,4},{7,5},{8,10},{9,11},{10,... | collective-permute-start | bytes 1179656 | tf_op jit(solution)/shard_map/ppermute | solution.py:67
  16.5 9.9 %collective-permute-start.4 = (bf16[640,256]{1,0:T(8,128)(2,1)S(1)}, bf16[640,256]{1,0:T(8,128)(2,1)S(1)}, u32[]{:S(2)}, u32[]{:S(2)}) collective-permute-start(bf16[640,256]{1,0:T(8,128)(2,1)S(1)} %collective-permute-done.refs_1_), channel_id=1, source_target_pairs={{0,1},{1,0},{2,3},{3,2},{4,5},{5,4},{6,7},{7,6},{8,9},{9,8},{10,11... | collective-permute-start | bytes 983048 | tf_op jit(solution)/shard_map/ppermute | solution.py:63
  16.5 11.9 %collective-permute-start.3 = (bf16[640,256]{1,0:T(8,128)(2,1)S(1)}, bf16[640,256]{1,0:T(8,128)(2,1)S(1)}, u32[]{:S(2)}, u32[]{:S(2)}) collective-permute-start(bf16[640,256]{1,0:T(8,128)(2,1)S(1)} %collective-permute-done.refs_1_), channel_id=1, source_target_pairs={{0,4},{1,5},{4,8},{5,9},{8,12},{9,13},{6,2},{7,3},{10,6},{11,7},{1... | collective-permute-start | bytes 983048 | tf_op jit(solution)/shard_map/ppermute | solution.py:77
  26.3 2.8 %collective-permute-start.6 = (bf16[768,256]{1,0:T(8,128)(2,1)S(1)}, bf16[768,256]{1,0:T(8,128)(2,1)S(1)}, u32[]{:S(2)}, u32[]{:S(2)}) collective-permute-start(bf16[768,256]{1,0:T(8,128)(2,1)S(1)} %collective-permute-done.5.refs_1_.refs_2_), channel_id=1, source_target_pairs={{0,1},{1,0},{2,3},{3,2},{4,5},{5,4},{6,7},{7,6},{8,9},{9,8},{10,11... | collective-permute-start | bytes 1179656 | tf_op jit(solution)/shard_map/ppermute | solution.py:63
  27.3 3.0 %copy-start.1 = (bf16[256,256]{1,0:T(8,128)(2,1)S(1)}, bf16[256,256]{1,0:T(8,128)(2,1)}, u32[]{:S(2)}) copy-start(bf16[256,256]{1,0:T(8,128)(2,1)} %r_ref.3) | copy-start | bytes 393220
  27.3 3.0 %copy-start.2 = (bf16[1024,256]{1,0:T(8,128)(2,1)S(1)}, bf16[1024,256]{1,0:T(8,128)(2,1)}, u32[]{:S(2)}) copy-start(bf16[1024,256]{1,0:T(8,128)(2,1)} %cot_ref.1) | copy-start | bytes 1572868
  27.3 3.0 %copy-start.3 = (bf16[256,256]{1,0:T(8,128)(2,1)S(1)}, bf16[256,256]{1,0:T(8,128)(2,1)}, u32[]{:S(2)}) copy-start(bf16[256,256]{1,0:T(8,128)(2,1)} %w_ref.1) | copy-start | bytes 393220
  28.4 1.8 %collective-permute-start.7 = (bf16[640,256]{1,0:T(8,128)(2,1)S(1)}, bf16[640,256]{1,0:T(8,128)(2,1)S(1)}, u32[]{:S(2)}, u32[]{:S(2)}) collective-permute-start(bf16[640,256]{1,0:T(8,128)(2,1)S(1)} %collective-permute-done.3.refs_1_), channel_id=1, source_target_pairs={{0,1},{1,0},{2,3},{3,2},{4,5},{5,4},{6,7},{7,6},{8,9},{9,8},{10,11... | collective-permute-start | bytes 983048 | tf_op jit(solution)/shard_map/ppermute | solution.py:63
  32.9 2.4 %collective-permute-start.8 = (bf16[768,256]{1,0:T(8,128)(2,1)S(1)}, bf16[768,256]{1,0:T(8,128)(2,1)S(1)}, u32[]{:S(2)}, u32[]{:S(2)}) collective-permute-start(bf16[768,256]{1,0:T(8,128)(2,1)S(1)} %get-tuple-element.39), channel_id=1, source_target_pairs={{0,1},{1,0},{2,3},{3,2},{4,5},{5,4},{6,7},{7,6},{8,9},{9,8},{10,11... | collective-permute-start | bytes 1179656 | tf_op jit(solution)/shard_map/ppermute | solution.py:63
  33.5 3.3 %collective-permute-start.9 = (bf16[256,256]{1,0:T(8,128)(2,1)S(1)}, bf16[256,256]{1,0:T(8,128)(2,1)S(1)}, u32[]{:S(2)}, u32[]{:S(2)}) collective-permute-start(bf16[256,256]{1,0:T(8,128)(2,1)S(1)} %get-tuple-element.41), channel_id=1, source_target_pairs={{0,1},{1,0},{2,3},{3,2},{4,5},{5,4},{6,7},{7,6},{8,9},{9,8},{10,11... | collective-permute-start | bytes 393224 | tf_op jit(solution)/shard_map/ppermute | solution.py:63
  33.6 3.8 %collective-permute-start.11 = (bf16[256,256]{1,0:T(8,128)(2,1)S(1)}, bf16[256,256]{1,0:T(8,128)(2,1)S(1)}, u32[]{:S(2)}, u32[]{:S(2)}) collective-permute-start(bf16[256,256]{1,0:T(8,128)(2,1)S(1)} %get-tuple-element.47), channel_id=1, source_target_pairs={{0,1},{1,0},{2,3},{3,2},{4,5},{5,4},{6,7},{7,6},{8,9},{9,8},{10,11... | collective-permute-start | bytes 393224 | tf_op jit(solution)/shard_map/ppermute | solution.py:63
  35.2 1.6 %collective-permute-start.10 = (f32[256,256]{1,0:T(8,128)S(1)}, f32[256,256]{1,0:T(8,128)S(1)}, u32[]{:S(2)}, u32[]{:S(2)}) collective-permute-start(f32[256,256]{1,0:T(8,128)S(1)} %get-tuple-element.45), channel_id=1, source_target_pairs={{0,1},{1,0},{2,3},{3,2},{4,5},{5,4},{6,7},{7,6},{8,9},{9,8},{10,11... | collective-permute-start | bytes 786440 | tf_op jit(solution)/shard_map/ppermute | solution.py:63
  35.4 12.6 %collective-permute-start.15 = (bf16[768,256]{1,0:T(8,128)(2,1)S(1)}, bf16[768,256]{1,0:T(8,128)(2,1)S(1)}, u32[]{:S(2)}, u32[]{:S(2)}) collective-permute-start(bf16[768,256]{1,0:T(8,128)(2,1)S(1)} %add_convert_fusion.1), channel_id=1, source_target_pairs={{4,0},{5,1},{8,4},{9,5},{12,8},{13,9},{2,6},{3,7},{6,10},{7,11},{1... | collective-permute-start | bytes 1179656 | tf_op jit(solution)/shard_map/ppermute | solution.py:77
  36.9 9.2 %collective-permute-start.13 = (bf16[512,256]{1,0:T(8,128)(2,1)S(1)}, bf16[512,256]{1,0:T(8,128)(2,1)S(1)}, u32[]{:S(2)}, u32[]{:S(2)}) collective-permute-start(bf16[512,256]{1,0:T(8,128)(2,1)S(1)} %pack.1.packed_ref), channel_id=1, source_target_pairs={{0,2},{1,3},{2,0},{3,1},{4,6},{5,7},{6,4},{7,5},{8,10},{9,11},{10,... | collective-permute-start | bytes 786440 | tf_op jit(solution)/shard_map/ppermute | solution.py:67
  37.5 10.6 %collective-permute-start.14 = (bf16[256,256]{1,0:T(8,128)(2,1)S(1)}, bf16[256,256]{1,0:T(8,128)(2,1)S(1)}, u32[]{:S(2)}, u32[]{:S(2)}) collective-permute-start(bf16[256,256]{1,0:T(8,128)(2,1)S(1)} %add_convert_fusion.3), channel_id=1, source_target_pairs={{0,2},{1,3},{2,0},{3,1},{4,6},{5,7},{6,4},{7,5},{8,10},{9,11},{10,... | collective-permute-start | bytes 393224 | tf_op jit(solution)/shard_map/ppermute | solution.py:67
  41.8 6.3 %collective-permute-start.16 = (bf16[768,256]{1,0:T(8,128)(2,1)S(1)}, bf16[768,256]{1,0:T(8,128)(2,1)S(1)}, u32[]{:S(2)}, u32[]{:S(2)}) collective-permute-start(bf16[768,256]{1,0:T(8,128)(2,1)S(1)} %spread_side_x_low.1), channel_id=1, source_target_pairs={{0,1},{1,0},{2,3},{3,2},{4,5},{5,4},{6,7},{7,6},{8,9},{9,8},{10,11... | collective-permute-start | bytes 1179656 | tf_op jit(solution)/shard_map/ppermute | solution.py:63
  41.9 16.8 %collective-permute-start.12 = (bf16[1024,256]{1,0:T(8,128)(2,1)S(1)}, bf16[1024,256]{1,0:T(8,128)(2,1)S(1)}, u32[]{:S(2)}, u32[]{:S(2)}) collective-permute-start(bf16[1024,256]{1,0:T(8,128)(2,1)S(1)} %spread_own_x.1), channel_id=1, source_target_pairs={{0,1},{1,0},{2,3},{3,2},{4,5},{5,4},{6,7},{7,6},{8,9},{9,8},{10,11... | collective-permute-start | bytes 1572872 | tf_op jit(solution)/shard_map/ppermute | solution.py:63
  46.1 5.0 %collective-permute-start.19 = (bf16[256,256]{1,0:T(8,128)(2,1)S(1)}, bf16[256,256]{1,0:T(8,128)(2,1)S(1)}, u32[]{:S(2)}, u32[]{:S(2)}) collective-permute-start(bf16[256,256]{1,0:T(8,128)(2,1)S(1)} %get-tuple-element.53), channel_id=1, source_target_pairs={{0,4},{1,5},{2,6},{3,7},{4,0},{5,1},{6,2},{7,3},{8,12},{9,13},{10,... | collective-permute-start | bytes 393224 | tf_op jit(solution)/shard_map/ppermute | solution.py:418
  48.2 10.5 %collective-permute-start.17 = (bf16[768,256]{1,0:T(8,128)(2,1)S(1)}, bf16[768,256]{1,0:T(8,128)(2,1)S(1)}, u32[]{:S(2)}, u32[]{:S(2)}) collective-permute-start(bf16[768,256]{1,0:T(8,128)(2,1)S(1)} %add_convert_fusion), channel_id=1, source_target_pairs={{0,2},{1,3},{2,0},{3,1},{4,6},{5,7},{6,4},{7,5},{8,10},{9,11},{10,... | collective-permute-start | bytes 1179656 | tf_op jit(solution)/shard_map/ppermute | solution.py:67
  51.2 7.3 %collective-permute-start.20 = (bf16[256,256]{1,0:T(8,128)(2,1)S(1)}, bf16[256,256]{1,0:T(8,128)(2,1)S(1)}, u32[]{:S(2)}, u32[]{:S(2)}) collective-permute-start(bf16[256,256]{1,0:T(8,128)(2,1)S(1)} %add_convert_fusion.2), channel_id=1, source_target_pairs={{0,8},{1,9},{2,10},{3,11},{4,12},{5,13},{6,14},{7,15},{8,0},{9,1},... | collective-permute-start | bytes 393224 | tf_op jit(solution)/shard_map/ppermute | solution.py:346
  51.8 6.9 %collective-permute-start.18 = (bf16[256,256]{1,0:T(8,128)(2,1)S(1)}, bf16[256,256]{1,0:T(8,128)(2,1)S(1)}, u32[]{:S(2)}, u32[]{:S(2)}) collective-permute-start(bf16[256,256]{1,0:T(8,128)(2,1)S(1)} %get-tuple-element.52), channel_id=1, source_target_pairs={{0,4},{1,5},{4,8},{5,9},{8,12},{9,13},{6,2},{7,3},{10,6},{11,7},{1... | collective-permute-start | bytes 393224 | tf_op jit(solution)/shard_map/ppermute | solution.py:77
  58.6 1.6 %collective-permute-start.21 = (f32[256,256]{1,0:T(8,128)S(1)}, f32[256,256]{1,0:T(8,128)S(1)}, u32[]{:S(2)}, u32[]{:S(2)}) collective-permute-start(f32[256,256]{1,0:T(8,128)S(1)} %convert_add_fusion.kept_ref), channel_id=1, source_target_pairs={{0,1},{1,0},{2,3},{3,2},{4,5},{5,4},{6,7},{7,6},{8,9},{9,8},{10,11... | collective-permute-start | bytes 786440 | tf_op jit(solution)/shard_map/ppermute | solution.py:63

commit v6 on v5

--- a/solution.py
+++ b/solution.py
@@ -90,6 +90,7 @@
     stripe = lax.axis_index("row")
     core, side = stripe & 1, (stripe >> 1) & 1
     first = (stripe >> 1) * (2 * blocks)
+    near = jnp.where(side == 0, 2, 0)
 
     def clear(i, carry):
         for part in range(PARTS):
@@ -98,11 +99,9 @@
 
     def placed(slot):
         away = cols_ref[slot] - first + 2 * blocks
-        chip = away // (2 * blocks)
-        within = away - chip * (2 * blocks)
-        other = within // blocks
-        column = within - other * blocks
-        near = jnp.where(side == 0, 2, 0)
+        stripe_at = lax.div(away, blocks) if blocks & (blocks - 1) else away >> (blocks.bit_length() - 1)
+        column = away - stripe_at * blocks
+        chip, other = stripe_at >> 1, stripe_at & 1
         part = jnp.where(chip == 1, OWN, jnp.where(chip == near, SIDE, PLANE)) + (other ^ core)
         target = a_ref.at[
             part,
@@ -115,15 +114,21 @@
         placed(slot).start()
         return carry
 
+    def start_four(group, carry):
+        for i in range(4):
+            placed(4 * group + i).start()
+        return carry
+
     def finish(slot, carry):
-        placed(slot).wait()
+        pltpu.make_async_copy(tiles_ref.at[0], a_ref.at[0, pl.ds(0, block), pl.ds(0, block)], sem).wait()
         return carry
 
     lax.fori_loop(0, width // 64, clear, 0)
     for fetch in fetches:
         fetch.wait()
     live = count_ref[0]
-    lax.fori_loop(0, live, start, 0)
+    lax.fori_loop(0, live >> 2, start_four, 0)
+    lax.fori_loop((live >> 2) * 4, live, start, 0)
     lax.fori_loop(0, live, finish, 0)
 
 
@@ -251,7 +256,7 @@
         ],
         in_specs=[vmem_spec()] * len(args),
         out_specs=[hbm_spec()] + [vmem_spec()] * (3 + len(shares)),
-        scratch_shapes=[wide, pltpu.SemaphoreType.DMA((4,))],
+        scratch_shapes=[wide, pltpu.SemaphoreType.DMA((2,))],
         compiler_params=pltpu.CompilerParams(vmem_limit_bytes=LIMIT),
         cost_estimate=SHORT,
         name="middle",
@@ -370,7 +375,7 @@
     total = gathered(dense, [(SIDE, *first), (SIDE_X, *first)], [side_low, side_x_low], total, "gather_side")
     plane_low = after(plane_low, total)
     plane_x_low = flip_core(plane_low, count)
-    highs_x = flip_core(highs, count)
+    highs_x = flip_core(after(highs, total), count)
     total = gathered(dense, [(SIDE, *rest), (PLANE, split, rows, rows - split)], [highs, highs], total, "gather_high")
     total = gathered(
         dense,
@@ -403,15 +408,17 @@
         unpack_kernel, "unpack", [((high, width), BF16), (wide, BF16)], [packed, flip_side(packed, count)]
     )
 
-    (s_high,) = spread(dense, after(ht, packed), SIDE, back[1:], F32, "spread_side_high")
+    ht = after(ht, packed)
+    (ox,) = spread(dense, ht, OWN_X, [(0, rows)], BF16, "spread_own_x")
+    own = kernel_call(own_kernel, "spread_own", [((rows, width), F32)], [dense, ht, grad_pre, root_weight])[0]
+    ht = after(ht, own, ox)
+    (s_high,) = spread(dense, ht, SIDE, back[1:], F32, "spread_side_high")
     s_high = added(s_high, flip_core(sx_high, count))
     near_high = flip_side(s_high, count)
     ht = after(ht, s_high)
     (sx_low,) = spread(dense, ht, SIDE_X, back[:1], BF16, "spread_side_x_low")
     sx_low = flip_core(sx_low, count)
     (s_low,) = spread(dense, after(ht, mine), SIDE, back[:1], F32, "spread_side_low")
-    (ox,) = spread(dense, ht, OWN_X, [(0, rows)], BF16, "spread_own_x")
-    own = kernel_call(own_kernel, "spread_own", [((rows, width), F32)], [dense, ht, grad_pre, root_weight])[0]
     through = added(relayed(after(s_low, own, ox, near_high), far), sx_low)
     near_low = flip_side(through, count)
     direct = over_planes(passing, count, False, None)

time: 61.5 us -> 60.2 us (0.979)
  Pallas kernels: 19.9 us -> 17.5 us
  starting transfers between devices: 18 us -> 19.8 us
    pallas_call x1, Pallas kernels: 5.82 us -> 3.8 us  [dense_adjacency(): pl.pallas_call(dense_kernel, out_shape=pltpu.VMEM((PARTS, width, width),...]
    ppermute x4, starting transfers between devices: 8.07 us -> 9.77 us  [over_planes(): lax.ppermute(array, 'row', [(b, a) for a, b in step] if back else step)]
    ppermute x4, waiting for transfers between devices: 1.1 us -> 2.76 us  [over_planes(): lax.ppermute(array, 'row', [(b, a) for a, b in step] if back else step)]
    ppermute x5, waiting for transfers between devices: 13.1 us -> 11.5 us  [flip_side(): return lax.ppermute(array, 'row', [(i, i ^ 2) for i in range(count)])]
    ppermute x1, starting transfers between devices: 1.13 us -> 0.36 us  [body(): lax.ppermute(after(mine, own), 'row', [(i, i ^ 4) for i in range(count)])]
  transfers between devices with their start and end apart: 22 -> 22, of which waited for: 7 -> 8; matrix products, arithmetic and copies ran while one was open for 0% -> 0% of each run, Pallas kernels for 25% -> 22%
where the time goes in v6:
time: 60.2 us; the launch traced here: 59.9 us
  waiting for transfers between devices  20.7 us (34%)
  starting transfers between devices  19.8 us (33%)
  Pallas kernels  17.5 us (29%)
  between operations  1.64 us (3%)
    ppermute x5, waiting for transfers between devices, flip_side(): return lax.ppermute(array, 'row', [(i, i ^ 2) for i in range(count)])  11.5 us
    ppermute x4, starting transfers between devices, over_planes(): lax.ppermute(array, 'row', [(b, a) for a, b in step] if back else step)  9.77 us
    pallas_call x17, Pallas kernels, kernel_call(): pl.pallas_call(kernel, out_shape=[pltpu.VMEM(shape, dtype) for shape, dty...  9.36 us
    ppermute x5, starting transfers between devices, flip_side(): return lax.ppermute(array, 'row', [(i, i ^ 2) for i in range(count)])  6.17 us
    pallas_call x1, Pallas kernels, dense_adjacency(): pl.pallas_call(dense_kernel, out_shape=pltpu.VMEM((PARTS, width, width),...  3.8 us
    ppermute x1, waiting for transfers between devices, exchanged(): lax.ppermute(mine, 'row', [(i, i ^ hop) for i in range(count)])  3.15 us
    ppermute x4, waiting for transfers between devices, over_planes(): lax.ppermute(array, 'row', [(b, a) for a, b in step] if back else step)  2.76 us
    ppermute x11, starting transfers between devices, flip_core(): return lax.ppermute(array, 'row', [(i, i ^ 1) for i in range(count)])  2.4 us
  transfers between devices with their start and end apart: 22, of which 8 were waited for; matrix products, arithmetic and copies ran while one was open for 0% of the time, Pallas kernels for 22%

profile of v6, /device:TPU:0, one launch (start us, length us, event | category | flops | bytes accessed | tf_op | source)
XLA Modules:
  0.0 59.9 jit_solution(11882430954194928414)
XLA Ops:
  0.6 0.0 copy-start
  0.6 1.2 %cut.1 = (bf16[640,256]{1,0:T(8,128)(2,1)S(1)}, bf16[384,256]{1,0:T(8,128)(2,1)S(1)}) custom-call(bf16[1024,256]{1,0:T(8,128)(2,1)} %x_ref.3), custom_call_target="tpu_custom_call" | custom-call | tf_op jit(solution)/shard_map/cut/pallas_call | solution.py:197
  1.8 0.5 collective-permute-start.2
  2.4 2.6 %collective-permute-start = (bf16[640,256]{1,0:T(8,128)(2,1)S(1)}, bf16[640,256]{1,0:T(8,128)(2,1)S(1)}, u32[]{:S(2)}, u32[]{:S(2)}) collective-permute-start(bf16[640,256]{1,0:T(8,128)(2,1)S(1)} %get-tuple-element.33), channel_id=1, source_target_pairs={{0,2},{1,3},{2,0},{3,1},{4,6},{5,7},{6,4},{7,5},{8,10},{9,11},{10,... | collective-permute-start | bytes 983048 | tf_op jit(solution)/shard_map/ppermute | solution.py:67
  5.0 3.6 %collective-permute-start.1 = (bf16[384,256]{1,0:T(8,128)(2,1)S(1)}, bf16[384,256]{1,0:T(8,128)(2,1)S(1)}, u32[]{:S(2)}, u32[]{:S(2)}) collective-permute-start(bf16[384,256]{1,0:T(8,128)(2,1)S(1)} %get-tuple-element.34.a_ref), channel_id=1, source_target_pairs={{4,0},{5,1},{8,4},{9,5},{12,8},{13,9},{2,6},{3,7},{6,10},{7,11},{1... | collective-permute-start | bytes 589832 | tf_op jit(solution)/shard_map/ppermute | solution.py:77
  9.2 3.8 %dense_adjacency.1.refs_0_.a_ref = bf16[6,1024,1024]{2,1,0:T(8,128)(2,1)S(1)} custom-call(s32[1]{0:T(128)S(6)} %copy.12.count_ref, s32[192]{0:T(256)} %rows_hbm.1, s32[192]{0:T(256)} %cols_hbm.1, bf16[192,128,128]{2,1,0:T(8,128)(2,1)} %tiles_ref.1), custom_call_target="tpu_custom_call" | custom-call | tf_op jit(solution)/shard_map/dense_adjacency/pallas_call | solution.py:137
  13.0 0.0 collective-permute-done.2.refs_2_
  13.0 1.3 %gather_own.1.refs_3_ = f32[1024,256]{1,0:T(8,128)S(1)} custom-call(bf16[6,1024,1024]{2,1,0:T(8,128)(2,1)S(1)} %dense_adjacency.1.refs_0_.a_ref, bf16[1024,256]{1,0:T(8,128)(2,1)S(1)} %copy-done, bf16[1024,256]{1,0:T(8,128)(2,1)S(1)} %collective-permute-done.2.refs_2_), custom_call_target="tpu_custom_call" | custom-call | tf_op jit(solution)/shard_map/gather_own/pallas_call | solution.py:51
  14.3 0.0 collective-permute-done.1.b_ref
  14.3 0.0 collective-permute-done.refs_1_
  14.4 0.8 %collective-permute-start.5 = (bf16[768,256]{1,0:T(8,128)(2,1)S(1)}, bf16[768,256]{1,0:T(8,128)(2,1)S(1)}, u32[]{:S(2)}, u32[]{:S(2)}) collective-permute-start(bf16[768,256]{1,0:T(8,128)(2,1)S(1)} %join.1), channel_id=1, source_target_pairs={{0,2},{1,3},{2,0},{3,1},{4,6},{5,7},{6,4},{7,5},{8,10},{9,11},{10,... | collective-permute-start | bytes 1179656 | tf_op jit(solution)/shard_map/ppermute | solution.py:67
  15.1 0.0 collective-permute-start.4
  15.1 1.6 %collective-permute-start.3 = (bf16[640,256]{1,0:T(8,128)(2,1)S(1)}, bf16[640,256]{1,0:T(8,128)(2,1)S(1)}, u32[]{:S(2)}, u32[]{:S(2)}) collective-permute-start(bf16[640,256]{1,0:T(8,128)(2,1)S(1)} %collective-permute-done.refs_1_), channel_id=1, source_target_pairs={{0,4},{1,5},{4,8},{5,9},{8,12},{9,13},{6,2},{7,3},{10,6},{11,7},{1... | collective-permute-start | bytes 983048 | tf_op jit(solution)/shard_map/ppermute | solution.py:77
  16.7 0.0 collective-permute-done.4.refs_2_
  16.7 1.0 %gather_side.1.refs_3_ = f32[1024,256]{1,0:T(8,128)S(1)} custom-call(bf16[6,1024,1024]{2,1,0:T(8,128)(2,1)S(1)} %dense_adjacency.1.refs_0_.a_ref, bf16[640,256]{1,0:T(8,128)(2,1)S(1)} %collective-permute-done.refs_1_, bf16[640,256]{1,0:T(8,128)(2,1)S(1)} %collective-permute-done.4.refs_2_, f32[1024,256]{1,0:T(8,128)S(1)} %gather_own.1.refs_3_), custom_call_target="tpu_custom_call" | custom-call | tf_op jit(solution)/shard_map/gather_side/pallas_call | solution.py:51
  17.7 0.0 copy-start.1
  17.7 0.0 copy-start.2
  17.7 0.0 copy-start.3
  17.7 6.6 %collective-permute-done.5.refs_1_.refs_2_ = bf16[768,256]{1,0:T(8,128)(2,1)S(1)} collective-permute-done((bf16[768,256]{1,0:T(8,128)(2,1)S(1)}, bf16[768,256]{1,0:T(8,128)(2,1)S(1)}, u32[]{:S(2)}, u32[]{:S(2)}) %collective-permute-start.5) | collective-permute-done | bytes 393248 | tf_op jit(solution)/shard_map/ppermute | solution.py:67
  24.3 2.8 %collective-permute-done.3.refs_1_ = bf16[640,256]{1,0:T(8,128)(2,1)S(1)} collective-permute-done((bf16[640,256]{1,0:T(8,128)(2,1)S(1)}, bf16[640,256]{1,0:T(8,128)(2,1)S(1)}, u32[]{:S(2)}, u32[]{:S(2)}) %collective-permute-start.3) | collective-permute-done | bytes 327712 | tf_op jit(solution)/shard_map/ppermute | solution.py:77
  27.1 0.0 collective-permute-start.7
  27.1 0.7 %gather_high.1.refs_4_ = f32[1024,256]{1,0:T(8,128)S(1)} custom-call(bf16[6,1024,1024]{2,1,0:T(8,128)(2,1)S(1)} %dense_adjacency.1.refs_0_.a_ref, bf16[768,256]{1,0:T(8,128)(2,1)S(1)} %collective-permute-done.5.refs_1_.refs_2_, bf16[768,256]{1,0:T(8,128)(2,1)S(1)} %collective-permute-done.5.refs_1_.refs_2_, f32[1024,256]{1,0:T(8,128)S(1)} %gather_side.1.refs_3_), custom_call_target="tpu_custom_call" | custom-call | tf_op jit(solution)/shard_map/gather_high/pallas_call | solution.py:51
  27.8 0.0 collective-permute-done.6.refs_2_.refs_3_
  27.8 1.1 %gather_high_x.1.total_ref = f32[1024,256]{1,0:T(8,128)S(1)} custom-call(bf16[6,1024,1024]{2,1,0:T(8,128)(2,1)S(1)} %dense_adjacency.1.refs_0_.a_ref, bf16[640,256]{1,0:T(8,128)(2,1)S(1)} %collective-permute-done.3.refs_1_, bf16[768,256]{1,0:T(8,128)(2,1)S(1)} %collective-permute-done.6.refs_2_.refs_3_, ...), custom_call_target="tpu_custom_call" | custom-call | flops 500000000 | tf_op jit(solution)/shard_map/gather_high_x/pallas_call | solution.py:51
  28.9 0.0 collective-permute-done.7.refs_0_
  29.0 2.2 %middle.1 = (bf16[1024,256]{1,0:T(8,128)(2,1)}, bf16[1024,256]{1,0:T(8,128)(2,1)S(1)}, bf16[1024,256]{1,0:T(8,128)(2,1)S(1)}, bf16[256,1024]{1,0:T(8,128)(2,1)S(...) custom-call(bf16[6,1024,1024]{2,1,0:T(8,128)(2,1)S(1)} %dense_adjacency.1.refs_0_.a_ref, ...), custom_call_target="tpu_custom_call" | custom-call | tf_op jit(solution)/shard_map/middle/pallas_call | solution.py:251
  31.1 0.6 collective-permute-start.8
  31.7 0.1 collective-permute-start.9
  31.8 0.4 collective-permute-start.12
  32.2 0.7 %spread_plane_low.1 = bf16[768,256]{1,0:T(8,128)(2,1)S(1)} custom-call(bf16[6,1024,1024]{2,1,0:T(8,128)(2,1)S(1)} %dense_adjacency.1.refs_0_.a_ref, bf16[256,1024]{1,0:T(8,128)(2,1)S(1)} %get-tuple-element.54.ht_ref), custom_call_target="tpu_custom_call" | custom-call | tf_op jit(solution)/shard_map/spread_plane_low/pallas_call | solution.py:51
  32.9 0.5 weight_products.1
  33.4 0.1 collective-permute-start.10
  33.5 0.1 add_convert_fusion.1
  33.6 1.8 %collective-permute-start.15 = (bf16[768,256]{1,0:T(8,128)(2,1)S(1)}, bf16[768,256]{1,0:T(8,128)(2,1)S(1)}, u32[]{:S(2)}, u32[]{:S(2)}) collective-permute-start(bf16[768,256]{1,0:T(8,128)(2,1)S(1)} %add_convert_fusion.1), channel_id=1, source_target_pairs={{4,0},{5,1},{8,4},{9,5},{12,8},{13,9},{2,6},{3,7},{6,10},{7,11},{1... | collective-permute-start | bytes 1179656 | tf_op jit(solution)/shard_map/ppermute | solution.py:77
  35.4 0.4 spread_plane_high.1.share_ref
  35.8 0.0 collective-permute-done.10.arrived_ref
  35.8 0.1 pack.1.packed_ref
  35.9 0.1 collective-permute-start.13
  36.0 0.9 %spread_own.1.own_ref = f32[1024,256]{1,0:T(8,128)S(1)} custom-call(bf16[6,1024,1024]{2,1,0:T(8,128)(2,1)S(1)} %dense_adjacency.1.refs_0_.a_ref, bf16[256,1024]{1,0:T(8,128)(2,1)S(1)} %get-tuple-element.54.ht_ref, bf16[1024,256]{1,0:T(8,128)(2,1)S(1)} %get-tuple-element.46.grad_ref, bf16[256,256]{1,0:T(8,128)(2,1)S(1)} %copy-done.1), custom_call_target="tpu_custom_call" | custom-call | tf_op jit(solution)/shard_map/spread_own/pallas_call | solution.py:51
  36.9 0.8 %spread_own_x.1 = bf16[1024,256]{1,0:T(8,128)(2,1)S(1)} custom-call(bf16[6,1024,1024]{2,1,0:T(8,128)(2,1)S(1)} %dense_adjacency.1.refs_0_.a_ref, bf16[256,1024]{1,0:T(8,128)(2,1)S(1)} %get-tuple-element.54.ht_ref), custom_call_target="tpu_custom_call" | custom-call | tf_op jit(solution)/shard_map/spread_own_x/pallas_call | solution.py:51
  37.7 0.4 spread_side_high.1
  38.1 0.0 collective-permute-done.12
  38.1 2.1 %collective-permute-start.14 = (bf16[256,256]{1,0:T(8,128)(2,1)S(1)}, bf16[256,256]{1,0:T(8,128)(2,1)S(1)}, u32[]{:S(2)}, u32[]{:S(2)}) collective-permute-start(bf16[256,256]{1,0:T(8,128)(2,1)S(1)} %add_convert_fusion.3), channel_id=1, source_target_pairs={{0,2},{1,3},{2,0},{3,1},{4,6},{5,7},{6,4},{7,5},{8,10},{9,11},{10,... | collective-permute-start | bytes 393224 | tf_op jit(solution)/shard_map/ppermute | solution.py:67
  40.2 0.7 %spread_side_x_low.1 = bf16[768,256]{1,0:T(8,128)(2,1)S(1)} custom-call(bf16[6,1024,1024]{2,1,0:T(8,128)(2,1)S(1)} %dense_adjacency.1.refs_0_.a_ref, bf16[256,1024]{1,0:T(8,128)(2,1)S(1)} %get-tuple-element.54.ht_ref), custom_call_target="tpu_custom_call" | custom-call | tf_op jit(solution)/shard_map/spread_side_x_low/pallas_call | solution.py:51
  40.8 0.6 collective-permute-start.16
  41.4 3.7 %collective-permute-done.13.arrived_ref = bf16[512,256]{1,0:T(8,128)(2,1)S(1)} collective-permute-done((bf16[512,256]{1,0:T(8,128)(2,1)S(1)}, bf16[512,256]{1,0:T(8,128)(2,1)S(1)}, u32[]{:S(2)}, u32[]{:S(2)}) %collective-permute-start.13) | collective-permute-done | bytes 262176 | tf_op jit(solution)/shard_map/ppermute | solution.py:67
  45.1 0.4 collective-permute-start.19
  45.5 0.7 %spread_side_low.1.own_ref = f32[768,256]{1,0:T(8,128)S(1)} custom-call(bf16[6,1024,1024]{2,1,0:T(8,128)(2,1)S(1)} %dense_adjacency.1.refs_0_.a_ref, bf16[256,1024]{1,0:T(8,128)(2,1)S(1)} %get-tuple-element.54.ht_ref), custom_call_target="tpu_custom_call" | custom-call | tf_op jit(solution)/shard_map/spread_side_low/pallas_call | solution.py:51
  46.2 0.9 %collective-permute-done.14.high_ref = bf16[256,256]{1,0:T(8,128)(2,1)S(1)} collective-permute-done((bf16[256,256]{1,0:T(8,128)(2,1)S(1)}, bf16[256,256]{1,0:T(8,128)(2,1)S(1)}, u32[]{:S(2)}, u32[]{:S(2)}) %collective-permute-start.14) | collective-permute-done | bytes 131104 | tf_op jit(solution)/shard_map/ppermute | solution.py:67
  47.1 0.1 relay.1
  47.2 0.0 collective-permute-done.16
  47.2 0.1 add_convert_fusion
  47.3 0.7 %collective-permute-start.17 = (bf16[768,256]{1,0:T(8,128)(2,1)S(1)}, bf16[768,256]{1,0:T(8,128)(2,1)S(1)}, u32[]{:S(2)}, u32[]{:S(2)}) collective-permute-start(bf16[768,256]{1,0:T(8,128)(2,1)S(1)} %add_convert_fusion), channel_id=1, source_target_pairs={{0,2},{1,3},{2,0},{3,1},{4,6},{5,7},{6,4},{7,5},{8,10},{9,11},{10,... | collective-permute-start | bytes 1179656 | tf_op jit(solution)/shard_map/ppermute | solution.py:67
  48.0 2.2 %collective-permute-done.19 = bf16[256,256]{1,0:T(8,128)(2,1)S(1)} collective-permute-done((bf16[256,256]{1,0:T(8,128)(2,1)S(1)}, bf16[256,256]{1,0:T(8,128)(2,1)S(1)}, u32[]{:S(2)}, u32[]{:S(2)}) %collective-permute-start.19) | collective-permute-done | bytes 131104 | tf_op jit(solution)/shard_map/ppermute | solution.py:425
  50.2 1.1 %collective-permute-start.20 = (bf16[256,256]{1,0:T(8,128)(2,1)S(1)}, bf16[256,256]{1,0:T(8,128)(2,1)S(1)}, u32[]{:S(2)}, u32[]{:S(2)}) collective-permute-start(bf16[256,256]{1,0:T(8,128)(2,1)S(1)} %add_convert_fusion.2), channel_id=1, source_target_pairs={{0,8},{1,9},{2,10},{3,11},{4,12},{5,13},{6,14},{7,15},{8,0},{9,1},... | collective-permute-start | bytes 393224 | tf_op jit(solution)/shard_map/ppermute | solution.py:351
  51.3 2.8 %collective-permute-start.18 = (bf16[256,256]{1,0:T(8,128)(2,1)S(1)}, bf16[256,256]{1,0:T(8,128)(2,1)S(1)}, u32[]{:S(2)}, u32[]{:S(2)}) collective-permute-start(bf16[256,256]{1,0:T(8,128)(2,1)S(1)} %get-tuple-element.56), channel_id=1, source_target_pairs={{0,4},{1,5},{4,8},{5,9},{8,12},{9,13},{6,2},{7,3},{10,6},{11,7},{1... | collective-permute-start | bytes 393224 | tf_op jit(solution)/shard_map/ppermute | solution.py:77
  54.1 3.2 %collective-permute-done.20 = bf16[256,256]{1,0:T(8,128)(2,1)S(1)} collective-permute-done((bf16[256,256]{1,0:T(8,128)(2,1)S(1)}, bf16[256,256]{1,0:T(8,128)(2,1)S(1)}, u32[]{:S(2)}, u32[]{:S(2)}) %collective-permute-start.20) | collective-permute-done | bytes 131104 | tf_op jit(solution)/shard_map/ppermute | solution.py:351
  57.3 0.1 collective-permute-start.21
  57.4 0.0 collective-permute-done.18.direct_ref
  57.4 0.0 collective-permute-done.11.other_ref
  57.4 0.3 collective-permute-done.17.low_ref
  57.7 0.2 final.1.out_ref
  58.0 1.0 %collective-permute-done.21.other_ref = f32[256,256]{1,0:T(8,128)S(1)} collective-permute-done((f32[256,256]{1,0:T(8,128)S(1)}, f32[256,256]{1,0:T(8,128)S(1)}, u32[]{:S(2)}, u32[]{:S(2)}) %collective-permute-start.21) | collective-permute-done | bytes 262176 | tf_op jit(solution)/shard_map/ppermute | solution.py:63
  58.9 1.0 %scaled.1 = (bf16[1024,256]{1,0:T(8,128)(2,1)}, f32[256,256]{1,0:T(8,128)}, f32[256,256]{1,0:T(8,128)}) custom-call(bf16[1024,256]{1,0:T(8,128)(2,1)S(1)} %final.1.out_ref, f32[256,256]{1,0:T(8,128)S(1)} %convert_add_fusion.kept_ref, f32[256,256]{1,0:T(8,128)S(1)} %collective-permute-done.21.other_ref), custom_call_target="tpu_custom_call" | custom-call | tf_op jit(solution)/shard_map/scaled/pallas_call | solution.py:321
  (14 shorter events, 0.2 us)
Async XLA Ops:
  0.6 12.4 %copy-start = (bf16[1024,256]{1,0:T(8,128)(2,1)S(1)}, bf16[1024,256]{1,0:T(8,128)(2,1)}, u32[]{:S(2)}) copy-start(bf16[1024,256]{1,0:T(8,128)(2,1)} %x_ref.3) | copy-start | bytes 1572868
  1.8 11.2 %collective-permute-start.2 = (bf16[1024,256]{1,0:T(8,128)(2,1)}, bf16[1024,256]{1,0:T(8,128)(2,1)S(1)}, u32[]{:S(2)}, u32[]{:S(2)}) collective-permute-start(bf16[1024,256]{1,0:T(8,128)(2,1)} %x_ref.3), channel_id=1, source_target_pairs={{0,1},{1,0},{2,3},{3,2},{4,5},{5,4},{6,7},{7,6},{8,9},{9,8},{10,11... | collective-permute-start | bytes 1572872 | tf_op jit(solution)/shard_map/ppermute | solution.py:63
  2.4 12.0 %collective-permute-start = (bf16[640,256]{1,0:T(8,128)(2,1)S(1)}, bf16[640,256]{1,0:T(8,128)(2,1)S(1)}, u32[]{:S(2)}, u32[]{:S(2)}) collective-permute-start(bf16[640,256]{1,0:T(8,128)(2,1)S(1)} %get-tuple-element.33), channel_id=1, source_target_pairs={{0,2},{1,3},{2,0},{3,1},{4,6},{5,7},{6,4},{7,5},{8,10},{9,11},{10,... | collective-permute-start | bytes 983048 | tf_op jit(solution)/shard_map/ppermute | solution.py:67
  5.0 9.3 %collective-permute-start.1 = (bf16[384,256]{1,0:T(8,128)(2,1)S(1)}, bf16[384,256]{1,0:T(8,128)(2,1)S(1)}, u32[]{:S(2)}, u32[]{:S(2)}) collective-permute-start(bf16[384,256]{1,0:T(8,128)(2,1)S(1)} %get-tuple-element.34.a_ref), channel_id=1, source_target_pairs={{4,0},{5,1},{8,4},{9,5},{12,8},{13,9},{2,6},{3,7},{6,10},{7,11},{1... | collective-permute-start | bytes 589832 | tf_op jit(solution)/shard_map/ppermute | solution.py:77
  14.4 10.0 %collective-permute-start.5 = (bf16[768,256]{1,0:T(8,128)(2,1)S(1)}, bf16[768,256]{1,0:T(8,128)(2,1)S(1)}, u32[]{:S(2)}, u32[]{:S(2)}) collective-permute-start(bf16[768,256]{1,0:T(8,128)(2,1)S(1)} %join.1), channel_id=1, source_target_pairs={{0,2},{1,3},{2,0},{3,1},{4,6},{5,7},{6,4},{7,5},{8,10},{9,11},{10,... | collective-permute-start | bytes 1179656 | tf_op jit(solution)/shard_map/ppermute | solution.py:67
  15.1 1.6 %collective-permute-start.4 = (bf16[640,256]{1,0:T(8,128)(2,1)S(1)}, bf16[640,256]{1,0:T(8,128)(2,1)S(1)}, u32[]{:S(2)}, u32[]{:S(2)}) collective-permute-start(bf16[640,256]{1,0:T(8,128)(2,1)S(1)} %collective-permute-done.refs_1_), channel_id=1, source_target_pairs={{0,1},{1,0},{2,3},{3,2},{4,5},{5,4},{6,7},{7,6},{8,9},{9,8},{10,11... | collective-permute-start | bytes 983048 | tf_op jit(solution)/shard_map/ppermute | solution.py:63
  15.1 12.0 %collective-permute-start.3 = (bf16[640,256]{1,0:T(8,128)(2,1)S(1)}, bf16[640,256]{1,0:T(8,128)(2,1)S(1)}, u32[]{:S(2)}, u32[]{:S(2)}) collective-permute-start(bf16[640,256]{1,0:T(8,128)(2,1)S(1)} %collective-permute-done.refs_1_), channel_id=1, source_target_pairs={{0,4},{1,5},{4,8},{5,9},{8,12},{9,13},{6,2},{7,3},{10,6},{11,7},{1... | collective-permute-start | bytes 983048 | tf_op jit(solution)/shard_map/ppermute | solution.py:77
  17.7 11.2 %copy-start.1 = (bf16[256,256]{1,0:T(8,128)(2,1)S(1)}, bf16[256,256]{1,0:T(8,128)(2,1)}, u32[]{:S(2)}) copy-start(bf16[256,256]{1,0:T(8,128)(2,1)} %r_ref.3) | copy-start | bytes 393220
  17.7 11.2 %copy-start.2 = (bf16[1024,256]{1,0:T(8,128)(2,1)S(1)}, bf16[1024,256]{1,0:T(8,128)(2,1)}, u32[]{:S(2)}) copy-start(bf16[1024,256]{1,0:T(8,128)(2,1)} %cot_ref.1) | copy-start | bytes 1572868
  17.7 11.2 %copy-start.3 = (bf16[256,256]{1,0:T(8,128)(2,1)S(1)}, bf16[256,256]{1,0:T(8,128)(2,1)}, u32[]{:S(2)}) copy-start(bf16[256,256]{1,0:T(8,128)(2,1)} %w_ref.1) | copy-start | bytes 393220
  24.3 3.5 %collective-permute-start.6 = (bf16[768,256]{1,0:T(8,128)(2,1)S(1)}, bf16[768,256]{1,0:T(8,128)(2,1)S(1)}, u32[]{:S(2)}, u32[]{:S(2)}) collective-permute-start(bf16[768,256]{1,0:T(8,128)(2,1)S(1)} %collective-permute-done.5.refs_1_.refs_2_), channel_id=1, source_target_pairs={{0,1},{1,0},{2,3},{3,2},{4,5},{5,4},{6,7},{7,6},{8,9},{9,8},{10,11... | collective-permute-start | bytes 1179656 | tf_op jit(solution)/shard_map/ppermute | solution.py:63
  27.1 1.8 %collective-permute-start.7 = (bf16[640,256]{1,0:T(8,128)(2,1)S(1)}, bf16[640,256]{1,0:T(8,128)(2,1)S(1)}, u32[]{:S(2)}, u32[]{:S(2)}) collective-permute-start(bf16[640,256]{1,0:T(8,128)(2,1)S(1)} %collective-permute-done.3.refs_1_), channel_id=1, source_target_pairs={{0,1},{1,0},{2,3},{3,2},{4,5},{5,4},{6,7},{7,6},{8,9},{9,8},{10,11... | collective-permute-start | bytes 983048 | tf_op jit(solution)/shard_map/ppermute | solution.py:63
  31.1 2.4 %collective-permute-start.8 = (bf16[768,256]{1,0:T(8,128)(2,1)S(1)}, bf16[768,256]{1,0:T(8,128)(2,1)S(1)}, u32[]{:S(2)}, u32[]{:S(2)}) collective-permute-start(bf16[768,256]{1,0:T(8,128)(2,1)S(1)} %get-tuple-element.42), channel_id=1, source_target_pairs={{0,1},{1,0},{2,3},{3,2},{4,5},{5,4},{6,7},{7,6},{8,9},{9,8},{10,11... | collective-permute-start | bytes 1179656 | tf_op jit(solution)/shard_map/ppermute | solution.py:63
  31.7 4.1 %collective-permute-start.9 = (bf16[256,256]{1,0:T(8,128)(2,1)S(1)}, bf16[256,256]{1,0:T(8,128)(2,1)S(1)}, u32[]{:S(2)}, u32[]{:S(2)}) collective-permute-start(bf16[256,256]{1,0:T(8,128)(2,1)S(1)} %get-tuple-element.44), channel_id=1, source_target_pairs={{0,1},{1,0},{2,3},{3,2},{4,5},{5,4},{6,7},{7,6},{8,9},{9,8},{10,11... | collective-permute-start | bytes 393224 | tf_op jit(solution)/shard_map/ppermute | solution.py:63
  31.8 6.3 %collective-permute-start.12 = (bf16[256,256]{1,0:T(8,128)(2,1)S(1)}, bf16[256,256]{1,0:T(8,128)(2,1)S(1)}, u32[]{:S(2)}, u32[]{:S(2)}) collective-permute-start(bf16[256,256]{1,0:T(8,128)(2,1)S(1)} %get-tuple-element.51), channel_id=1, source_target_pairs={{0,1},{1,0},{2,3},{3,2},{4,5},{5,4},{6,7},{7,6},{8,9},{9,8},{10,11... | collective-permute-start | bytes 393224 | tf_op jit(solution)/shard_map/ppermute | solution.py:63
  33.4 2.4 %collective-permute-start.10 = (f32[256,256]{1,0:T(8,128)S(1)}, f32[256,256]{1,0:T(8,128)S(1)}, u32[]{:S(2)}, u32[]{:S(2)}) collective-permute-start(f32[256,256]{1,0:T(8,128)S(1)} %get-tuple-element.48), channel_id=1, source_target_pairs={{0,1},{1,0},{2,3},{3,2},{4,5},{5,4},{6,7},{7,6},{8,9},{9,8},{10,11... | collective-permute-start | bytes 786440 | tf_op jit(solution)/shard_map/ppermute | solution.py:63
  33.6 13.5 %collective-permute-start.15 = (bf16[768,256]{1,0:T(8,128)(2,1)S(1)}, bf16[768,256]{1,0:T(8,128)(2,1)S(1)}, u32[]{:S(2)}, u32[]{:S(2)}) collective-permute-start(bf16[768,256]{1,0:T(8,128)(2,1)S(1)} %add_convert_fusion.1), channel_id=1, source_target_pairs={{4,0},{5,1},{8,4},{9,5},{12,8},{13,9},{2,6},{3,7},{6,10},{7,11},{1... | collective-permute-start | bytes 1179656 | tf_op jit(solution)/shard_map/ppermute | solution.py:77
  35.9 9.2 %collective-permute-start.13 = (bf16[512,256]{1,0:T(8,128)(2,1)S(1)}, bf16[512,256]{1,0:T(8,128)(2,1)S(1)}, u32[]{:S(2)}, u32[]{:S(2)}) collective-permute-start(bf16[512,256]{1,0:T(8,128)(2,1)S(1)} %pack.1.packed_ref), channel_id=1, source_target_pairs={{0,2},{1,3},{2,0},{3,1},{4,6},{5,7},{6,4},{7,5},{8,10},{9,11},{10,... | collective-permute-start | bytes 786440 | tf_op jit(solution)/shard_map/ppermute | solution.py:67
  38.1 9.0 %collective-permute-start.14 = (bf16[256,256]{1,0:T(8,128)(2,1)S(1)}, bf16[256,256]{1,0:T(8,128)(2,1)S(1)}, u32[]{:S(2)}, u32[]{:S(2)}) collective-permute-start(bf16[256,256]{1,0:T(8,128)(2,1)S(1)} %add_convert_fusion.3), channel_id=1, source_target_pairs={{0,2},{1,3},{2,0},{3,1},{4,6},{5,7},{6,4},{7,5},{8,10},{9,11},{10,... | collective-permute-start | bytes 393224 | tf_op jit(solution)/shard_map/ppermute | solution.py:67
  40.2 17.2 %collective-permute-start.11 = (bf16[1024,256]{1,0:T(8,128)(2,1)S(1)}, bf16[1024,256]{1,0:T(8,128)(2,1)S(1)}, u32[]{:S(2)}, u32[]{:S(2)}) collective-permute-start(bf16[1024,256]{1,0:T(8,128)(2,1)S(1)} %spread_own_x.1), channel_id=1, source_target_pairs={{0,1},{1,0},{2,3},{3,2},{4,5},{5,4},{6,7},{7,6},{8,9},{9,8},{10,11... | collective-permute-start | bytes 1572872 | tf_op jit(solution)/shard_map/ppermute | solution.py:63
  40.8 6.4 %collective-permute-start.16 = (bf16[768,256]{1,0:T(8,128)(2,1)S(1)}, bf16[768,256]{1,0:T(8,128)(2,1)S(1)}, u32[]{:S(2)}, u32[]{:S(2)}) collective-permute-start(bf16[768,256]{1,0:T(8,128)(2,1)S(1)} %spread_side_x_low.1), channel_id=1, source_target_pairs={{0,1},{1,0},{2,3},{3,2},{4,5},{5,4},{6,7},{7,6},{8,9},{9,8},{10,11... | collective-permute-start | bytes 1179656 | tf_op jit(solution)/shard_map/ppermute | solution.py:63
  45.1 5.0 %collective-permute-start.19 = (bf16[256,256]{1,0:T(8,128)(2,1)S(1)}, bf16[256,256]{1,0:T(8,128)(2,1)S(1)}, u32[]{:S(2)}, u32[]{:S(2)}) collective-permute-start(bf16[256,256]{1,0:T(8,128)(2,1)S(1)} %get-tuple-element.57), channel_id=1, source_target_pairs={{0,4},{1,5},{2,6},{3,7},{4,0},{5,1},{6,2},{7,3},{8,12},{9,13},{10,... | collective-permute-start | bytes 393224 | tf_op jit(solution)/shard_map/ppermute | solution.py:425
  47.3 10.4 %collective-permute-start.17 = (bf16[768,256]{1,0:T(8,128)(2,1)S(1)}, bf16[768,256]{1,0:T(8,128)(2,1)S(1)}, u32[]{:S(2)}, u32[]{:S(2)}) collective-permute-start(bf16[768,256]{1,0:T(8,128)(2,1)S(1)} %add_convert_fusion), channel_id=1, source_target_pairs={{0,2},{1,3},{2,0},{3,1},{4,6},{5,7},{6,4},{7,5},{8,10},{9,11},{10,... | collective-permute-start | bytes 1179656 | tf_op jit(solution)/shard_map/ppermute | solution.py:67
  50.2 7.1 %collective-permute-start.20 = (bf16[256,256]{1,0:T(8,128)(2,1)S(1)}, bf16[256,256]{1,0:T(8,128)(2,1)S(1)}, u32[]{:S(2)}, u32[]{:S(2)}) collective-permute-start(bf16[256,256]{1,0:T(8,128)(2,1)S(1)} %add_convert_fusion.2), channel_id=1, source_target_pairs={{0,8},{1,9},{2,10},{3,11},{4,12},{5,13},{6,14},{7,15},{8,0},{9,1},... | collective-permute-start | bytes 393224 | tf_op jit(solution)/shard_map/ppermute | solution.py:351
  51.3 6.1 %collective-permute-start.18 = (bf16[256,256]{1,0:T(8,128)(2,1)S(1)}, bf16[256,256]{1,0:T(8,128)(2,1)S(1)}, u32[]{:S(2)}, u32[]{:S(2)}) collective-permute-start(bf16[256,256]{1,0:T(8,128)(2,1)S(1)} %get-tuple-element.56), channel_id=1, source_target_pairs={{0,4},{1,5},{4,8},{5,9},{8,12},{9,13},{6,2},{7,3},{10,6},{11,7},{1... | collective-permute-start | bytes 393224 | tf_op jit(solution)/shard_map/ppermute | solution.py:77
  57.3 1.6 %collective-permute-start.21 = (f32[256,256]{1,0:T(8,128)S(1)}, f32[256,256]{1,0:T(8,128)S(1)}, u32[]{:S(2)}, u32[]{:S(2)}) collective-permute-start(f32[256,256]{1,0:T(8,128)S(1)} %convert_add_fusion.kept_ref), channel_id=1, source_target_pairs={{0,1},{1,0},{2,3},{3,2},{4,5},{5,4},{6,7},{7,6},{8,9},{9,8},{10,11... | collective-permute-start | bytes 786440 | tf_op jit(solution)/shard_map/ppermute | solution.py:63

commit v7 on v6

--- a/solution.py
+++ b/solution.py
@@ -214,11 +214,10 @@
 
 def middle_kernel(terms, shares, a_ref, total_ref, x_ref, w_ref, r_ref, cot_ref, *refs):
     last_ref, *refs = refs
-    out_hbm, grad_ref, ax_ref, ht_ref, *share_refs, out_ref, sems = refs
+    out_ref, grad_ref, ax_ref, ht_ref, *share_refs = refs
     rows = x_ref.shape[0]
-    step = rows // sems.shape[0]
-    copies = []
-    for i in range(sems.shape[0]):
+    step = rows // 2
+    for i in range(2):
         here = slice(i * step, (i + 1) * step)
         ax = total_ref[here, :]
         at = 0
@@ -230,19 +229,14 @@
         pre = dot(ax, w_ref[...]) + dot(x_ref[here, :], r_ref[...])
         gate = jax.nn.sigmoid(pre)
         out_ref[here, :] = (pre * gate).astype(BF16)
-        copies.append(
-            pltpu.make_async_copy(
-                out_ref.at[pl.ds(i * step, step)], out_hbm.at[pl.ds(i * step, step)], sems.at[i]
-            )
-        )
-        copies[-1].start()
         grad = (cot_ref[here, :].astype(F32) * (gate * (1.0 + pre * (1.0 - gate)))).astype(BF16)
         grad_ref[here, :] = grad
         ht_ref[:, here] = dot_nt(w_ref[...], grad).astype(BF16)
-    for (part, low, high), share_ref in zip(shares, share_refs):
-        share_ref[...] = dot(ht_ref[...], a_ref[part, :, low:high]).T.astype(BF16)
-    for copy in copies:
-        copy.wait()
+    for share, share_ref in zip(shares, share_refs):
+        at = 0
+        for part, low, high in share:
+            share_ref[at : at + high - low, :] = dot(ht_ref[...], a_ref[part, :, low:high]).T.astype(BF16)
+            at += high - low
 
 
 def middle(terms, shares, *args):
@@ -251,12 +245,11 @@
     return pl.pallas_call(
         functools.partial(middle_kernel, terms, shares),
         out_shape=[
-            pltpu.HBM((rows, width), BF16), wide, wide, pltpu.VMEM((width, rows), BF16),
-            *[pltpu.VMEM((high - low, width), BF16) for _, low, high in shares],
+            wide, wide, wide, pltpu.VMEM((width, rows), BF16),
+            *[pltpu.VMEM((sum(high - low for _, low, high in share), width), BF16) for share in shares],
         ],
         in_specs=[vmem_spec()] * len(args),
-        out_specs=[hbm_spec()] + [vmem_spec()] * (3 + len(shares)),
-        scratch_shapes=[wide, pltpu.SemaphoreType.DMA((2,))],
+        out_specs=[vmem_spec()] * (4 + len(shares)),
         compiler_params=pltpu.CompilerParams(vmem_limit_bytes=LIMIT),
         cost_estimate=SHORT,
         name="middle",
@@ -275,7 +268,7 @@
 
 def pack_kernel(share_ref, other_ref, kept_ref, arrived_ref, out_ref):
     rows = share_ref.shape[0]
-    out_ref[:rows, :] = (share_ref[...].astype(F32) + other_ref[...].astype(F32)).astype(BF16)
+    out_ref[:rows, :] = (share_ref[...].astype(F32) + other_ref[:rows, :].astype(F32)).astype(BF16)
     out_ref[rows:, :] = (kept_ref[...] + arrived_ref[...]).astype(BF16)
 
 
@@ -285,10 +278,27 @@
     sum_ref[...] = (packed_ref[rows:, :].astype(F32) + arrived_ref[rows:, :].astype(F32)).astype(BF16)
 
 
-def own_kernel(a_ref, ht_ref, grad_ref, r_ref, out_ref):
+def own_kernel(a_ref, ht_ref, grad_ref, r_ref, done_ref, out_ref, done_hbm, sem):
+    copy = pltpu.make_async_copy(done_ref, done_hbm, sem)
+    copy.start()
     half = out_ref.shape[0] // 2
     for here in (slice(0, half), slice(half, None)):
         out_ref[here, :] = dot(ht_ref[...], a_ref[OWN, :, here]).T + dot_nt(grad_ref[here, :], r_ref[...])
+    copy.wait()
+
+
+def own_share(*args):
+    shape = args[-1].shape
+    return pl.pallas_call(
+        own_kernel,
+        out_shape=[pltpu.VMEM(shape, F32), pltpu.HBM(shape, BF16)],
+        in_specs=[vmem_spec()] * len(args),
+        out_specs=[vmem_spec(), hbm_spec()],
+        scratch_shapes=[pltpu.SemaphoreType.DMA],
+        compiler_params=pltpu.CompilerParams(vmem_limit_bytes=LIMIT),
+        cost_estimate=SHORT,
+        name="spread_own",
+    )(*[in_vmem(a) for a in args])
 
 
 def final_kernel(split, own_ref, other_ref, low_ref, high_ref, direct_ref, out_ref):
@@ -373,10 +383,10 @@
     plane_low = over_planes(side_low, count, False, "around")
     side_x_low = flip_core(side_low, count)
     total = gathered(dense, [(SIDE, *first), (SIDE_X, *first)], [side_low, side_x_low], total, "gather_side")
+    highs_x = flip_core(after(highs, total), count)
+    total = gathered(dense, [(SIDE, *rest), (PLANE, split, rows, rows - split)], [highs, highs], total, "gather_high")
     plane_low = after(plane_low, total)
     plane_x_low = flip_core(plane_low, count)
-    highs_x = flip_core(after(highs, total), count)
-    total = gathered(dense, [(SIDE, *rest), (PLANE, split, rows, rows - split)], [highs, highs], total, "gather_high")
     total = gathered(
         dense,
         [(PLANE, *first), (SIDE_X, *rest), (PLANE_X, split, rows, rows - split)],
@@ -388,8 +398,8 @@
 
     split_back = rows * BACKWARD // 16
     back = [(0, split_back), (split_back, rows)]
-    layer_out, grad_pre, gathered_x, ht, px_low, px_high, sx_high = middle(
-        [(PLANE_X, 0, split)], [(PLANE_X, *back[0]), (PLANE_X, *back[1]), (SIDE_X, *back[1])],
+    layer_out, grad_pre, gathered_x, ht, px_low, x_high = middle(
+        [(PLANE_X, 0, split)], [[(PLANE_X, *back[0])], [(PLANE_X, *back[1]), (SIDE_X, *back[1])]],
         dense, total, features, weight, root_weight, cotangent, plane_x_low,
     )
 
@@ -397,12 +407,13 @@
     p_low = added(p_low, flip_core(px_low, count))
     far = over_planes(p_low, count, True, "around")
     (p_high,) = spread(dense, after(ht, p_low), PLANE, back[1:], BF16, "spread_plane_high")
+    x_high = flip_core(x_high, count)
 
     square = ((width, width), F32)
     kept, sent = kernel_call(weight_kernel, "weight_products", [square, square], [gathered_x, features, grad_pre])
     high, wide = rows - split_back, (width, width)
     packed = kernel_call(
-        pack_kernel, "pack", [((high + width, width), BF16)], [p_high, flip_core(px_high, count), kept, flip_core(sent, count)]
+        pack_kernel, "pack", [((high + width, width), BF16)], [p_high, x_high, kept, flip_core(sent, count)]
     )[0]
     passing, mine = kernel_call(
         unpack_kernel, "unpack", [((high, width), BF16), (wide, BF16)], [packed, flip_side(packed, count)]
@@ -410,10 +421,10 @@
 
     ht = after(ht, packed)
     (ox,) = spread(dense, ht, OWN_X, [(0, rows)], BF16, "spread_own_x")
-    own = kernel_call(own_kernel, "spread_own", [((rows, width), F32)], [dense, ht, grad_pre, root_weight])[0]
+    own, layer_out = own_share(dense, ht, grad_pre, root_weight, layer_out)
     ht = after(ht, own, ox)
     (s_high,) = spread(dense, ht, SIDE, back[1:], F32, "spread_side_high")
-    s_high = added(s_high, flip_core(sx_high, count))
+    s_high = added(s_high, x_high[high:])
     near_high = flip_side(s_high, count)
     ht = after(ht, s_high)
     (sx_low,) = spread(dense, ht, SIDE_X, back[:1], BF16, "spread_side_x_low")

time: 60.2 us -> 59.6 us (0.990)
  starting transfers between devices: 19.8 us -> 18.7 us
    ppermute x4, waiting for transfers between devices: 2.76 us -> 0.57 us  [over_planes(): lax.ppermute(array, 'row', [(b, a) for a, b in step] if back else step)]
    ppermute x5, waiting for transfers between devices: 11.5 us -> 13.3 us  [flip_side(): return lax.ppermute(array, 'row', [(i, i ^ 2) for i in range(count)])]
    pallas_call x0 -> x1, Pallas kernels: none -> 0.93 us  [own_share(): pl.pallas_call(own_kernel, out_shape=[pltpu.VMEM(shape, F32), pltpu.HBM(s...]
    pallas_call x17 -> x16, Pallas kernels: 9.36 us -> 8.43 us  [kernel_call(): pl.pallas_call(kernel, out_shape=[pltpu.VMEM(shape, dtype) for shape, dty...]
    ppermute x11 -> x10, starting transfers between devices: 2.4 us -> 1.95 us  [flip_core(): return lax.ppermute(array, 'row', [(i, i ^ 1) for i in range(count)])]
    ppermute x11 -> x10, waiting for transfers between devices: 1.04 us -> 1.47 us  [flip_core(): return lax.ppermute(array, 'row', [(i, i ^ 1) for i in range(count)])]
  transfers between devices with their start and end apart: 22 -> 21, of which waited for: 8 -> 10; matrix products, arithmetic and copies ran while one was open for 0% -> 0% of each run, Pallas kernels for 22% -> 23%
where the time goes in v7:
time: 59.6 us; the launch traced here: 59.2 us
  waiting for transfers between devices  20.9 us (35%)
  starting transfers between devices  18.7 us (31%)
  Pallas kernels  17.8 us (30%)
  between operations  1.59 us (3%)
    ppermute x5, waiting for transfers between devices, flip_side(): return lax.ppermute(array, 'row', [(i, i ^ 2) for i in range(count)])  13.3 us
    ppermute x4, starting transfers between devices, over_planes(): lax.ppermute(array, 'row', [(b, a) for a, b in step] if back else step)  10.2 us
    pallas_call x16, Pallas kernels, kernel_call(): pl.pallas_call(kernel, out_shape=[pltpu.VMEM(shape, dtype) for shape, dty...  8.43 us
    ppermute x5, starting transfers between devices, flip_side(): return lax.ppermute(array, 'row', [(i, i ^ 2) for i in range(count)])  5.6 us
    pallas_call x1, Pallas kernels, dense_adjacency(): pl.pallas_call(dense_kernel, out_shape=pltpu.VMEM((PARTS, width, width),...  4.09 us
    ppermute x1, waiting for transfers between devices, exchanged(): lax.ppermute(mine, 'row', [(i, i ^ hop) for i in range(count)])  3.03 us
    ppermute x1, waiting for transfers between devices, body(): lax.ppermute(after(mine, own), 'row', [(i, i ^ 4) for i in range(count)])  2.56 us
    pallas_call x1, Pallas kernels, middle(): pl.pallas_call(functools.partial(middle_kernel, terms, shares), out_shape...  2.15 us
  transfers between devices with their start and end apart: 21, of which 10 were waited for; matrix products, arithmetic and copies ran while one was open for 0% of the time, Pallas kernels for 23%

profile of v7, /device:TPU:0, one launch (start us, length us, event | category | flops | bytes accessed | tf_op | source)
XLA Modules:
  0.0 59.2 jit_solution(10814710537677502868)
XLA Ops:
  0.6 0.0 copy-start
  0.6 1.2 %cut.1 = (bf16[640,256]{1,0:T(8,128)(2,1)S(1)}, bf16[384,256]{1,0:T(8,128)(2,1)S(1)}) custom-call(bf16[1024,256]{1,0:T(8,128)(2,1)} %x_ref.3), custom_call_target="tpu_custom_call" | custom-call | tf_op jit(solution)/shard_map/cut/pallas_call | solution.py:197
  1.8 0.5 collective-permute-start.2
  2.4 2.6 %collective-permute-start = (bf16[640,256]{1,0:T(8,128)(2,1)S(1)}, bf16[640,256]{1,0:T(8,128)(2,1)S(1)}, u32[]{:S(2)}, u32[]{:S(2)}) collective-permute-start(bf16[640,256]{1,0:T(8,128)(2,1)S(1)} %get-tuple-element.34), channel_id=1, source_target_pairs={{0,2},{1,3},{2,0},{3,1},{4,6},{5,7},{6,4},{7,5},{8,10},{9,11},{10,... | collective-permute-start | bytes 983048 | tf_op jit(solution)/shard_map/ppermute | solution.py:67
  5.0 3.6 %collective-permute-start.1 = (bf16[384,256]{1,0:T(8,128)(2,1)S(1)}, bf16[384,256]{1,0:T(8,128)(2,1)S(1)}, u32[]{:S(2)}, u32[]{:S(2)}) collective-permute-start(bf16[384,256]{1,0:T(8,128)(2,1)S(1)} %get-tuple-element.35.a_ref), channel_id=1, source_target_pairs={{4,0},{5,1},{8,4},{9,5},{12,8},{13,9},{2,6},{3,7},{6,10},{7,11},{1... | collective-permute-start | bytes 589832 | tf_op jit(solution)/shard_map/ppermute | solution.py:77
  9.2 4.1 %dense_adjacency.1.refs_0_.a_ref = bf16[6,1024,1024]{2,1,0:T(8,128)(2,1)S(1)} custom-call(s32[1]{0:T(128)S(6)} %copy.12.count_ref, s32[192]{0:T(256)} %rows_hbm.1, s32[192]{0:T(256)} %cols_hbm.1, bf16[192,128,128]{2,1,0:T(8,128)(2,1)} %tiles_ref.1), custom_call_target="tpu_custom_call" | custom-call | tf_op jit(solution)/shard_map/dense_adjacency/pallas_call | solution.py:137
  13.3 0.0 collective-permute-done.2.refs_2_
  13.3 1.3 %gather_own.1.refs_3_ = f32[1024,256]{1,0:T(8,128)S(1)} custom-call(bf16[6,1024,1024]{2,1,0:T(8,128)(2,1)S(1)} %dense_adjacency.1.refs_0_.a_ref, bf16[1024,256]{1,0:T(8,128)(2,1)S(1)} %copy-done, bf16[1024,256]{1,0:T(8,128)(2,1)S(1)} %collective-permute-done.2.refs_2_), custom_call_target="tpu_custom_call" | custom-call | tf_op jit(solution)/shard_map/gather_own/pallas_call | solution.py:51
  14.6 0.0 collective-permute-done.1.b_ref
  14.6 0.0 collective-permute-done.refs_1_
  14.6 0.5 collective-permute-start.4
  15.1 1.6 %collective-permute-start.3 = (bf16[640,256]{1,0:T(8,128)(2,1)S(1)}, bf16[640,256]{1,0:T(8,128)(2,1)S(1)}, u32[]{:S(2)}, u32[]{:S(2)}) collective-permute-start(bf16[640,256]{1,0:T(8,128)(2,1)S(1)} %collective-permute-done.refs_1_), channel_id=1, source_target_pairs={{0,4},{1,5},{4,8},{5,9},{8,12},{9,13},{6,2},{7,3},{10,6},{11,7},{1... | collective-permute-start | bytes 983048 | tf_op jit(solution)/shard_map/ppermute | solution.py:77
  16.7 0.0 collective-permute-done.5.refs_2_
  16.7 1.0 %gather_side.1.refs_3_ = f32[1024,256]{1,0:T(8,128)S(1)} custom-call(bf16[6,1024,1024]{2,1,0:T(8,128)(2,1)S(1)} %dense_adjacency.1.refs_0_.a_ref, bf16[640,256]{1,0:T(8,128)(2,1)S(1)} %collective-permute-done.refs_1_, bf16[640,256]{1,0:T(8,128)(2,1)S(1)} %collective-permute-done.5.refs_2_, f32[1024,256]{1,0:T(8,128)S(1)} %gather_own.1.refs_3_), custom_call_target="tpu_custom_call" | custom-call | tf_op jit(solution)/shard_map/gather_side/pallas_call | solution.py:51
  17.7 0.0 copy-start.1
  17.7 0.0 copy-start.2
  17.7 0.0 copy-start.3
  17.7 8.1 %collective-permute-done.4.refs_1_.refs_2_ = bf16[768,256]{1,0:T(8,128)(2,1)S(1)} collective-permute-done((bf16[768,256]{1,0:T(8,128)(2,1)S(1)}, bf16[768,256]{1,0:T(8,128)(2,1)S(1)}, u32[]{:S(2)}, u32[]{:S(2)}) %collective-permute-start.4) | collective-permute-done | bytes 393248 | tf_op jit(solution)/shard_map/ppermute | solution.py:67
  25.8 0.0 collective-permute-start.6
  25.8 0.7 %gather_high.1.refs_4_ = f32[1024,256]{1,0:T(8,128)S(1)} custom-call(bf16[6,1024,1024]{2,1,0:T(8,128)(2,1)S(1)} %dense_adjacency.1.refs_0_.a_ref, bf16[768,256]{1,0:T(8,128)(2,1)S(1)} %collective-permute-done.4.refs_1_.refs_2_, bf16[768,256]{1,0:T(8,128)(2,1)S(1)} %collective-permute-done.4.refs_1_.refs_2_, f32[1024,256]{1,0:T(8,128)S(1)} %gather_side.1.refs_3_), custom_call_target="tpu_custom_call" | custom-call | tf_op jit(solution)/shard_map/gather_high/pallas_call | solution.py:51
  26.5 0.6 collective-permute-done.3.refs_1_
  27.1 0.0 collective-permute-start.7
  27.1 0.4 collective-permute-done.6.refs_2_.refs_3_
  27.6 1.1 %gather_high_x.1.total_ref = f32[1024,256]{1,0:T(8,128)S(1)} custom-call(bf16[6,1024,1024]{2,1,0:T(8,128)(2,1)S(1)} %dense_adjacency.1.refs_0_.a_ref, bf16[640,256]{1,0:T(8,128)(2,1)S(1)} %collective-permute-done.3.refs_1_, bf16[768,256]{1,0:T(8,128)(2,1)S(1)} %collective-permute-done.6.refs_2_.refs_3_, ...), custom_call_target="tpu_custom_call" | custom-call | flops 500000000 | tf_op jit(solution)/shard_map/gather_high_x/pallas_call | solution.py:51
  28.7 0.1 collective-permute-done.7.refs_0_
  28.7 2.1 %middle.1 = (bf16[1024,256]{1,0:T(8,128)(2,1)S(1)}, bf16[1024,256]{1,0:T(8,128)(2,1)S(1)}, bf16[1024,256]{1,0:T(8,128)(2,1)S(1)}, bf16[256,1024]{1,0:T(8,128)(2,...) custom-call(bf16[6,1024,1024]{2,1,0:T(8,128)(2,1)S(1)} %dense_adjacency.1.refs_0_.a_ref, ...), custom_call_target="tpu_custom_call" | custom-call | tf_op jit(solution)/shard_map/middle/pallas_call | solution.py:245
  30.9 0.2 collective-permute-start.8
  31.1 0.4 collective-permute-start.9
  31.5 0.7 %spread_plane_low.1 = bf16[768,256]{1,0:T(8,128)(2,1)S(1)} custom-call(bf16[6,1024,1024]{2,1,0:T(8,128)(2,1)S(1)} %dense_adjacency.1.refs_0_.a_ref, bf16[256,1024]{1,0:T(8,128)(2,1)S(1)} %get-tuple-element.56.ht_ref), custom_call_target="tpu_custom_call" | custom-call | tf_op jit(solution)/shard_map/spread_plane_low/pallas_call | solution.py:51
  32.1 0.5 weight_products.1
  32.6 0.2 collective-permute-start.10
  32.8 0.0 collective-permute-done.8
  32.8 0.1 add_convert_fusion.1
  32.9 2.1 %collective-permute-start.14 = (bf16[768,256]{1,0:T(8,128)(2,1)S(1)}, bf16[768,256]{1,0:T(8,128)(2,1)S(1)}, u32[]{:S(2)}, u32[]{:S(2)}) collective-permute-start(bf16[768,256]{1,0:T(8,128)(2,1)S(1)} %add_convert_fusion.1), channel_id=1, source_target_pairs={{4,0},{5,1},{8,4},{9,5},{12,8},{13,9},{2,6},{3,7},{6,10},{7,11},{1... | collective-permute-start | bytes 1179656 | tf_op jit(solution)/shard_map/ppermute | solution.py:77
  35.0 0.4 spread_plane_high.1.share_ref
  35.4 0.0 collective-permute-done.10.arrived_ref
  35.4 0.1 pack.1.packed_ref
  35.5 0.1 collective-permute-start.12
  35.6 0.8 %spread_own_x.1 = bf16[1024,256]{1,0:T(8,128)(2,1)S(1)} custom-call(bf16[6,1024,1024]{2,1,0:T(8,128)(2,1)S(1)} %dense_adjacency.1.refs_0_.a_ref, bf16[256,1024]{1,0:T(8,128)(2,1)S(1)} %get-tuple-element.56.ht_ref), custom_call_target="tpu_custom_call" | custom-call | tf_op jit(solution)/shard_map/spread_own_x/pallas_call | solution.py:51
  36.3 0.9 %spread_own.1 = (f32[1024,256]{1,0:T(8,128)S(1)}, bf16[1024,256]{1,0:T(8,128)(2,1)}) custom-call(bf16[6,1024,1024]{2,1,0:T(8,128)(2,1)S(1)} %dense_adjacency.1.refs_0_.a_ref, bf16[256,1024]{1,0:T(8,128)(2,1)S(1)} %get-tuple-element.56.ht_ref, bf16[1024,256]{1,0:T(8,128)(2,1)S(1)} %get-tuple-element.46.grad_ref, bf16[256,256]{1,0:T(8,128)(2,1)S(1)} %copy-done.1, ...), custom_call_target="tpu_custom_call" | custom-call | tf_op jit(solution)/shard_map/spread_own/pallas_call | solution.py:292
  37.3 0.4 spread_side_high.1
  37.7 2.1 %collective-permute-start.13 = (bf16[256,256]{1,0:T(8,128)(2,1)S(1)}, bf16[256,256]{1,0:T(8,128)(2,1)S(1)}, u32[]{:S(2)}, u32[]{:S(2)}) collective-permute-start(bf16[256,256]{1,0:T(8,128)(2,1)S(1)} %add_convert_fusion.3), channel_id=1, source_target_pairs={{0,2},{1,3},{2,0},{3,1},{4,6},{5,7},{6,4},{7,5},{8,10},{9,11},{10,... | collective-permute-start | bytes 393224 | tf_op jit(solution)/shard_map/ppermute | solution.py:67
  39.8 0.0 collective-permute-start.11
  39.8 0.7 %spread_side_x_low.1 = bf16[768,256]{1,0:T(8,128)(2,1)S(1)} custom-call(bf16[6,1024,1024]{2,1,0:T(8,128)(2,1)S(1)} %dense_adjacency.1.refs_0_.a_ref, bf16[256,1024]{1,0:T(8,128)(2,1)S(1)} %get-tuple-element.56.ht_ref), custom_call_target="tpu_custom_call" | custom-call | tf_op jit(solution)/shard_map/spread_side_x_low/pallas_call | solution.py:51
  40.4 0.6 collective-permute-start.15
  41.0 3.7 %collective-permute-done.12.arrived_ref = bf16[512,256]{1,0:T(8,128)(2,1)S(1)} collective-permute-done((bf16[512,256]{1,0:T(8,128)(2,1)S(1)}, bf16[512,256]{1,0:T(8,128)(2,1)S(1)}, u32[]{:S(2)}, u32[]{:S(2)}) %collective-permute-start.12) | collective-permute-done | bytes 262176 | tf_op jit(solution)/shard_map/ppermute | solution.py:67
  44.8 0.1 collective-permute-start.18
  44.8 0.7 %spread_side_low.1.own_ref = f32[768,256]{1,0:T(8,128)S(1)} custom-call(bf16[6,1024,1024]{2,1,0:T(8,128)(2,1)S(1)} %dense_adjacency.1.refs_0_.a_ref, bf16[256,1024]{1,0:T(8,128)(2,1)S(1)} %get-tuple-element.56.ht_ref), custom_call_target="tpu_custom_call" | custom-call | tf_op jit(solution)/shard_map/spread_side_low/pallas_call | solution.py:51
  45.6 1.1 %collective-permute-done.13.high_ref = bf16[256,256]{1,0:T(8,128)(2,1)S(1)} collective-permute-done((bf16[256,256]{1,0:T(8,128)(2,1)S(1)}, bf16[256,256]{1,0:T(8,128)(2,1)S(1)}, u32[]{:S(2)}, u32[]{:S(2)}) %collective-permute-start.13) | collective-permute-done | bytes 131104 | tf_op jit(solution)/shard_map/ppermute | solution.py:67
  46.7 0.1 relay.1
  46.7 0.0 collective-permute-done.15
  46.7 0.1 add_convert_fusion
  46.8 0.4 collective-permute-start.16
  47.2 2.6 %collective-permute-done.18 = bf16[256,256]{1,0:T(8,128)(2,1)S(1)} collective-permute-done((bf16[256,256]{1,0:T(8,128)(2,1)S(1)}, bf16[256,256]{1,0:T(8,128)(2,1)S(1)}, u32[]{:S(2)}, u32[]{:S(2)}) %collective-permute-start.18) | collective-permute-done | bytes 131104 | tf_op jit(solution)/shard_map/ppermute | solution.py:436
  49.8 0.8 %collective-permute-start.19 = (bf16[256,256]{1,0:T(8,128)(2,1)S(1)}, bf16[256,256]{1,0:T(8,128)(2,1)S(1)}, u32[]{:S(2)}, u32[]{:S(2)}) collective-permute-start(bf16[256,256]{1,0:T(8,128)(2,1)S(1)} %add_convert_fusion.2), channel_id=1, source_target_pairs={{0,8},{1,9},{2,10},{3,11},{4,12},{5,13},{6,14},{7,15},{8,0},{9,1},... | collective-permute-start | bytes 393224 | tf_op jit(solution)/shard_map/ppermute | solution.py:361
  50.7 2.9 %collective-permute-start.17 = (bf16[256,256]{1,0:T(8,128)(2,1)S(1)}, bf16[256,256]{1,0:T(8,128)(2,1)S(1)}, u32[]{:S(2)}, u32[]{:S(2)}) collective-permute-start(bf16[256,256]{1,0:T(8,128)(2,1)S(1)} %get-tuple-element.58), channel_id=1, source_target_pairs={{0,4},{1,5},{4,8},{5,9},{8,12},{9,13},{6,2},{7,3},{10,6},{11,7},{1... | collective-permute-start | bytes 393224 | tf_op jit(solution)/shard_map/ppermute | solution.py:77
  53.6 3.0 %collective-permute-done.19 = bf16[256,256]{1,0:T(8,128)(2,1)S(1)} collective-permute-done((bf16[256,256]{1,0:T(8,128)(2,1)S(1)}, bf16[256,256]{1,0:T(8,128)(2,1)S(1)}, u32[]{:S(2)}, u32[]{:S(2)}) %collective-permute-start.19) | collective-permute-done | bytes 131104 | tf_op jit(solution)/shard_map/ppermute | solution.py:361
  56.7 0.1 collective-permute-start.20
  56.7 0.0 collective-permute-done.17.direct_ref
  56.8 0.0 collective-permute-done.11.other_ref
  56.8 0.4 collective-permute-done.16.low_ref
  57.2 0.2 final.1.out_ref
  57.4 0.9 %collective-permute-done.20.other_ref = f32[256,256]{1,0:T(8,128)S(1)} collective-permute-done((f32[256,256]{1,0:T(8,128)S(1)}, f32[256,256]{1,0:T(8,128)S(1)}, u32[]{:S(2)}, u32[]{:S(2)}) %collective-permute-start.20) | collective-permute-done | bytes 262176 | tf_op jit(solution)/shard_map/ppermute | solution.py:63
  58.3 1.0 %scaled.1 = (bf16[1024,256]{1,0:T(8,128)(2,1)}, f32[256,256]{1,0:T(8,128)}, f32[256,256]{1,0:T(8,128)}) custom-call(bf16[1024,256]{1,0:T(8,128)(2,1)S(1)} %final.1.out_ref, f32[256,256]{1,0:T(8,128)S(1)} %convert_add_fusion.kept_ref, f32[256,256]{1,0:T(8,128)S(1)} %collective-permute-done.20.other_ref), custom_call_target="tpu_custom_call" | custom-call | tf_op jit(solution)/shard_map/scaled/pallas_call | solution.py:331
  (12 shorter events, 0.2 us)
Async XLA Ops:
  0.6 12.7 %copy-start = (bf16[1024,256]{1,0:T(8,128)(2,1)S(1)}, bf16[1024,256]{1,0:T(8,128)(2,1)}, u32[]{:S(2)}) copy-start(bf16[1024,256]{1,0:T(8,128)(2,1)} %x_ref.3) | copy-start | bytes 1572868
  1.8 11.5 %collective-permute-start.2 = (bf16[1024,256]{1,0:T(8,128)(2,1)}, bf16[1024,256]{1,0:T(8,128)(2,1)S(1)}, u32[]{:S(2)}, u32[]{:S(2)}) collective-permute-start(bf16[1024,256]{1,0:T(8,128)(2,1)} %x_ref.3), channel_id=1, source_target_pairs={{0,1},{1,0},{2,3},{3,2},{4,5},{5,4},{6,7},{7,6},{8,9},{9,8},{10,11... | collective-permute-start | bytes 1572872 | tf_op jit(solution)/shard_map/ppermute | solution.py:63
  2.4 12.2 %collective-permute-start = (bf16[640,256]{1,0:T(8,128)(2,1)S(1)}, bf16[640,256]{1,0:T(8,128)(2,1)S(1)}, u32[]{:S(2)}, u32[]{:S(2)}) collective-permute-start(bf16[640,256]{1,0:T(8,128)(2,1)S(1)} %get-tuple-element.34), channel_id=1, source_target_pairs={{0,2},{1,3},{2,0},{3,1},{4,6},{5,7},{6,4},{7,5},{8,10},{9,11},{10,... | collective-permute-start | bytes 983048 | tf_op jit(solution)/shard_map/ppermute | solution.py:67
  5.0 9.6 %collective-permute-start.1 = (bf16[384,256]{1,0:T(8,128)(2,1)S(1)}, bf16[384,256]{1,0:T(8,128)(2,1)S(1)}, u32[]{:S(2)}, u32[]{:S(2)}) collective-permute-start(bf16[384,256]{1,0:T(8,128)(2,1)S(1)} %get-tuple-element.35.a_ref), channel_id=1, source_target_pairs={{4,0},{5,1},{8,4},{9,5},{12,8},{13,9},{2,6},{3,7},{6,10},{7,11},{1... | collective-permute-start | bytes 589832 | tf_op jit(solution)/shard_map/ppermute | solution.py:77
  14.6 11.2 %collective-permute-start.4 = (bf16[768,256]{1,0:T(8,128)(2,1)S(1)}, bf16[768,256]{1,0:T(8,128)(2,1)S(1)}, u32[]{:S(2)}, u32[]{:S(2)}) collective-permute-start(bf16[768,256]{1,0:T(8,128)(2,1)S(1)} %join.1), channel_id=1, source_target_pairs={{0,2},{1,3},{2,0},{3,1},{4,6},{5,7},{6,4},{7,5},{8,10},{9,11},{10,... | collective-permute-start | bytes 1179656 | tf_op jit(solution)/shard_map/ppermute | solution.py:67
  15.1 1.6 %collective-permute-start.5 = (bf16[640,256]{1,0:T(8,128)(2,1)S(1)}, bf16[640,256]{1,0:T(8,128)(2,1)S(1)}, u32[]{:S(2)}, u32[]{:S(2)}) collective-permute-start(bf16[640,256]{1,0:T(8,128)(2,1)S(1)} %collective-permute-done.refs_1_), channel_id=1, source_target_pairs={{0,1},{1,0},{2,3},{3,2},{4,5},{5,4},{6,7},{7,6},{8,9},{9,8},{10,11... | collective-permute-start | bytes 983048 | tf_op jit(solution)/shard_map/ppermute | solution.py:63
  15.1 12.0 %collective-permute-start.3 = (bf16[640,256]{1,0:T(8,128)(2,1)S(1)}, bf16[640,256]{1,0:T(8,128)(2,1)S(1)}, u32[]{:S(2)}, u32[]{:S(2)}) collective-permute-start(bf16[640,256]{1,0:T(8,128)(2,1)S(1)} %collective-permute-done.refs_1_), channel_id=1, source_target_pairs={{0,4},{1,5},{4,8},{5,9},{8,12},{9,13},{6,2},{7,3},{10,6},{11,7},{1... | collective-permute-start | bytes 983048 | tf_op jit(solution)/shard_map/ppermute | solution.py:77
  17.7 11.0 %copy-start.1 = (bf16[256,256]{1,0:T(8,128)(2,1)S(1)}, bf16[256,256]{1,0:T(8,128)(2,1)}, u32[]{:S(2)}) copy-start(bf16[256,256]{1,0:T(8,128)(2,1)} %r_ref.3) | copy-start | bytes 393220
  17.7 11.0 %copy-start.2 = (bf16[1024,256]{1,0:T(8,128)(2,1)S(1)}, bf16[1024,256]{1,0:T(8,128)(2,1)}, u32[]{:S(2)}) copy-start(bf16[1024,256]{1,0:T(8,128)(2,1)} %cot_ref.1) | copy-start | bytes 1572868
  17.7 11.0 %copy-start.3 = (bf16[256,256]{1,0:T(8,128)(2,1)S(1)}, bf16[256,256]{1,0:T(8,128)(2,1)}, u32[]{:S(2)}) copy-start(bf16[256,256]{1,0:T(8,128)(2,1)} %w_ref.1) | copy-start | bytes 393220
  25.8 1.7 %collective-permute-start.6 = (bf16[768,256]{1,0:T(8,128)(2,1)S(1)}, bf16[768,256]{1,0:T(8,128)(2,1)S(1)}, u32[]{:S(2)}, u32[]{:S(2)}) collective-permute-start(bf16[768,256]{1,0:T(8,128)(2,1)S(1)} %collective-permute-done.4.refs_1_.refs_2_), channel_id=1, source_target_pairs={{0,1},{1,0},{2,3},{3,2},{4,5},{5,4},{6,7},{7,6},{8,9},{9,8},{10,11... | collective-permute-start | bytes 1179656 | tf_op jit(solution)/shard_map/ppermute | solution.py:63
  27.1 1.6 %collective-permute-start.7 = (bf16[640,256]{1,0:T(8,128)(2,1)S(1)}, bf16[640,256]{1,0:T(8,128)(2,1)S(1)}, u32[]{:S(2)}, u32[]{:S(2)}) collective-permute-start(bf16[640,256]{1,0:T(8,128)(2,1)S(1)} %collective-permute-done.3.refs_1_), channel_id=1, source_target_pairs={{0,1},{1,0},{2,3},{3,2},{4,5},{5,4},{6,7},{7,6},{8,9},{9,8},{10,11... | collective-permute-start | bytes 983048 | tf_op jit(solution)/shard_map/ppermute | solution.py:63
  30.9 1.9 %collective-permute-start.8 = (bf16[768,256]{1,0:T(8,128)(2,1)S(1)}, bf16[768,256]{1,0:T(8,128)(2,1)S(1)}, u32[]{:S(2)}, u32[]{:S(2)}) collective-permute-start(bf16[768,256]{1,0:T(8,128)(2,1)S(1)} %get-tuple-element.42), channel_id=1, source_target_pairs={{0,1},{1,0},{2,3},{3,2},{4,5},{5,4},{6,7},{7,6},{8,9},{9,8},{10,11... | collective-permute-start | bytes 1179656 | tf_op jit(solution)/shard_map/ppermute | solution.py:63
  31.1 4.3 %collective-permute-start.9 = (bf16[512,256]{1,0:T(8,128)(2,1)S(1)}, bf16[512,256]{1,0:T(8,128)(2,1)S(1)}, u32[]{:S(2)}, u32[]{:S(2)}) collective-permute-start(bf16[512,256]{1,0:T(8,128)(2,1)S(1)} %get-tuple-element.44), channel_id=1, source_target_pairs={{0,1},{1,0},{2,3},{3,2},{4,5},{5,4},{6,7},{7,6},{8,9},{9,8},{10,11... | collective-permute-start | bytes 786440 | tf_op jit(solution)/shard_map/ppermute | solution.py:63
  32.6 2.8 %collective-permute-start.10 = (f32[256,256]{1,0:T(8,128)S(1)}, f32[256,256]{1,0:T(8,128)S(1)}, u32[]{:S(2)}, u32[]{:S(2)}) collective-permute-start(f32[256,256]{1,0:T(8,128)S(1)} %get-tuple-element.48), channel_id=1, source_target_pairs={{0,1},{1,0},{2,3},{3,2},{4,5},{5,4},{6,7},{7,6},{8,9},{9,8},{10,11... | collective-permute-start | bytes 786440 | tf_op jit(solution)/shard_map/ppermute | solution.py:63
  32.9 13.7 %collective-permute-start.14 = (bf16[768,256]{1,0:T(8,128)(2,1)S(1)}, bf16[768,256]{1,0:T(8,128)(2,1)S(1)}, u32[]{:S(2)}, u32[]{:S(2)}) collective-permute-start(bf16[768,256]{1,0:T(8,128)(2,1)S(1)} %add_convert_fusion.1), channel_id=1, source_target_pairs={{4,0},{5,1},{8,4},{9,5},{12,8},{13,9},{2,6},{3,7},{6,10},{7,11},{1... | collective-permute-start | bytes 1179656 | tf_op jit(solution)/shard_map/ppermute | solution.py:77
  35.5 9.2 %collective-permute-start.12 = (bf16[512,256]{1,0:T(8,128)(2,1)S(1)}, bf16[512,256]{1,0:T(8,128)(2,1)S(1)}, u32[]{:S(2)}, u32[]{:S(2)}) collective-permute-start(bf16[512,256]{1,0:T(8,128)(2,1)S(1)} %pack.1.packed_ref), channel_id=1, source_target_pairs={{0,2},{1,3},{2,0},{3,1},{4,6},{5,7},{6,4},{7,5},{8,10},{9,11},{10,... | collective-permute-start | bytes 786440 | tf_op jit(solution)/shard_map/ppermute | solution.py:67
  37.7 9.0 %collective-permute-start.13 = (bf16[256,256]{1,0:T(8,128)(2,1)S(1)}, bf16[256,256]{1,0:T(8,128)(2,1)S(1)}, u32[]{:S(2)}, u32[]{:S(2)}) collective-permute-start(bf16[256,256]{1,0:T(8,128)(2,1)S(1)} %add_convert_fusion.3), channel_id=1, source_target_pairs={{0,2},{1,3},{2,0},{3,1},{4,6},{5,7},{6,4},{7,5},{8,10},{9,11},{10,... | collective-permute-start | bytes 393224 | tf_op jit(solution)/shard_map/ppermute | solution.py:67
  39.8 17.0 %collective-permute-start.11 = (bf16[1024,256]{1,0:T(8,128)(2,1)S(1)}, bf16[1024,256]{1,0:T(8,128)(2,1)S(1)}, u32[]{:S(2)}, u32[]{:S(2)}) collective-permute-start(bf16[1024,256]{1,0:T(8,128)(2,1)S(1)} %spread_own_x.1), channel_id=1, source_target_pairs={{0,1},{1,0},{2,3},{3,2},{4,5},{5,4},{6,7},{7,6},{8,9},{9,8},{10,11... | collective-permute-start | bytes 1572872 | tf_op jit(solution)/shard_map/ppermute | solution.py:63
  40.4 6.3 %collective-permute-start.15 = (bf16[768,256]{1,0:T(8,128)(2,1)S(1)}, bf16[768,256]{1,0:T(8,128)(2,1)S(1)}, u32[]{:S(2)}, u32[]{:S(2)}) collective-permute-start(bf16[768,256]{1,0:T(8,128)(2,1)S(1)} %spread_side_x_low.1), channel_id=1, source_target_pairs={{0,1},{1,0},{2,3},{3,2},{4,5},{5,4},{6,7},{7,6},{8,9},{9,8},{10,11... | collective-permute-start | bytes 1179656 | tf_op jit(solution)/shard_map/ppermute | solution.py:63
  44.8 5.0 %collective-permute-start.18 = (bf16[256,256]{1,0:T(8,128)(2,1)S(1)}, bf16[256,256]{1,0:T(8,128)(2,1)S(1)}, u32[]{:S(2)}, u32[]{:S(2)}) collective-permute-start(bf16[256,256]{1,0:T(8,128)(2,1)S(1)} %get-tuple-element.59), channel_id=1, source_target_pairs={{0,4},{1,5},{2,6},{3,7},{4,0},{5,1},{6,2},{7,3},{8,12},{9,13},{10,... | collective-permute-start | bytes 393224 | tf_op jit(solution)/shard_map/ppermute | solution.py:436
  46.8 10.3 %collective-permute-start.16 = (bf16[768,256]{1,0:T(8,128)(2,1)S(1)}, bf16[768,256]{1,0:T(8,128)(2,1)S(1)}, u32[]{:S(2)}, u32[]{:S(2)}) collective-permute-start(bf16[768,256]{1,0:T(8,128)(2,1)S(1)} %add_convert_fusion), channel_id=1, source_target_pairs={{0,2},{1,3},{2,0},{3,1},{4,6},{5,7},{6,4},{7,5},{8,10},{9,11},{10,... | collective-permute-start | bytes 1179656 | tf_op jit(solution)/shard_map/ppermute | solution.py:67
  49.8 6.8 %collective-permute-start.19 = (bf16[256,256]{1,0:T(8,128)(2,1)S(1)}, bf16[256,256]{1,0:T(8,128)(2,1)S(1)}, u32[]{:S(2)}, u32[]{:S(2)}) collective-permute-start(bf16[256,256]{1,0:T(8,128)(2,1)S(1)} %add_convert_fusion.2), channel_id=1, source_target_pairs={{0,8},{1,9},{2,10},{3,11},{4,12},{5,13},{6,14},{7,15},{8,0},{9,1},... | collective-permute-start | bytes 393224 | tf_op jit(solution)/shard_map/ppermute | solution.py:361
  50.7 6.1 %collective-permute-start.17 = (bf16[256,256]{1,0:T(8,128)(2,1)S(1)}, bf16[256,256]{1,0:T(8,128)(2,1)S(1)}, u32[]{:S(2)}, u32[]{:S(2)}) collective-permute-start(bf16[256,256]{1,0:T(8,128)(2,1)S(1)} %get-tuple-element.58), channel_id=1, source_target_pairs={{0,4},{1,5},{4,8},{5,9},{8,12},{9,13},{6,2},{7,3},{10,6},{11,7},{1... | collective-permute-start | bytes 393224 | tf_op jit(solution)/shard_map/ppermute | solution.py:77
  56.7 1.6 %collective-permute-start.20 = (f32[256,256]{1,0:T(8,128)S(1)}, f32[256,256]{1,0:T(8,128)S(1)}, u32[]{:S(2)}, u32[]{:S(2)}) collective-permute-start(f32[256,256]{1,0:T(8,128)S(1)} %convert_add_fusion.kept_ref), channel_id=1, source_target_pairs={{0,1},{1,0},{2,3},{3,2},{4,5},{5,4},{6,7},{7,6},{8,9},{9,8},{10,11... | collective-permute-start | bytes 786440 | tf_op jit(solution)/shard_map/ppermute | solution.py:63
